TPU v7x, 32 devices: a whole 2x2x4 slice. The times are simulated.
32 devices in a mesh: row: 4 (over y, x), col: 8 (over z, core).
Axes of the slice: x: 2, y: 2, z: 4, core: 2. Of those that a mesh axis runs over, the one named last changes fastest.
Arguments:
- queries: bfloat16 [4096, 768], P(('row', 'col')), may hold values from -8 to 8
- tools: bfloat16 [6144, 768], P(('col', 'row')), may hold values from -8 to 8
- query_mass: float32 [4096], P('row'), may hold values from 0.5 to 5
- tool_mass: float32 [6144], P('col'), may hold values from 0.5 to 5
Outputs:
- mapped_queries: bfloat16 [4096, 768], P(('row', 'col'))
- query_potential: float32 [4096], P('row')
- tool_potential: float32 [6144], P('col')
All inputs are finite; a program needn't handle non-finite values.
Results may differ from a plain program's by a relative error of at most 0.0025.
Values may be sent and summed in bfloat16 or wider, within the bound.
No kernel may reach another device: no remote copies, remote signals or barrier semaphores. Data moves between devices by JAX's collectives and lax.ppermute only.
A program may use at most 64 MiB of HBM per device.

v0:
```python
import math

import jax
import jax.numpy as jnp
from jax import lax
from jax.sharding import PartitionSpec as P

ITERS = 3


EPSILON = 0.5


def row_lse(scores):
    local_max = jnp.max(scores, axis=1)
    highest = lax.pmax(local_max, "col")
    summed = lax.psum(jnp.sum(jnp.exp(scores - highest[:, None]), axis=1), "col")
    return highest + jnp.log(summed)


def column_lse(scores):
    local_max = jnp.max(scores, axis=0)
    highest = lax.pmax(local_max, "row")
    summed = lax.psum(jnp.sum(jnp.exp(scores - highest[None, :]), axis=0), "row")
    return highest + jnp.log(summed)


def local(queries, tools, query_mass, tool_mass):
    tool_block = lax.all_gather(tools, "row", axis=0, tiled=True)
    features = queries.shape[1]
    scaling = -1.0 / math.sqrt(features)
    products = lax.dot_general(
        lax.all_gather(queries, "col", axis=0, tiled=True),
        tool_block,
        (((1,), (1,)), ((), ())),
        preferred_element_type=jnp.float32,
    )
    cost_tile = products * scaling
    log_query = jnp.log(query_mass)
    log_tool = jnp.log(tool_mass)
    tool_potential = jnp.zeros((cost_tile.shape[1],), jnp.float32)
    query_potential = jnp.zeros((cost_tile.shape[0],), jnp.float32)
    for sweep in range(ITERS):
        query_potential = EPSILON * log_query - EPSILON * row_lse(
            (tool_potential[None, :] - cost_tile) / EPSILON
        )
        tool_potential = EPSILON * log_tool - EPSILON * column_lse(
            (query_potential[:, None] - cost_tile) / EPSILON
        )
    final_scores = (tool_potential[None, :] - cost_tile) / EPSILON
    peaks = lax.pmax(jnp.max(final_scores, axis=1), "col")
    exps = jnp.exp(final_scores - peaks[:, None])
    local_total = jnp.sum(exps, axis=1)
    weights = exps.astype(jnp.bfloat16)
    own_rows = cost_tile.shape[0] // lax.axis_size("col")
    totals = lax.psum(local_total, "col")
    own_totals = lax.dynamic_slice_in_dim(totals, lax.axis_index("col") * own_rows, own_rows, 0)
    summed = lax.psum_scatter(
        jnp.dot(weights, tool_block, preferred_element_type=jnp.float32),
        "col",
        scatter_dimension=0,
        tiled=True,
    )
    mapped_queries = (summed / own_totals[:, None]).astype(jnp.bfloat16)
    return (mapped_queries, query_potential, tool_potential)


def solution(mesh):
    in_specs = (P(("row", "col"), None), P(("col", "row"), None), P("row"), P("col"))
    out_specs = (P(("row", "col"), None), P("row"), P("col"))
    return jax.shard_map(local, mesh=mesh, in_specs=in_specs, out_specs=out_specs, check_vma=False)
```

profile of v0, /device:TPU:0, one launch (start us, length us, event | category | flops | bytes accessed | tf_op | source)
XLA Modules:
  0.0 277.5 jit_solution(328591060711582152)
XLA Ops:
  7.2 0.0 all-gather.5.cloned.1.call-start
  7.2 0.7 all-gather.5.cloned.1.call-update
  7.9 0.0 all-gather.3.cloned.1.call-start
  7.9 0.7 all-gather.3.cloned.1.call-update
  8.6 0.0 reduce-scatter.2.cloned.1.call-start
  8.7 31.6 %all-gather.5.cloned.1.call-done = bf16[768,768]{1,0:T(8,128)(2,1)} async-done(((bf16[192,768]{1,0:T(8,128)(2,1)}), bf16[768,768]{1,0:T(8,128)(2,1)}) %all-gather.5.cloned.1.call-update) | async-done | bytes 1179664 | tf_op jit(solution)/shard_map/all_gather | solution.py:29
  40.3 26.7 %all-gather.3.cloned.1.call-done = bf16[1024,768]{1,0:T(8,128)(2,1)} async-done(((bf16[128,768]{1,0:T(8,128)(2,1)}), bf16[1024,768]{1,0:T(8,128)(2,1)}) %all-gather.3.cloned.1.call-update) | async-done | bytes 1572880 | tf_op jit(solution)/shard_map/all_gather | solution.py:33
  67.0 3.2 %fusion = (f32[1024]{0:T(1024)S(1)}, f32[1024,768]{0,1:T(8,128)S(1)}) fusion(bf16[1024,768]{1,0:T(8,128)(2,1)} %all-gather.3.cloned.1.call-done, bf16[768,768]{1,0:T(8,128)(2,1)} %all-gather.5.cloned.1.call-done), kind=kOutput, calls=%fused_computation.14 | convolution fusion | flops 1211104256 | bytes 5902336 | tf_op jit(solution)/shard_map/dot_general | solution.py:32
  70.2 0.0 copy-start.2
  70.2 15.4 %pmax.49 = f32[1024]{0:T(1024)S(1)} all-reduce(f32[1024]{0:T(1024)S(1)} %get-tuple-element.3), channel_id=1, replica_groups=mesh['row'=4,'col'=8] {'col'}, use_global_device_ids=true, to_apply=%region_1.0 | all-reduce | flops 1024 | bytes 8192 | tf_op jit(solution)/shard_map/pmax | solution.py:16
  85.6 0.6 exponential_reduce_fusion.5
  86.2 13.6 %psum.49 = f32[1024]{0:T(1024)S(1)} all-reduce(f32[1024]{0:T(1024)S(1)} %exponential_reduce_fusion.5), channel_id=1, replica_groups=mesh['row'=4,'col'=8] {'col'}, use_global_device_ids=true, to_apply=%region_3.0 | all-reduce | flops 1024 | bytes 8192 | tf_op jit(solution)/shard_map/psum | solution.py:17
  99.8 0.0 copy-done.2
  99.9 0.0 copy-start.3
  99.9 0.4 fusion.1
  100.3 9.8 %pmax.50 = f32[768]{0:T(1024)S(1)} all-reduce(f32[768]{0:T(1024)S(1)} %fusion.1), channel_id=1, replica_groups=mesh['row'=4,'col'=8] {'row'}, use_global_device_ids=true, to_apply=%region_5.0 | all-reduce | flops 768 | bytes 6144 | tf_op jit(solution)/shard_map/pmax | solution.py:23
  110.1 0.8 exponential_reduce_fusion.4
  110.9 8.0 %psum.50 = f32[768]{0:T(1024)S(1)} all-reduce(f32[768]{0:T(1024)S(1)} %exponential_reduce_fusion.4), channel_id=1, replica_groups=mesh['row'=4,'col'=8] {'row'}, use_global_device_ids=true, to_apply=%region_7.0 | all-reduce | flops 768 | bytes 6144 | tf_op jit(solution)/shard_map/psum | solution.py:24
  118.9 0.0 copy-done.3
  119.0 0.4 fusion.2
  119.4 13.6 %pmax.51 = f32[1024]{0:T(1024)S(1)} all-reduce(f32[1024]{0:T(1024)S(1)} %fusion.2), channel_id=1, replica_groups=mesh['row'=4,'col'=8] {'col'}, use_global_device_ids=true, to_apply=%region_9.0 | all-reduce | flops 1024 | bytes 8192 | tf_op jit(solution)/shard_map/pmax | solution.py:16
  133.0 0.7 exponential_reduce_fusion.3
  133.7 13.6 %psum.51 = f32[1024]{0:T(1024)S(1)} all-reduce(f32[1024]{0:T(1024)S(1)} %exponential_reduce_fusion.3), channel_id=1, replica_groups=mesh['row'=4,'col'=8] {'col'}, use_global_device_ids=true, to_apply=%region_11.0 | all-reduce | flops 1024 | bytes 8192 | tf_op jit(solution)/shard_map/psum | solution.py:17
  147.3 0.4 fusion.3
  147.7 8.9 %pmax.52 = f32[768]{0:T(1024)S(1)} all-reduce(f32[768]{0:T(1024)S(1)} %fusion.3), channel_id=1, replica_groups=mesh['row'=4,'col'=8] {'row'}, use_global_device_ids=true, to_apply=%region_13.0 | all-reduce | flops 768 | bytes 6144 | tf_op jit(solution)/shard_map/pmax | solution.py:23
  156.6 0.8 exponential_reduce_fusion.2
  157.4 8.1 %psum.52 = f32[768]{0:T(1024)S(1)} all-reduce(f32[768]{0:T(1024)S(1)} %exponential_reduce_fusion.2), channel_id=1, replica_groups=mesh['row'=4,'col'=8] {'row'}, use_global_device_ids=true, to_apply=%region_15.0 | all-reduce | flops 768 | bytes 6144 | tf_op jit(solution)/shard_map/psum | solution.py:24
  165.5 0.4 fusion.4
  165.9 13.6 %pmax.53 = f32[1024]{0:T(1024)S(1)} all-reduce(f32[1024]{0:T(1024)S(1)} %fusion.4), channel_id=1, replica_groups=mesh['row'=4,'col'=8] {'col'}, use_global_device_ids=true, to_apply=%region_17.0 | all-reduce | flops 1024 | bytes 8192 | tf_op jit(solution)/shard_map/pmax | solution.py:16
  179.5 0.7 exponential_reduce_fusion.1
  180.2 13.6 %psum.53 = f32[1024]{0:T(1024)S(1)} all-reduce(f32[1024]{0:T(1024)S(1)} %exponential_reduce_fusion.1), channel_id=1, replica_groups=mesh['row'=4,'col'=8] {'col'}, use_global_device_ids=true, to_apply=%region_19.0 | all-reduce | flops 1024 | bytes 8192 | tf_op jit(solution)/shard_map/psum | solution.py:17
  193.8 0.0 copy-start
  193.8 0.4 fusion.5
  194.2 9.7 %pmax.54 = f32[768]{0:T(1024)S(1)} all-reduce(f32[768]{0:T(1024)S(1)} %fusion.5), channel_id=1, replica_groups=mesh['row'=4,'col'=8] {'row'}, use_global_device_ids=true, to_apply=%region_21.0 | all-reduce | flops 768 | bytes 6144 | tf_op jit(solution)/shard_map/pmax | solution.py:23
  203.9 0.8 exponential_reduce_fusion
  204.7 0.0 copy-done
  204.7 8.1 %psum.54 = f32[768]{0:T(1024)S(1)} all-reduce(f32[768]{0:T(1024)S(1)} %exponential_reduce_fusion), channel_id=1, replica_groups=mesh['row'=4,'col'=8] {'row'}, use_global_device_ids=true, to_apply=%region_23.0 | all-reduce | flops 768 | bytes 6144 | tf_op jit(solution)/shard_map/psum | solution.py:24
  212.8 0.0 copy-start.1
  212.8 0.4 fusion.6
  213.2 13.6 %pmax.55 = f32[1024]{0:T(1024)S(1)} all-reduce(f32[1024]{0:T(1024)S(1)} %fusion.6), channel_id=1, replica_groups=mesh['row'=4,'col'=8] {'col'}, use_global_device_ids=true, to_apply=%region_25.0 | all-reduce | flops 1024 | bytes 8192 | tf_op jit(solution)/shard_map/pmax | solution.py:51
  226.8 4.5 %fusion.9 = f32[1024,768]{1,0:T(8,128)} fusion(bf16[768,768]{1,0:T(8,128)(2,1)} %all-gather.5.cloned.1.call-done, f32[1024,768]{0,1:T(8,128)S(1)} %get-tuple-element.4, f32[1024]{0:T(1024)S(1)} %pmax.55, f32[768]{0:T(1024)S(1)} %multiply_subtract_fusion), kind=kOutput, calls=%fused_computation.24 | convolution fusion | flops 1211105280 | bytes 7478272 | tf_op jit(solution)/shard_map/dot_general | solution.py:59
  231.3 0.0 reduce-scatter.2.cloned.1.call-update
  231.3 0.0 copy-done.1
  231.3 0.7 fusion.7
  232.0 13.9 %psum.55 = f32[1024]{0:T(1024)S(1)} all-reduce(f32[1024]{0:T(1024)S(1)} %fusion.7), channel_id=1, replica_groups=mesh['row'=4,'col'=8] {'col'}, use_global_device_ids=true, to_apply=%region_28.0 | all-reduce | flops 1024 | bytes 8192 | tf_op jit(solution)/shard_map/psum | solution.py:56
  245.9 0.1 dynamic_slice.3
  246.0 23.3 %reduce-scatter.2.cloned.1.call-done = f32[128,768]{1,0:T(8,128)} async-done(((f32[1024,768]{1,0:T(8,128)}), f32[128,768]{1,0:T(8,128)}) %reduce-scatter.2.cloned.1.call-update) | async-done | bytes 393232 | tf_op jit(solution)/shard_map/reduce_scatter | solution.py:58
  269.2 1.8 divide_convert_fusion
  (6 shorter events, 0.1 us)
Async XLA Ops:
  7.2 33.1 %all-gather.5.cloned.1.call-start = ((), (), s32[]{:S(2)}) async-start(), calls=%async_computation.2 | async-start | bytes 1474560 | tf_op jit(solution)/shard_map/all_gather | solution.py:29
  7.9 59.1 %all-gather.3.cloned.1.call-start = ((), (), s32[]{:S(2)}) async-start(), calls=%async_computation.1 | async-start | bytes 1769472 | tf_op jit(solution)/shard_map/all_gather | solution.py:33
  8.6 260.6 %reduce-scatter.2.cloned.1.call-start = ((), (), s32[]{:S(2)}) async-start(), calls=%async_computation.3 | async-start | bytes 3538944 | tf_op jit(solution)/shard_map/reduce_scatter | solution.py:58
  70.2 29.6 %copy-start.2 = (f32[1024]{0:T(1024)S(1)}, f32[1024]{0:T(1024)}, u32[]{:S(2)}) copy-start(f32[1024]{0:T(1024)} %param.6) | copy-start | bytes 12292
  99.9 19.1 %copy-start.3 = (f32[768]{0:T(1024)S(1)}, f32[768]{0:T(1024)}, u32[]{:S(2)}) copy-start(f32[768]{0:T(1024)} %param.7) | copy-start | bytes 9220
  193.8 10.9 %copy-start = (f32[1024]{0:T(1024)}, f32[1024]{0:T(1024)S(1)}, u32[]{:S(2)}) copy-start(f32[1024]{0:T(1024)S(1)} %multiply_subtract_fusion.1) | copy-start | bytes 12292
  212.8 18.6 %copy-start.1 = (f32[768]{0:T(1024)}, f32[768]{0:T(1024)S(1)}, u32[]{:S(2)}) copy-start(f32[768]{0:T(1024)S(1)} %multiply_subtract_fusion) | copy-start | bytes 9220
Sparse Core Ops, SparseCore 0:
  9.8 30.4 all-gather.4
  41.9 25.0 all-gather.2
  231.4 37.7 reduce-scatter.1
where the time goes:
time: 278 us
  blocking collectives  163 us (59%)
  waiting for transfers between devices  83 us (30%)
  between operations  13.9 us (5%)
  other arithmetic  9.27 us (3%)
  matrix products  7.72 us (3%)
    pmax x3, blocking collectives, row_lse(): highest = lax.pmax(local_max, 'col')  42.6 us
    psum x3, blocking collectives, row_lse(): lax.psum(jnp.sum(jnp.exp(scores - highest[:, None]), axis=1), 'col')  40.8 us
    all_gather x1, waiting for transfers between devices, local(): tool_block = lax.all_gather(tools, 'row', axis=0, tiled=True)  31.6 us
    pmax x3, blocking collectives, column_lse(): highest = lax.pmax(local_max, 'row')  28.5 us
    all_gather x1, waiting for transfers between devices, local(): lax.all_gather(queries, 'col', axis=0, tiled=True)  26.7 us
    psum x3, blocking collectives, column_lse(): lax.psum(jnp.sum(jnp.exp(scores - highest[None, :]), axis=0), 'row')  24.1 us
    reduce_scatter x1, waiting for transfers between devices, local(): lax.psum_scatter(jnp.dot(weights, tool_block, preferred_element_type=jnp....  23.3 us
    psum x1, blocking collectives, local(): totals = lax.psum(local_total, 'col')  13.9 us
  transfers between devices with their start and end apart: 3, of which 3 were waited for; matrix products, arithmetic and copies ran while one was open for 0% of the time, Pallas kernels for 0%

commit v1 on v0

v1 whole, which is shorter than its diff:
```python
import math

import jax
import jax.numpy as jnp
from jax import lax
from jax.sharding import PartitionSpec as P

ITERS = 3
EPSILON = 0.5
LOG2E = 1.0 / math.log(2.0)


def swap(x, axis, k):
    n = lax.axis_size(axis)
    return lax.ppermute(x, axis, [(i, i ^ k) for i in range(n)])


def place(blocks, index):
    whole = jnp.zeros((len(blocks),) + blocks[0].shape, blocks[0].dtype)
    for k, block in enumerate(blocks):
        whole = lax.dynamic_update_index_in_dim(whole, block, index ^ k, 0)
    return whole


def lse_of(parts):
    highest = parts[0]
    for part in parts[1:]:
        highest = jnp.maximum(highest, part)
    total = jnp.exp2(parts[0] - highest)
    for part in parts[1:]:
        total = total + jnp.exp2(part - highest)
    return highest + jnp.log2(total)


def local_lse(scores, axis):
    highest = jnp.max(scores, axis=axis, keepdims=True)
    total = jnp.sum(jnp.exp2(scores - highest), axis=axis)
    return jnp.squeeze(highest, axis) + jnp.log2(total)


def dot_t(a, b):
    return lax.dot_general(a, b, (((1,), (1,)), ((), ())), preferred_element_type=jnp.float32)


def local(queries, tools, query_mass, tool_mass):
    rows, cols = lax.axis_size("row"), lax.axis_size("col")
    ri, ci = lax.axis_index("row"), lax.axis_index("col")
    chips = cols // 2
    zi, core = ci // 2, ci % 2
    bq, features = queries.shape
    bt = tools.shape[0]
    scaling = LOG2E / (math.sqrt(features) * EPSILON)

    own = place([queries] + [swap(queries, "col", 2 * k) for k in range(1, chips)], zi)
    near = swap(tools, "col", 2)
    near_mass = swap(tool_mass, "col", 2)
    tile_tools = []
    for source in (tools, near):
        tile_tools.append(place([source] + [swap(source, "row", k) for k in range(1, rows)], ri))
    far = [swap(tools, "col", 4 * j + b) for j in range(1, chips // 2) for b in (0, 2)]
    sibling_query = swap(queries, "col", 1)
    both = place([own, swap(own, "col", 1)], core)
    tile_queries = both.reshape(-1, features)
    tile_tools = jnp.stack(tile_tools).reshape(-1, features)

    tile = dot_t(tile_queries, tile_tools) * scaling
    log_query = jnp.log2(query_mass).reshape(chips, 2, bq).transpose(1, 0, 2).reshape(-1)
    log_tool = jnp.log2(jnp.concatenate([tool_mass, near_mass]))

    far_peers = [4 * j for j in range(1, chips // 2)]
    query_side = None
    tool_side = jnp.zeros((tile.shape[1],), jnp.float32)
    for sweep in range(ITERS):
        part = local_lse(tile + tool_side[None, :], 1)
        part = lse_of([part, swap(part, "col", 1)])
        part = lse_of([part] + [swap(part, "col", k) for k in far_peers])
        query_side = log_query - part
        if sweep == 0:
            far, query_side = lax.optimization_barrier((far, query_side))
            spread = jnp.stack(far)
            spread = [spread] + [swap(spread, "row", k) for k in range(1, rows)]
        part = local_lse(tile + query_side[:, None], 0)
        part = lse_of([part] + [swap(part, "row", k) for k in range(1, rows)])
        tool_side = log_tool - part

    far_tools = jnp.moveaxis(place(spread, ri), 0, 1).reshape(-1, features)
    chip_queries = jnp.concatenate([queries, sibling_query])
    far_tile = dot_t(chip_queries, far_tools) * scaling
    by_block = tile.reshape(2, chips, bq, -1)
    near_tile = jnp.concatenate(
        [lax.dynamic_slice(by_block, (c, zi, 0, 0), (1, 1) + by_block.shape[2:])[0, 0] for c in (core, 1 - core)]
    )
    far_side = jnp.concatenate([swap(tool_side, "col", k) for k in far_peers])
    near_scores = near_tile + tool_side[None, :]
    far_scores = far_tile + far_side[None, :]
    peak = jnp.maximum(jnp.max(near_scores, axis=1), jnp.max(far_scores, axis=1))
    other = swap(peak, "col", 1)
    peak = jnp.maximum(peak, jnp.concatenate([other[bq:], other[:bq]]))
    near_exps = jnp.exp2(near_scores - peak[:, None])
    far_exps = jnp.exp2(far_scores - peak[:, None])
    total = jnp.sum(near_exps, axis=1) + jnp.sum(far_exps, axis=1)
    summed = jnp.dot(near_exps.astype(jnp.bfloat16), tile_tools, preferred_element_type=jnp.float32)
    summed = summed + jnp.dot(far_exps.astype(jnp.bfloat16), far_tools, preferred_element_type=jnp.float32)
    total = total[:bq] + swap(total[bq:], "col", 1)
    summed = summed[:bq] + swap(summed[bq:], "col", 1)
    mapped = (summed / total[:, None]).astype(jnp.bfloat16)

    unit = EPSILON / LOG2E
    query_potential = unit * query_side.reshape(2, chips, bq).transpose(1, 0, 2).reshape(-1)
    tool_potential = unit * tool_side[: tool_mass.shape[0]]
    return (mapped, query_potential, tool_potential)


def solution(mesh):
    in_specs = (P(("row", "col"), None), P(("col", "row"), None), P("row"), P("col"))
    out_specs = (P(("row", "col"), None), P("row"), P("col"))
    return jax.shard_map(local, mesh=mesh, in_specs=in_specs, out_specs=out_specs, check_vma=False)
```

time: 278 us -> 160 us (0.58)
  blocking collectives: 163 us -> 0 us
  starting transfers between devices: 0.11 us -> 40.5 us
  between operations: 13.9 us -> 1.14 us
  waiting for transfers between devices: 83 us -> 92.4 us
  other arithmetic: 9.27 us -> 16.1 us
  local copies, waits for them, and re-layouts: 0.1 us -> 3.92 us
    ppermute x0 -> x37, waiting for transfers between devices: none -> 92.4 us  [swap(): return lax.ppermute(x, axis, [(i, i ^ k) for i in range(n)])]
    pmax x7 -> x0, blocking collectives: 84.7 us -> none  [the longest x3 42.6 us: row_lse(): highest = lax.pmax(local_max, 'col')]
    psum x7 -> x0, blocking collectives: 78.8 us -> none  [the longest x3 40.8 us: row_lse(): lax.psum(jnp.sum(jnp.exp(scores - highest[:, None]), axis=1), 'col')]
    all_gather x2 -> x0, waiting for transfers between devices: 58.3 us -> none  [the longest x1 31.6 us: local(): tool_block = lax.all_gather(tools, 'row', axis=0, tiled=True)]
    ppermute x0 -> x37, starting transfers between devices: none -> 40.5 us  [swap(): return lax.ppermute(x, axis, [(i, i ^ k) for i in range(n)])]
    reduce_scatter x1 -> x0, waiting for transfers between devices: 23.3 us -> none  [local(): lax.psum_scatter(jnp.dot(weights, tool_block, preferred_element_type=jnp....]
    reduce_sum x7, other arithmetic: 5.14 us -> 8.53 us  [the longest x6 7.82 us: local_lse(): total = jnp.sum(jnp.exp2(scores - highest), axis=axis)]
    reduce_max x6, other arithmetic: 2.3 us -> 5.59 us  [the longest x5 5.4 us: local_lse(): highest = jnp.max(scores, axis=axis, keepdims=True)]
  transfers between devices with their start and end apart: 3 -> 37, of which waited for: 3 -> 19; matrix products, arithmetic and copies ran while one was open for 0% -> 7% of each run, Pallas kernels for 0% -> 0%
where the time goes in v1:
time: 160 us; the launch traced here: 159 us
  waiting for transfers between devices  92.4 us (58%)
  starting transfers between devices  40.5 us (25%)
  other arithmetic  16.1 us (10%)
  matrix products  5.42 us (3%)
  local copies, waits for them, and re-layouts  3.92 us (2%)
    ppermute x37, waiting for transfers between devices, swap(): return lax.ppermute(x, axis, [(i, i ^ k) for i in range(n)])  92.4 us
    ppermute x37, starting transfers between devices, swap(): return lax.ppermute(x, axis, [(i, i ^ k) for i in range(n)])  40.5 us
    reduce_sum x6, other arithmetic, local_lse(): total = jnp.sum(jnp.exp2(scores - highest), axis=axis)  7.82 us
    reduce_max x5, other arithmetic, local_lse(): highest = jnp.max(scores, axis=axis, keepdims=True)  5.4 us
    dot_general x2, matrix products, dot_t(): lax.dot_general(a, b, (((1,), (1,)), ((), ())), preferred_element_type=jn...  3.63 us
  transfers between devices with their start and end apart: 37, of which 19 were waited for; matrix products, arithmetic and copies ran while one was open for 7% of the time, Pallas kernels for 0%

profile of v1, /device:TPU:0, one launch (start us, length us, event | category | flops | bytes accessed | tf_op | source)
XLA Modules:
  0.0 159.4 jit_solution(7863773480232072006)
XLA Ops:
  0.7 3.1 %collective-permute-start = (bf16[128,768]{1,0:T(8,128)(2,1)}, bf16[128,768]{1,0:T(8,128)(2,1)S(1)}, u32[]{:S(2)}, u32[]{:S(2)}) collective-permute-start(bf16[128,768]{1,0:T(8,128)(2,1)} %param.4), channel_id=1, source_target_pairs={{0,2},{1,3},{2,0},{3,1},{4,6},{5,7},{6,4},{7,5},{8,10},{9,11},{10,... | collective-permute-start | bytes 589832 | tf_op jit(solution)/shard_map/ppermute | solution.py:15
  3.7 2.6 %collective-permute-start.1 = (bf16[128,768]{1,0:T(8,128)(2,1)}, bf16[128,768]{1,0:T(8,128)(2,1)S(1)}, u32[]{:S(2)}, u32[]{:S(2)}) collective-permute-start(bf16[128,768]{1,0:T(8,128)(2,1)} %param.4), channel_id=1, source_target_pairs={{0,4},{1,5},{2,6},{3,7},{4,0},{5,1},{6,2},{7,3},{8,12},{9,13},{10,... | collective-permute-start | bytes 589832 | tf_op jit(solution)/shard_map/ppermute | solution.py:15
  6.3 0.9 collective-permute-start.7
  7.2 1.5 collective-permute-start.4
  8.8 1.0 bitcast_dynamic-update-slice_fusion.13
  9.9 3.2 %collective-permute-done = bf16[128,768]{1,0:T(8,128)(2,1)S(1)} collective-permute-done((bf16[128,768]{1,0:T(8,128)(2,1)}, bf16[128,768]{1,0:T(8,128)(2,1)S(1)}, u32[]{:S(2)}, u32[]{:S(2)}) %collective-permute-start) | collective-permute-done | bytes 196640 | tf_op jit(solution)/shard_map/ppermute | solution.py:15
  13.1 2.0 %collective-permute-start.5 = (bf16[192,768]{1,0:T(8,128)(2,1)S(1)}, bf16[192,768]{1,0:T(8,128)(2,1)S(1)}, u32[]{:S(2)}, u32[]{:S(2)}) collective-permute-start(bf16[192,768]{1,0:T(8,128)(2,1)S(1)} %copy-done.2), channel_id=1, source_target_pairs={{0,16},{8,24},{16,0},{24,8},{1,17},{9,25},{17,1},{25,9},{2,18},{10... | collective-permute-start | bytes 884744 | tf_op jit(solution)/shard_map/ppermute | solution.py:15
  15.2 6.0 %collective-permute-done.1 = bf16[128,768]{1,0:T(8,128)(2,1)S(1)} collective-permute-done((bf16[128,768]{1,0:T(8,128)(2,1)}, bf16[128,768]{1,0:T(8,128)(2,1)S(1)}, u32[]{:S(2)}, u32[]{:S(2)}) %collective-permute-start.1) | collective-permute-done | bytes 196640 | tf_op jit(solution)/shard_map/ppermute | solution.py:15
  21.1 2.4 %collective-permute-start.6 = (bf16[192,768]{1,0:T(8,128)(2,1)S(1)}, bf16[192,768]{1,0:T(8,128)(2,1)S(1)}, u32[]{:S(2)}, u32[]{:S(2)}) collective-permute-start(bf16[192,768]{1,0:T(8,128)(2,1)S(1)} %copy-done.2), channel_id=1, source_target_pairs={{0,24},{8,16},{16,8},{24,0},{1,25},{9,17},{17,9},{25,1},{2,26},{10... | collective-permute-start | bytes 884744 | tf_op jit(solution)/shard_map/ppermute | solution.py:15
  23.9 1.3 collective-permute-start.8
  25.4 1.6 collective-permute-start.9
  27.8 2.8 %collective-permute-done.6 = bf16[192,768]{1,0:T(8,128)(2,1)S(1)} collective-permute-done((bf16[192,768]{1,0:T(8,128)(2,1)S(1)}, bf16[192,768]{1,0:T(8,128)(2,1)S(1)}, u32[]{:S(2)}, u32[]{:S(2)}) %collective-permute-start.6) | collective-permute-done | bytes 294944 | tf_op jit(solution)/shard_map/ppermute | solution.py:15
  30.6 6.3 %collective-permute-done.8 = bf16[192,768]{1,0:T(8,128)(2,1)S(1)} collective-permute-done((bf16[192,768]{1,0:T(8,128)(2,1)S(1)}, bf16[192,768]{1,0:T(8,128)(2,1)S(1)}, u32[]{:S(2)}, u32[]{:S(2)}) %collective-permute-start.8) | collective-permute-done | bytes 294944 | tf_op jit(solution)/shard_map/ppermute | solution.py:15
  37.0 4.7 %collective-permute-done.9 = bf16[192,768]{1,0:T(8,128)(2,1)S(1)} collective-permute-done((bf16[192,768]{1,0:T(8,128)(2,1)S(1)}, bf16[192,768]{1,0:T(8,128)(2,1)S(1)}, u32[]{:S(2)}, u32[]{:S(2)}) %collective-permute-start.9) | collective-permute-done | bytes 294944 | tf_op jit(solution)/shard_map/ppermute | solution.py:15
  42.0 2.7 %fusion.41 = (f32[1024]{0:T(1024)S(1)}, f32[1024,1536]{1,0:T(8,128)S(1)}) fusion(bf16[1024,768]{1,0:T(8,128)(2,1)S(1)} %bitcast.72, bf16[1536,768]{1,0:T(8,128)(2,1)S(1)} %bitcast.70), kind=kOutput, calls=%fused_computation.103 | convolution fusion | flops 2419063808 | bytes 10227712 | tf_op jit(solution)/shard_map/dot_general | solution.py:42
  44.8 1.2 exponential_reduce_fusion.5
  46.0 1.4 collective-permute-start.12
  47.4 1.4 collective-permute-start.13
  48.8 1.8 %collective-permute-start.15 = (f32[1024]{0:T(1024)S(1)}, f32[1024]{0:T(1024)S(1)}, u32[]{:S(2)}, u32[]{:S(2)}) collective-permute-start(f32[1024]{0:T(1024)S(1)} %multiply_add_fusion.7), channel_id=1, source_target_pairs={{0,4},{1,5},{2,6},{3,7},{4,0},{5,1},{6,2},{7,3},{8,12},{9,13},{10,... | collective-permute-start | bytes 12296 | tf_op jit(solution)/shard_map/ppermute | solution.py:15
  50.6 24.6 %collective-permute-done.15 = f32[1024]{0:T(1024)S(1)} collective-permute-done((f32[1024]{0:T(1024)S(1)}, f32[1024]{0:T(1024)S(1)}, u32[]{:S(2)}, u32[]{:S(2)}) %collective-permute-start.15) | collective-permute-done | bytes 4128 | tf_op jit(solution)/shard_map/ppermute | solution.py:15
  75.8 1.3 exponential_reduce_fusion.4
  77.1 1.3 collective-permute-start.16
  78.5 1.8 %collective-permute-start.17 = (f32[1536]{0:T(1024)S(1)}, f32[1536]{0:T(1024)S(1)}, u32[]{:S(2)}, u32[]{:S(2)}) collective-permute-start(f32[1536]{0:T(1024)S(1)} %multiply_add_fusion.2), channel_id=1, source_target_pairs={{0,16},{8,24},{16,0},{24,8},{1,17},{9,25},{17,1},{25,9},{2,18},{10... | collective-permute-start | bytes 18440 | tf_op jit(solution)/shard_map/ppermute | solution.py:15
  81.2 3.1 %collective-permute-done.11 = f32[768]{0:T(1024)S(1)} collective-permute-done((f32[768]{0:T(1024)S(1)}, f32[768]{0:T(1024)S(1)}, u32[]{:S(2)}, u32[]{:S(2)}) %collective-permute-start.11) | collective-permute-done | bytes 3104 | tf_op jit(solution)/shard_map/ppermute | solution.py:15
  85.4 1.4 exponential_reduce_fusion.3
  86.8 1.2 collective-permute-done.19
  88.0 1.0 collective-permute-start.20
  89.0 3.5 %collective-permute-done.20 = f32[1024]{0:T(1024)S(1)} collective-permute-done((f32[1024]{0:T(1024)S(1)}, f32[1024]{0:T(1024)S(1)}, u32[]{:S(2)}, u32[]{:S(2)}) %collective-permute-start.20) | collective-permute-done | bytes 4128 | tf_op jit(solution)/shard_map/ppermute | solution.py:15
  93.1 1.3 exponential_reduce_fusion.2
  95.2 1.8 %collective-permute-start.22 = (f32[1536]{0:T(1024)S(1)}, f32[1536]{0:T(1024)S(1)}, u32[]{:S(2)}, u32[]{:S(2)}) collective-permute-start(f32[1536]{0:T(1024)S(1)} %multiply_add_fusion.1), channel_id=1, source_target_pairs={{0,16},{8,24},{16,0},{24,8},{1,17},{9,25},{17,1},{25,9},{2,18},{10... | collective-permute-start | bytes 18440 | tf_op jit(solution)/shard_map/ppermute | solution.py:15
  97.1 0.9 collective-permute-start.23
  98.9 2.7 %collective-permute-done.23 = f32[1536]{0:T(1024)S(1)} collective-permute-done((f32[1536]{0:T(1024)S(1)}, f32[1536]{0:T(1024)S(1)}, u32[]{:S(2)}, u32[]{:S(2)}) %collective-permute-start.23) | collective-permute-done | bytes 6176 | tf_op jit(solution)/shard_map/ppermute | solution.py:15
  101.6 3.4 %add_reduce_fusion.1 = f32[1024]{0:T(1024)S(1)} fusion(f32[1024,1536]{1,0:T(8,128)} %copy-done, f32[1536]{0:T(1024)S(1)} %add_subtract_fusion.1), kind=kLoop, calls=%fused_computation.7 | loop fusion | flops 3144704 | bytes 6301696 | tf_op jit(solution)/shard_map/reduce_max | solution.py:36
  105.1 1.2 copy-done.1
  106.2 1.4 exponential_reduce_fusion.1
  107.8 1.0 collective-permute-done.24
  109.5 1.6 collective-permute-start.30
  111.0 2.4 %collective-permute-done.25 = f32[1024]{0:T(1024)S(1)} collective-permute-done((f32[1024]{0:T(1024)S(1)}, f32[1024]{0:T(1024)S(1)}, u32[]{:S(2)}, u32[]{:S(2)}) %collective-permute-start.25) | collective-permute-done | bytes 4128 | tf_op jit(solution)/shard_map/ppermute | solution.py:15
  114.0 1.3 exponential_reduce_fusion
  115.8 1.1 collective-permute-start.27
  116.8 2.0 %collective-permute-start.28 = (f32[1536]{0:T(1024)S(1)}, f32[1536]{0:T(1024)S(1)}, u32[]{:S(2)}, u32[]{:S(2)}) collective-permute-start(f32[1536]{0:T(1024)S(1)} %multiply_add_fusion), channel_id=1, source_target_pairs={{0,24},{8,16},{16,8},{24,0},{1,25},{9,17},{17,9},{25,1},{2,26},{10... | collective-permute-start | bytes 18440 | tf_op jit(solution)/shard_map/ppermute | solution.py:15
  119.1 5.9 %collective-permute-done.26 = f32[1536]{0:T(1024)S(1)} collective-permute-done((f32[1536]{0:T(1024)S(1)}, f32[1536]{0:T(1024)S(1)}, u32[]{:S(2)}, u32[]{:S(2)}) %collective-permute-start.26) | collective-permute-done | bytes 6176 | tf_op jit(solution)/shard_map/ppermute | solution.py:15
  124.9 1.0 collective-permute-start.31
  125.9 2.0 %collective-permute-start.32 = (bf16[2,192,768]{2,1,0:T(8,128)(2,1)S(1)}, bf16[2,192,768]{2,1,0:T(8,128)(2,1)S(1)}, u32[]{:S(2)}, u32[]{:S(2)}) collective-permute-start(bf16[2,192,768]{2,1,0:T(8,128)(2,1)S(1)} %pad_maximum_fusion.1), channel_id=1, source_target_pairs={{0,24},{8,16},{16,8},{24,0},{1,25},{9,17},{17,9},{25,1},{2,26},{10... | collective-permute-start | bytes 1769480 | tf_op jit(solution)/shard_map/ppermute | solution.py:15
  127.9 1.4 collective-permute-start.33
  129.6 22.1 %collective-permute-done.31 = bf16[2,192,768]{2,1,0:T(8,128)(2,1)S(1)} collective-permute-done((bf16[2,192,768]{2,1,0:T(8,128)(2,1)S(1)}, bf16[2,192,768]{2,1,0:T(8,128)(2,1)S(1)}, u32[]{:S(2)}, u32[]{:S(2)}) %collective-permute-start.31) | collective-permute-done | bytes 589856 | tf_op jit(solution)/shard_map/ppermute | solution.py:15
  151.9 0.9 fusion.42
  155.9 0.9 fusion.10
  (108 shorter events, 14.8 us)
Async XLA Ops:
  0.6 9.2 %copy-start.3 = (bf16[128,768]{1,0:T(8,128)(2,1)S(1)}, bf16[128,768]{1,0:T(8,128)(2,1)}, u32[]{:S(2)}) copy-start(bf16[128,768]{1,0:T(8,128)(2,1)} %param.4) | copy-start | bytes 589828
  0.6 12.5 %copy-start.2 = (bf16[192,768]{1,0:T(8,128)(2,1)S(1)}, bf16[192,768]{1,0:T(8,128)(2,1)}, u32[]{:S(2)}) copy-start(bf16[192,768]{1,0:T(8,128)(2,1)} %param.5) | copy-start | bytes 884740
  0.7 12.5 %collective-permute-start = (bf16[128,768]{1,0:T(8,128)(2,1)}, bf16[128,768]{1,0:T(8,128)(2,1)S(1)}, u32[]{:S(2)}, u32[]{:S(2)}) collective-permute-start(bf16[128,768]{1,0:T(8,128)(2,1)} %param.4), channel_id=1, source_target_pairs={{0,2},{1,3},{2,0},{3,1},{4,6},{5,7},{6,4},{7,5},{8,10},{9,11},{10,... | collective-permute-start | bytes 589832 | tf_op jit(solution)/shard_map/ppermute | solution.py:15
  3.7 17.4 %collective-permute-start.1 = (bf16[128,768]{1,0:T(8,128)(2,1)}, bf16[128,768]{1,0:T(8,128)(2,1)S(1)}, u32[]{:S(2)}, u32[]{:S(2)}) collective-permute-start(bf16[128,768]{1,0:T(8,128)(2,1)} %param.4), channel_id=1, source_target_pairs={{0,4},{1,5},{2,6},{3,7},{4,0},{5,1},{6,2},{7,3},{8,12},{9,13},{10,... | collective-permute-start | bytes 589832 | tf_op jit(solution)/shard_map/ppermute | solution.py:15
  6.3 17.3 %collective-permute-start.2 = (bf16[128,768]{1,0:T(8,128)(2,1)}, bf16[128,768]{1,0:T(8,128)(2,1)S(1)}, u32[]{:S(2)}, u32[]{:S(2)}) collective-permute-start(bf16[128,768]{1,0:T(8,128)(2,1)} %param.4), channel_id=1, source_target_pairs={{0,6},{1,7},{2,4},{3,5},{4,2},{5,3},{6,0},{7,1},{8,14},{9,15},{10,... | collective-permute-start | bytes 589832 | tf_op jit(solution)/shard_map/ppermute | solution.py:15
  6.3 17.6 %collective-permute-start.7 = (bf16[192,768]{1,0:T(8,128)(2,1)}, bf16[192,768]{1,0:T(8,128)(2,1)S(1)}, u32[]{:S(2)}, u32[]{:S(2)}) collective-permute-start(bf16[192,768]{1,0:T(8,128)(2,1)} %param.5), channel_id=1, source_target_pairs={{0,2},{1,3},{2,0},{3,1},{4,6},{5,7},{6,4},{7,5},{8,10},{9,11},{10,... | collective-permute-start | bytes 884744 | tf_op jit(solution)/shard_map/ppermute | solution.py:15
  7.2 18.1 %collective-permute-start.4 = (bf16[192,768]{1,0:T(8,128)(2,1)}, bf16[192,768]{1,0:T(8,128)(2,1)S(1)}, u32[]{:S(2)}, u32[]{:S(2)}) collective-permute-start(bf16[192,768]{1,0:T(8,128)(2,1)} %param.5), channel_id=1, source_target_pairs={{0,8},{8,0},{16,24},{24,16},{1,9},{9,1},{17,25},{25,17},{2,10},{10... | collective-permute-start | bytes 884744 | tf_op jit(solution)/shard_map/ppermute | solution.py:15
  13.1 13.9 %collective-permute-start.5 = (bf16[192,768]{1,0:T(8,128)(2,1)S(1)}, bf16[192,768]{1,0:T(8,128)(2,1)S(1)}, u32[]{:S(2)}, u32[]{:S(2)}) collective-permute-start(bf16[192,768]{1,0:T(8,128)(2,1)S(1)} %copy-done.2), channel_id=1, source_target_pairs={{0,16},{8,24},{16,0},{24,8},{1,17},{9,25},{17,1},{25,9},{2,18},{10... | collective-permute-start | bytes 884744 | tf_op jit(solution)/shard_map/ppermute | solution.py:15
  21.1 9.5 %collective-permute-start.6 = (bf16[192,768]{1,0:T(8,128)(2,1)S(1)}, bf16[192,768]{1,0:T(8,128)(2,1)S(1)}, u32[]{:S(2)}, u32[]{:S(2)}) collective-permute-start(bf16[192,768]{1,0:T(8,128)(2,1)S(1)} %copy-done.2), channel_id=1, source_target_pairs={{0,24},{8,16},{16,8},{24,0},{1,25},{9,17},{17,9},{25,1},{2,26},{10... | collective-permute-start | bytes 884744 | tf_op jit(solution)/shard_map/ppermute | solution.py:15
  23.7 18.3 %collective-permute-start.3 = (bf16[4,128,768]{2,1,0:T(8,128)(2,1)S(1)}, bf16[4,128,768]{2,1,0:T(8,128)(2,1)S(1)}, u32[]{:S(2)}, u32[]{:S(2)}) collective-permute-start(bf16[4,128,768]{2,1,0:T(8,128)(2,1)S(1)} %bitcast_dynamic-update-slice_fusion.14), channel_id=1, source_target_pairs={{0,1},{1,0},{2,3},{3,2},{4,5},{5,4},{6,7},{7,6},{8,9},{9,8},{10,11... | collective-permute-start | bytes 2359304 | tf_op jit(solution)/shard_map/ppermute | solution.py:15
  23.9 13.0 %collective-permute-start.8 = (bf16[192,768]{1,0:T(8,128)(2,1)S(1)}, bf16[192,768]{1,0:T(8,128)(2,1)S(1)}, u32[]{:S(2)}, u32[]{:S(2)}) collective-permute-start(bf16[192,768]{1,0:T(8,128)(2,1)S(1)} %collective-permute-done.7), channel_id=1, source_target_pairs={{0,8},{8,0},{16,24},{24,16},{1,9},{9,1},{17,25},{25,17},{2,10},{10... | collective-permute-start | bytes 884744 | tf_op jit(solution)/shard_map/ppermute | solution.py:15
  25.4 16.3 %collective-permute-start.9 = (bf16[192,768]{1,0:T(8,128)(2,1)S(1)}, bf16[192,768]{1,0:T(8,128)(2,1)S(1)}, u32[]{:S(2)}, u32[]{:S(2)}) collective-permute-start(bf16[192,768]{1,0:T(8,128)(2,1)S(1)} %collective-permute-done.7), channel_id=1, source_target_pairs={{0,16},{8,24},{16,0},{24,8},{1,17},{9,25},{17,1},{25,9},{2,18},{10... | collective-permute-start | bytes 884744 | tf_op jit(solution)/shard_map/ppermute | solution.py:15
  27.0 14.7 %collective-permute-start.10 = (bf16[192,768]{1,0:T(8,128)(2,1)S(1)}, bf16[192,768]{1,0:T(8,128)(2,1)S(1)}, u32[]{:S(2)}, u32[]{:S(2)}) collective-permute-start(bf16[192,768]{1,0:T(8,128)(2,1)S(1)} %collective-permute-done.7), channel_id=1, source_target_pairs={{0,24},{8,16},{16,8},{24,0},{1,25},{9,17},{17,9},{25,1},{2,26},{10... | collective-permute-start | bytes 884744 | tf_op jit(solution)/shard_map/ppermute | solution.py:15
  44.7 48.4 %copy-start = (f32[1024,1536]{1,0:T(8,128)}, f32[1024,1536]{1,0:T(8,128)S(1)}, u32[]{:S(2)}) copy-start(f32[1024,1536]{1,0:T(8,128)S(1)} %get-tuple-element.18) | copy-start | bytes 18874372
  44.7 5.9 %copy-start.5 = (f32[1024]{0:T(1024)S(1)}, f32[1024]{0:T(1024)}, u32[]{:S(2)}) copy-start(f32[1024]{0:T(1024)} %param.6) | copy-start | bytes 12292
  45.9 2.9 %collective-permute-start.14 = (f32[1024]{0:T(1024)S(1)}, f32[1024]{0:T(1024)S(1)}, u32[]{:S(2)}, u32[]{:S(2)}) collective-permute-start(f32[1024]{0:T(1024)S(1)} %multiply_add_fusion.8), channel_id=1, source_target_pairs={{0,1},{1,0},{2,3},{3,2},{4,5},{5,4},{6,7},{7,6},{8,9},{9,8},{10,11... | collective-permute-start | bytes 12296 | tf_op jit(solution)/shard_map/ppermute | solution.py:15
  46.0 29.3 %collective-permute-start.12 = (bf16[192,768]{1,0:T(8,128)(2,1)S(1)}, bf16[192,768]{1,0:T(8,128)(2,1)S(1)}, u32[]{:S(2)}, u32[]{:S(2)}) collective-permute-start(bf16[192,768]{1,0:T(8,128)(2,1)S(1)} %copy-done.2), channel_id=1, source_target_pairs={{0,4},{1,5},{2,6},{3,7},{4,0},{5,1},{6,2},{7,3},{8,12},{9,13},{10,... | collective-permute-start | bytes 884744 | tf_op jit(solution)/shard_map/ppermute | solution.py:15
  47.4 27.9 %collective-permute-start.13 = (bf16[192,768]{1,0:T(8,128)(2,1)S(1)}, bf16[192,768]{1,0:T(8,128)(2,1)S(1)}, u32[]{:S(2)}, u32[]{:S(2)}) collective-permute-start(bf16[192,768]{1,0:T(8,128)(2,1)S(1)} %copy-done.2), channel_id=1, source_target_pairs={{0,6},{1,7},{2,4},{3,5},{4,2},{5,3},{6,0},{7,1},{8,14},{9,15},{10,... | collective-permute-start | bytes 884744 | tf_op jit(solution)/shard_map/ppermute | solution.py:15
  48.8 26.4 %collective-permute-start.15 = (f32[1024]{0:T(1024)S(1)}, f32[1024]{0:T(1024)S(1)}, u32[]{:S(2)}, u32[]{:S(2)}) collective-permute-start(f32[1024]{0:T(1024)S(1)} %multiply_add_fusion.7), channel_id=1, source_target_pairs={{0,4},{1,5},{2,6},{3,7},{4,0},{5,1},{6,2},{7,3},{8,12},{9,13},{10,... | collective-permute-start | bytes 12296 | tf_op jit(solution)/shard_map/ppermute | solution.py:15
  75.8 4.9 %copy-start.4 = (f32[768]{0:T(1024)S(1)}, f32[768]{0:T(1024)}, u32[]{:S(2)}) copy-start(f32[768]{0:T(1024)} %param.7) | copy-start | bytes 9220
  77.1 7.2 %collective-permute-start.16 = (f32[1536]{0:T(1024)S(1)}, f32[1536]{0:T(1024)S(1)}, u32[]{:S(2)}, u32[]{:S(2)}) collective-permute-start(f32[1536]{0:T(1024)S(1)} %multiply_add_fusion.2), channel_id=1, source_target_pairs={{0,8},{8,0},{16,24},{24,16},{1,9},{9,1},{17,25},{25,17},{2,10},{10... | collective-permute-start | bytes 18440 | tf_op jit(solution)/shard_map/ppermute | solution.py:15
  78.5 5.8 %collective-permute-start.17 = (f32[1536]{0:T(1024)S(1)}, f32[1536]{0:T(1024)S(1)}, u32[]{:S(2)}, u32[]{:S(2)}) collective-permute-start(f32[1536]{0:T(1024)S(1)} %multiply_add_fusion.2), channel_id=1, source_target_pairs={{0,16},{8,24},{16,0},{24,8},{1,17},{9,25},{17,1},{25,9},{2,18},{10... | collective-permute-start | bytes 18440 | tf_op jit(solution)/shard_map/ppermute | solution.py:15
  80.3 4.5 %collective-permute-start.18 = (f32[1536]{0:T(1024)S(1)}, f32[1536]{0:T(1024)S(1)}, u32[]{:S(2)}, u32[]{:S(2)}) collective-permute-start(f32[1536]{0:T(1024)S(1)} %multiply_add_fusion.2), channel_id=1, source_target_pairs={{0,24},{8,16},{16,8},{24,0},{1,25},{9,17},{17,9},{25,1},{2,26},{10... | collective-permute-start | bytes 18440 | tf_op jit(solution)/shard_map/ppermute | solution.py:15
  80.7 3.6 %collective-permute-start.11 = (f32[768]{0:T(1024)S(1)}, f32[768]{0:T(1024)S(1)}, u32[]{:S(2)}, u32[]{:S(2)}) collective-permute-start(f32[768]{0:T(1024)S(1)} %copy-done.4), channel_id=1, source_target_pairs={{0,2},{1,3},{2,0},{3,1},{4,6},{5,7},{6,4},{7,5},{8,10},{9,11},{10,... | collective-permute-start | bytes 9224 | tf_op jit(solution)/shard_map/ppermute | solution.py:15
  86.7 1.2 collective-permute-start.19
  88.0 4.6 %collective-permute-start.20 = (f32[1024]{0:T(1024)S(1)}, f32[1024]{0:T(1024)S(1)}, u32[]{:S(2)}, u32[]{:S(2)}) collective-permute-start(f32[1024]{0:T(1024)S(1)} %multiply_add_fusion.5), channel_id=1, source_target_pairs={{0,4},{1,5},{2,6},{3,7},{4,0},{5,1},{6,2},{7,3},{8,12},{9,13},{10,... | collective-permute-start | bytes 12296 | tf_op jit(solution)/shard_map/ppermute | solution.py:15
  94.4 3.7 %collective-permute-start.21 = (f32[1536]{0:T(1024)S(1)}, f32[1536]{0:T(1024)S(1)}, u32[]{:S(2)}, u32[]{:S(2)}) collective-permute-start(f32[1536]{0:T(1024)S(1)} %multiply_add_fusion.1), channel_id=1, source_target_pairs={{0,8},{8,0},{16,24},{24,16},{1,9},{9,1},{17,25},{25,17},{2,10},{10... | collective-permute-start | bytes 18440 | tf_op jit(solution)/shard_map/ppermute | solution.py:15
  95.2 3.7 %collective-permute-start.22 = (f32[1536]{0:T(1024)S(1)}, f32[1536]{0:T(1024)S(1)}, u32[]{:S(2)}, u32[]{:S(2)}) collective-permute-start(f32[1536]{0:T(1024)S(1)} %multiply_add_fusion.1), channel_id=1, source_target_pairs={{0,16},{8,24},{16,0},{24,8},{1,17},{9,25},{17,1},{25,9},{2,18},{10... | collective-permute-start | bytes 18440 | tf_op jit(solution)/shard_map/ppermute | solution.py:15
  97.1 4.5 %collective-permute-start.23 = (f32[1536]{0:T(1024)S(1)}, f32[1536]{0:T(1024)S(1)}, u32[]{:S(2)}, u32[]{:S(2)}) collective-permute-start(f32[1536]{0:T(1024)S(1)} %multiply_add_fusion.1), channel_id=1, source_target_pairs={{0,24},{8,16},{16,8},{24,0},{1,25},{9,17},{17,9},{25,1},{2,26},{10... | collective-permute-start | bytes 18440 | tf_op jit(solution)/shard_map/ppermute | solution.py:15
  98.0 53.9 %collective-permute-start.29 = (bf16[128,768]{1,0:T(8,128)(2,1)S(1)}, bf16[128,768]{1,0:T(8,128)(2,1)S(1)}, u32[]{:S(2)}, u32[]{:S(2)}) collective-permute-start(bf16[128,768]{1,0:T(8,128)(2,1)S(1)} %copy-done.3), channel_id=1, source_target_pairs={{0,1},{1,0},{2,3},{3,2},{4,5},{5,4},{6,7},{7,6},{8,9},{9,8},{10,11... | collective-permute-start | bytes 589832 | tf_op jit(solution)/shard_map/ppermute | solution.py:15
  101.6 4.6 %copy-start.1 = (f32[1024,1536]{1,0:T(8,128)S(1)}, f32[1024,1536]{1,0:T(8,128)}, u32[]{:S(2)}) copy-start(f32[1024,1536]{1,0:T(8,128)} %copy-done) | copy-start | bytes 18874372
  107.6 1.2 collective-permute-start.24
  108.9 4.6 %collective-permute-start.25 = (f32[1024]{0:T(1024)S(1)}, f32[1024]{0:T(1024)S(1)}, u32[]{:S(2)}, u32[]{:S(2)}) collective-permute-start(f32[1024]{0:T(1024)S(1)} %multiply_add_fusion.3), channel_id=1, source_target_pairs={{0,4},{1,5},{2,6},{3,7},{4,0},{5,1},{6,2},{7,3},{8,12},{9,13},{10,... | collective-permute-start | bytes 12296 | tf_op jit(solution)/shard_map/ppermute | solution.py:15
  109.5 20.1 %collective-permute-start.30 = (bf16[2,192,768]{2,1,0:T(8,128)(2,1)S(1)}, bf16[2,192,768]{2,1,0:T(8,128)(2,1)S(1)}, u32[]{:S(2)}, u32[]{:S(2)}) collective-permute-start(bf16[2,192,768]{2,1,0:T(8,128)(2,1)S(1)} %pad_maximum_fusion.1), channel_id=1, source_target_pairs={{0,8},{8,0},{16,24},{24,16},{1,9},{9,1},{17,25},{25,17},{2,10},{10... | collective-permute-start | bytes 1769480 | tf_op jit(solution)/shard_map/ppermute | solution.py:15
  115.3 9.6 %collective-permute-start.26 = (f32[1536]{0:T(1024)S(1)}, f32[1536]{0:T(1024)S(1)}, u32[]{:S(2)}, u32[]{:S(2)}) collective-permute-start(f32[1536]{0:T(1024)S(1)} %multiply_add_fusion), channel_id=1, source_target_pairs={{0,8},{8,0},{16,24},{24,16},{1,9},{9,1},{17,25},{25,17},{2,10},{10... | collective-permute-start | bytes 18440 | tf_op jit(solution)/shard_map/ppermute | solution.py:15
  115.8 10.1 %collective-permute-start.27 = (f32[1536]{0:T(1024)S(1)}, f32[1536]{0:T(1024)S(1)}, u32[]{:S(2)}, u32[]{:S(2)}) collective-permute-start(f32[1536]{0:T(1024)S(1)} %multiply_add_fusion), channel_id=1, source_target_pairs={{0,16},{8,24},{16,0},{24,8},{1,17},{9,25},{17,1},{25,9},{2,18},{10... | collective-permute-start | bytes 18440 | tf_op jit(solution)/shard_map/ppermute | solution.py:15
  116.8 11.0 %collective-permute-start.28 = (f32[1536]{0:T(1024)S(1)}, f32[1536]{0:T(1024)S(1)}, u32[]{:S(2)}, u32[]{:S(2)}) collective-permute-start(f32[1536]{0:T(1024)S(1)} %multiply_add_fusion), channel_id=1, source_target_pairs={{0,24},{8,16},{16,8},{24,0},{1,25},{9,17},{17,9},{25,1},{2,26},{10... | collective-permute-start | bytes 18440 | tf_op jit(solution)/shard_map/ppermute | solution.py:15
  124.9 26.8 %collective-permute-start.31 = (bf16[2,192,768]{2,1,0:T(8,128)(2,1)S(1)}, bf16[2,192,768]{2,1,0:T(8,128)(2,1)S(1)}, u32[]{:S(2)}, u32[]{:S(2)}) collective-permute-start(bf16[2,192,768]{2,1,0:T(8,128)(2,1)S(1)} %pad_maximum_fusion.1), channel_id=1, source_target_pairs={{0,16},{8,24},{16,0},{24,8},{1,17},{9,25},{17,1},{25,9},{2,18},{10... | collective-permute-start | bytes 1769480 | tf_op jit(solution)/shard_map/ppermute | solution.py:15
  125.9 25.9 %collective-permute-start.32 = (bf16[2,192,768]{2,1,0:T(8,128)(2,1)S(1)}, bf16[2,192,768]{2,1,0:T(8,128)(2,1)S(1)}, u32[]{:S(2)}, u32[]{:S(2)}) collective-permute-start(bf16[2,192,768]{2,1,0:T(8,128)(2,1)S(1)} %pad_maximum_fusion.1), channel_id=1, source_target_pairs={{0,24},{8,16},{16,8},{24,0},{1,25},{9,17},{17,9},{25,1},{2,26},{10... | collective-permute-start | bytes 1769480 | tf_op jit(solution)/shard_map/ppermute | solution.py:15
  127.9 23.9 %collective-permute-start.33 = (f32[1536]{0:T(1024)S(1)}, f32[1536]{0:T(1024)S(1)}, u32[]{:S(2)}, u32[]{:S(2)}) collective-permute-start(f32[1536]{0:T(1024)S(1)} %add_subtract_fusion), channel_id=1, source_target_pairs={{0,4},{1,5},{2,6},{3,7},{4,0},{5,1},{6,2},{7,3},{8,12},{9,13},{10,... | collective-permute-start | bytes 18440 | tf_op jit(solution)/shard_map/ppermute | solution.py:15
  152.8 1.2 collective-permute-start.34
  155.6 2.2 %collective-permute-start.36 = (f32[128]{0:T(128)S(1)}, f32[128]{0:T(128)S(1)}, u32[]{:S(2)}, u32[]{:S(2)}) collective-permute-start(f32[128]{0:T(128)S(1)} %slice.26), channel_id=1, source_target_pairs={{0,1},{1,0},{2,3},{3,2},{4,5},{5,4},{6,7},{7,6},{8,9},{9,8},{10,11... | collective-permute-start | bytes 1544 | tf_op jit(solution)/shard_map/ppermute | solution.py:15
  156.8 1.8 %collective-permute-start.35 = (f32[128,768]{1,0:T(8,128)S(1)}, f32[128,768]{1,0:T(8,128)S(1)}, u32[]{:S(2)}, u32[]{:S(2)}) collective-permute-start(f32[128,768]{1,0:T(8,128)S(1)} %slice.29), channel_id=1, source_target_pairs={{0,1},{1,0},{2,3},{3,2},{4,5},{5,4},{6,7},{7,6},{8,9},{9,8},{10,11... | collective-permute-start | bytes 1179656 | tf_op jit(solution)/shard_map/ppermute | solution.py:15

commit v2 on v1

v2 whole, which is shorter than its diff:
```python
import functools
import math

import jax
import jax.numpy as jnp
from jax import lax
from jax.sharding import Mesh
from jax.sharding import PartitionSpec as P

ITERS = 3
EPSILON = 0.5
LOG2E = 1.0 / math.log(2.0)


def swap(x, axes, k):
    n = lax.axis_size(axes)
    return lax.ppermute(x, axes, [(i, i ^ k) for i in range(n)])


def swaps(x, axes):
    return [x] + [swap(x, axes, k) for k in range(1, lax.axis_size(axes))]


def place(blocks, index):
    whole = jnp.zeros((len(blocks),) + blocks[0].shape, blocks[0].dtype)
    for k, block in enumerate(blocks):
        whole = lax.dynamic_update_index_in_dim(whole, block, index ^ k, 0)
    return whole


def pick(x, index, axis):
    return lax.dynamic_index_in_dim(x, index, axis, False)


def lse_of(parts):
    highest = parts[0]
    for part in parts[1:]:
        highest = jnp.maximum(highest, part)
    total = jnp.exp2(parts[0] - highest)
    for part in parts[1:]:
        total = total + jnp.exp2(part - highest)
    return highest + jnp.log2(total)


def local_lse(scores, axis):
    highest = jnp.max(scores, axis=axis, keepdims=True)
    total = jnp.sum(jnp.exp2(scores - highest), axis=axis)
    return jnp.squeeze(highest, axis) + jnp.log2(total)


def dot_t(a, b):
    return lax.dot_general(a, b, (((1,), (1,)), ((), ())), preferred_element_type=jnp.float32)


def local(queries, tools, query_mass, tool_mass):
    rows = lax.axis_size("row")
    nh, nl = lax.axis_size("zh"), lax.axis_size("zl")
    ri, hi, li, core = (lax.axis_index(a) for a in ("row", "zh", "zl", "core"))
    bq, features = queries.shape
    bt = tools.shape[0]
    scaling = LOG2E / (math.sqrt(features) * EPSILON)

    tile_tools = place([place(swaps(t, "row"), ri) for t in swaps(tools, "zh")], hi).reshape(-1, features)
    log_tool = jnp.log2(place(swaps(tool_mass, "zh"), hi)).reshape(-1)
    tile_queries = place(swaps(place(swaps(queries, "zh"), hi), "zl"), li)
    tile_queries = place(swaps(tile_queries, "core"), core).reshape(-1, features)
    log_query = jnp.log2(query_mass).reshape(nh, nl, 2, bq).transpose(2, 1, 0, 3).reshape(-1)

    tile = dot_t(tile_queries, tile_tools) * scaling
    tool_side = jnp.zeros((tile.shape[1],), jnp.float32)
    for sweep in range(ITERS):
        part = lse_of(swaps(local_lse(tile + tool_side[None, :], 1), "core"))
        query_side = log_query - lse_of(swaps(part, "zl"))
        part = local_lse(tile + query_side[:, None], 0)
        tool_side = log_tool - lse_of(swaps(part, "row"))

    scores = pick(tile.reshape(2, nl, nh, bq, -1), hi, 2).reshape(2 * nl * bq, -1) + tool_side[None, :]
    peak = jnp.max(scores, axis=1)
    peak = functools.reduce(jnp.maximum, swaps(peak, "core"))
    peak = functools.reduce(jnp.maximum, swaps(peak, "zl"))
    exps = jnp.exp2(scores - peak[:, None])
    total = jnp.sum(exps, axis=1).reshape(2, nl, bq)
    summed = jnp.dot(exps.astype(jnp.bfloat16), tile_tools, preferred_element_type=jnp.float32)
    summed = summed.reshape(2, nl, bq, features)
    summed, total = (pick(x, core, 0) + swap(pick(x, 1 - core, 0), "core", 1) for x in (summed, total))
    summed, total = (
        sum([pick(x, li, 0)] + [swap(pick(x, li ^ k, 0), "zl", k) for k in range(1, nl)]) for x in (summed, total)
    )
    mapped = (summed / total[:, None]).astype(jnp.bfloat16)

    unit = EPSILON / LOG2E
    query_potential = unit * query_side.reshape(2, nl, nh, bq).transpose(2, 1, 0, 3).reshape(-1)
    tool_potential = unit * pick(tool_side.reshape(nh, -1), hi, 0)
    return (mapped, query_potential, tool_potential)


def solution(mesh):
    rows, cols = mesh.shape["row"], mesh.shape["col"]
    fine = Mesh(mesh.devices.reshape(rows, 2, cols // 4, 2), ("row", "zh", "zl", "core"))
    col = ("zh", "zl", "core")
    in_specs = (P(("row",) + col, None), P(col + ("row",), None), P("row"), P(col))
    out_specs = (P(("row",) + col, None), P("row"), P(col))
    return jax.shard_map(local, mesh=fine, in_specs=in_specs, out_specs=out_specs, check_vma=False)
```

time: 160 us -> 130 us (0.81)
  waiting for transfers between devices: 92.4 us -> 64.3 us
  starting transfers between devices: 40.5 us -> 30.6 us
  local copies, waits for them, and re-layouts: 3.92 us -> 7.87 us
  other arithmetic: 16.1 us -> 18.9 us
  matrix products: 5.42 us -> 7.05 us
    ppermute x37 -> x32, waiting for transfers between devices: 92.4 us -> 64.3 us  [swap(): return lax.ppermute(x, axes, [(i, i ^ k) for i in range(n)])]
    ppermute x37 -> x32, starting transfers between devices: 40.5 us -> 30.6 us  [swap(): return lax.ppermute(x, axes, [(i, i ^ k) for i in range(n)])]
    reduce_max x5, other arithmetic: 5.4 us -> 8.34 us  [local_lse(): highest = jnp.max(scores, axis=axis, keepdims=True)]
    unnamed x12 -> x16, local copies, waits for them, and re-layouts: 1.2 us -> 3.83 us
    dot_general x2 -> x1, matrix products: 1.79 us -> 4.33 us  [local(): jnp.dot(exps.astype(jnp.bfloat16), tile_tools, preferred_element_type=jnp...]
    dot_general x2 -> x1, matrix products: 3.63 us -> 2.72 us  [dot_t(): lax.dot_general(a, b, (((1,), (1,)), ((), ())), preferred_element_type=jn...]
  transfers between devices with their start and end apart: 37 -> 32, of which waited for: 19 -> 23; matrix products, arithmetic and copies ran while one was open for 7% -> 4% of each run, Pallas kernels for 0% -> 0%
where the time goes in v2:
time: 130 us
  waiting for transfers between devices  64.3 us (49%)
  starting transfers between devices  30.6 us (24%)
  other arithmetic  18.9 us (15%)
  local copies, waits for them, and re-layouts  7.87 us (6%)
  matrix products  7.05 us (5%)
    ppermute x32, waiting for transfers between devices, swap(): return lax.ppermute(x, axes, [(i, i ^ k) for i in range(n)])  64.3 us
    ppermute x32, starting transfers between devices, swap(): return lax.ppermute(x, axes, [(i, i ^ k) for i in range(n)])  30.6 us
    reduce_max x5, other arithmetic, local_lse(): highest = jnp.max(scores, axis=axis, keepdims=True)  8.34 us
    reduce_sum x6, other arithmetic, local_lse(): total = jnp.sum(jnp.exp2(scores - highest), axis=axis)  7.77 us
    dot_general x1, matrix products, local(): jnp.dot(exps.astype(jnp.bfloat16), tile_tools, preferred_element_type=jnp...  4.33 us
    unnamed x16, local copies, waits for them, and re-layouts  3.83 us
    dynamic_update_slice x18, local copies, waits for them, and re-layouts, place(): whole = lax.dynamic_update_index_in_dim(whole, block, index ^ k, 0)  2.79 us
    dot_general x1, matrix products, dot_t(): lax.dot_general(a, b, (((1,), (1,)), ((), ())), preferred_element_type=jn...  2.72 us
  transfers between devices with their start and end apart: 32, of which 23 were waited for; matrix products, arithmetic and copies ran while one was open for 4% of the time, Pallas kernels for 0%

profile of v2, /device:TPU:0, one launch (start us, length us, event | category | flops | bytes accessed | tf_op | source)
XLA Modules:
  0.0 129.8 jit_solution(7686029867380823476)
XLA Ops:
  0.6 3.0 %collective-permute-start.3 = (bf16[192,768]{1,0:T(8,128)(2,1)}, bf16[192,768]{1,0:T(8,128)(2,1)S(1)}, u32[]{:S(2)}, u32[]{:S(2)}) collective-permute-start(bf16[192,768]{1,0:T(8,128)(2,1)} %param.5), channel_id=1, source_target_pairs={{0,8},{8,0},{16,24},{24,16},{1,9},{9,1},{17,25},{25,17},{2,10},{10... | collective-permute-start | bytes 884744 | tf_op jit(solution)/shard_map/ppermute | solution.py:17
  3.6 1.5 %collective-permute-start.4 = (bf16[192,768]{1,0:T(8,128)(2,1)}, bf16[192,768]{1,0:T(8,128)(2,1)S(1)}, u32[]{:S(2)}, u32[]{:S(2)}) collective-permute-start(bf16[192,768]{1,0:T(8,128)(2,1)} %param.5), channel_id=1, source_target_pairs={{0,16},{8,24},{16,0},{24,8},{1,17},{9,25},{17,1},{25,9},{2,18},{10... | collective-permute-start | bytes 884744 | tf_op jit(solution)/shard_map/ppermute | solution.py:17
  5.2 3.0 %collective-permute-start.6 = (bf16[192,768]{1,0:T(8,128)(2,1)}, bf16[192,768]{1,0:T(8,128)(2,1)S(1)}, u32[]{:S(2)}, u32[]{:S(2)}) collective-permute-start(bf16[192,768]{1,0:T(8,128)(2,1)} %param.5), channel_id=1, source_target_pairs={{0,4},{4,0},{1,5},{5,1},{2,6},{6,2},{3,7},{7,3},{8,12},{12,8},{9,1... | collective-permute-start | bytes 884744 | tf_op jit(solution)/shard_map/ppermute | solution.py:17
  8.3 1.0 bitcast_dynamic-update-slice_fusion.11
  9.4 0.9 bitcast_dynamic-update-slice_fusion.13
  10.3 19.0 %collective-permute-done = bf16[128,768]{1,0:T(8,128)(2,1)S(1)} collective-permute-done((bf16[128,768]{1,0:T(8,128)(2,1)}, bf16[128,768]{1,0:T(8,128)(2,1)S(1)}, u32[]{:S(2)}, u32[]{:S(2)}) %collective-permute-start) | collective-permute-done | bytes 196640 | tf_op jit(solution)/shard_map/ppermute | solution.py:17
  29.4 0.9 collective-permute-start.1
  30.4 1.6 %collective-permute-start.7 = (bf16[192,768]{1,0:T(8,128)(2,1)S(1)}, bf16[192,768]{1,0:T(8,128)(2,1)S(1)}, u32[]{:S(2)}, u32[]{:S(2)}) collective-permute-start(bf16[192,768]{1,0:T(8,128)(2,1)S(1)} %collective-permute-done.6), channel_id=1, source_target_pairs={{0,8},{8,0},{16,24},{24,16},{1,9},{9,1},{17,25},{25,17},{2,10},{10... | collective-permute-start | bytes 884744 | tf_op jit(solution)/shard_map/ppermute | solution.py:17
  31.9 1.5 %collective-permute-start.8 = (bf16[192,768]{1,0:T(8,128)(2,1)S(1)}, bf16[192,768]{1,0:T(8,128)(2,1)S(1)}, u32[]{:S(2)}, u32[]{:S(2)}) collective-permute-start(bf16[192,768]{1,0:T(8,128)(2,1)S(1)} %collective-permute-done.6), channel_id=1, source_target_pairs={{0,16},{8,24},{16,0},{24,8},{1,17},{9,25},{17,1},{25,9},{2,18},{10... | collective-permute-start | bytes 884744 | tf_op jit(solution)/shard_map/ppermute | solution.py:17
  34.5 5.1 %collective-permute-done.1 = bf16[2,128,768]{2,1,0:T(8,128)(2,1)S(1)} collective-permute-done((bf16[2,128,768]{2,1,0:T(8,128)(2,1)S(1)}, bf16[2,128,768]{2,1,0:T(8,128)(2,1)S(1)}, u32[]{:S(2)}, u32[]{:S(2)}) %collective-permute-start.1) | collective-permute-done | bytes 393248 | tf_op jit(solution)/shard_map/ppermute | solution.py:17
  40.4 6.2 %collective-permute-done.8 = bf16[192,768]{1,0:T(8,128)(2,1)S(1)} collective-permute-done((bf16[192,768]{1,0:T(8,128)(2,1)S(1)}, bf16[192,768]{1,0:T(8,128)(2,1)S(1)}, u32[]{:S(2)}, u32[]{:S(2)}) %collective-permute-start.8) | collective-permute-done | bytes 294944 | tf_op jit(solution)/shard_map/ppermute | solution.py:17
  47.1 2.7 %fusion.33 = (f32[1024]{0:T(1024)S(1)}, f32[1024,1536]{1,0:T(8,128)S(1)}) fusion(bf16[1024,768]{1,0:T(8,128)(2,1)S(1)} %bitcast.95, bf16[1536,768]{1,0:T(8,128)(2,1)S(1)} %bitcast.93), kind=kOutput, calls=%fused_computation.95 | convolution fusion | flops 2419063808 | bytes 10227712 | tf_op jit(solution)/shard_map/dot_general | solution.py:52
  49.8 1.2 exponential_reduce_fusion.5
  51.0 1.5 %copy-done = f32[1024,1536]{1,0:T(8,128)} copy-done((f32[1024,1536]{1,0:T(8,128)}, f32[1024,1536]{1,0:T(8,128)S(1)}, u32[]{:S(2)}) %copy-start) | copy-done | bytes 6291480
  52.5 3.3 %collective-permute-start.10 = (f32[768]{0:T(1024)S(1)}, f32[768]{0:T(1024)S(1)}, u32[]{:S(2)}, u32[]{:S(2)}) collective-permute-start(f32[768]{0:T(1024)S(1)} %copy-done.4), channel_id=1, source_target_pairs={{0,4},{4,0},{1,5},{5,1},{2,6},{6,2},{3,7},{7,3},{8,12},{12,8},{9,1... | collective-permute-start | bytes 9224 | tf_op jit(solution)/shard_map/ppermute | solution.py:17
  56.3 1.1 collective-permute-done.10
  57.6 1.9 %collective-permute-done.12 = f32[1024]{0:T(1024)S(1)} collective-permute-done((f32[1024]{0:T(1024)S(1)}, f32[1024]{0:T(1024)S(1)}, u32[]{:S(2)}, u32[]{:S(2)}) %collective-permute-start.12) | collective-permute-done | bytes 4128 | tf_op jit(solution)/shard_map/ppermute | solution.py:17
  59.5 3.4 %add_reduce_fusion.4 = f32[1536]{0:T(1024)S(1)} fusion(f32[1024,1536]{1,0:T(8,128)} %copy-done, f32[1024]{0:T(1024)S(1)} %add_subtract_fusion.5), kind=kLoop, calls=%fused_computation.10 | loop fusion | flops 3144192 | bytes 6301696 | tf_op jit(solution)/shard_map/reduce_max | solution.py:46
  63.0 1.2 copy-done.1
  64.1 1.3 exponential_reduce_fusion.4
  65.5 1.6 %collective-permute-start.15 = (f32[1536]{0:T(1024)S(1)}, f32[1536]{0:T(1024)S(1)}, u32[]{:S(2)}, u32[]{:S(2)}) collective-permute-start(f32[1536]{0:T(1024)S(1)} %multiply_add_fusion.2), channel_id=1, source_target_pairs={{0,24},{8,16},{16,8},{24,0},{1,25},{9,17},{17,9},{25,1},{2,26},{10... | collective-permute-start | bytes 18440 | tf_op jit(solution)/shard_map/ppermute | solution.py:17
  67.0 1.2 collective-permute-start.14
  68.2 0.8 collective-permute-start.13
  69.0 1.0 collective-permute-done.15
  70.7 1.2 collective-permute-done.13
  71.9 3.4 %add_reduce_fusion.3 = f32[1024]{0:T(1024)S(1)} fusion(f32[1024,1536]{1,0:T(8,128)} %copy-done, f32[1536]{0:T(1024)S(1)} %add_subtract_fusion.2), kind=kLoop, calls=%fused_computation.9 | loop fusion | flops 3144704 | bytes 6301696 | tf_op jit(solution)/shard_map/reduce_max | solution.py:46
  75.3 1.2 copy-done.2
  76.5 1.4 %exponential_reduce_fusion.3 = f32[1024]{0:T(1024)S(1)} fusion(f32[1024,1536]{1,0:T(8,128)S(1)} %copy-done.2, f32[1024]{0:T(1024)S(1)} %add_reduce_fusion.3, f32[1536]{0:T(1024)S(1)} %add_subtract_fusion.2), kind=kLoop, calls=%fused_computation.3 | loop fusion | flops 6290432 | bytes 6305792 | tf_op jit(solution)/shard_map/reduce_sum | solution.py:47
  77.9 1.2 collective-permute-done.16
  79.4 3.3 %collective-permute-done.17 = f32[1024]{0:T(1024)S(1)} collective-permute-done((f32[1024]{0:T(1024)S(1)}, f32[1024]{0:T(1024)S(1)}, u32[]{:S(2)}, u32[]{:S(2)}) %collective-permute-start.17) | collective-permute-done | bytes 4128 | tf_op jit(solution)/shard_map/ppermute | solution.py:17
  83.3 1.3 exponential_reduce_fusion.2
  84.6 1.9 %collective-permute-start.20 = (f32[1536]{0:T(1024)S(1)}, f32[1536]{0:T(1024)S(1)}, u32[]{:S(2)}, u32[]{:S(2)}) collective-permute-start(f32[1536]{0:T(1024)S(1)} %multiply_add_fusion.1), channel_id=1, source_target_pairs={{0,24},{8,16},{16,8},{24,0},{1,25},{9,17},{17,9},{25,1},{2,26},{10... | collective-permute-start | bytes 18440 | tf_op jit(solution)/shard_map/ppermute | solution.py:17
  87.0 1.2 collective-permute-start.18
  88.1 1.1 collective-permute-done.20
  89.2 0.9 collective-permute-done.19
  91.1 1.4 %exponential_reduce_fusion.1 = f32[1024]{0:T(1024)S(1)} fusion(f32[1024,1536]{1,0:T(8,128)S(1)} %copy-done.2, f32[1024]{0:T(1024)S(1)} %add_reduce_fusion.1, f32[1536]{0:T(1024)S(1)} %add_subtract_fusion.1), kind=kLoop, calls=%fused_computation.1 | loop fusion | flops 6290432 | bytes 6305792 | tf_op jit(solution)/shard_map/reduce_sum | solution.py:47
  92.6 1.2 collective-permute-done.21
  94.1 3.3 %collective-permute-done.22 = f32[1024]{0:T(1024)S(1)} collective-permute-done((f32[1024]{0:T(1024)S(1)}, f32[1024]{0:T(1024)S(1)}, u32[]{:S(2)}, u32[]{:S(2)}) %collective-permute-start.22) | collective-permute-done | bytes 4128 | tf_op jit(solution)/shard_map/ppermute | solution.py:17
  97.9 1.3 exponential_reduce_fusion
  99.3 1.6 %collective-permute-start.25 = (f32[1536]{0:T(1024)S(1)}, f32[1536]{0:T(1024)S(1)}, u32[]{:S(2)}, u32[]{:S(2)}) collective-permute-start(f32[1536]{0:T(1024)S(1)} %multiply_add_fusion), channel_id=1, source_target_pairs={{0,24},{8,16},{16,8},{24,0},{1,25},{9,17},{17,9},{25,1},{2,26},{10... | collective-permute-start | bytes 18440 | tf_op jit(solution)/shard_map/ppermute | solution.py:17
  100.8 1.2 collective-permute-start.24
  102.8 1.1 collective-permute-done.25
  104.5 1.2 collective-permute-done.23
  106.0 1.1 collective-permute-done.26
  107.5 3.3 %collective-permute-done.27 = f32[512]{0:T(512)S(1)} collective-permute-done((f32[512]{0:T(512)S(1)}, f32[512]{0:T(512)S(1)}, u32[]{:S(2)}, u32[]{:S(2)}) %collective-permute-start.27) | collective-permute-done | bytes 2080 | tf_op jit(solution)/shard_map/ppermute | solution.py:17
  110.8 4.3 %fusion.4 = f32[2,2,128,768]{3,2,1,0:T(8,128)S(1)} fusion(bf16[1536,768,1,1]{1,0,3,2:T(8,128)(2,1)} %bitcast.94, f32[2,2,2,128,1536]{4,3,2,1,0:T(8,128)} %bitcast.88, s32[]{:T(128)S(6)} %select_n.62, f32[2,2,128]{2,1,0:T(2,128)S(1)} %bitcast.103, f32[1536]{0:T(1024)S(1)} %add_subtract_fusion), kind=kOutput, calls=%fused_computation.18 | convolution fusion | flops 1211105280 | bytes 7086084 | tf_op jit(solution)/shard_map/dot_general | solution.py:83
  118.1 1.8 %collective-permute-start.31 = (f32[128]{0:T(128)S(1)}, f32[128]{0:T(128)S(1)}, u32[]{:S(2)}, u32[]{:S(2)}) collective-permute-start(f32[128]{0:T(128)S(1)} %fusion.31), channel_id=1, source_target_pairs={{0,2},{2,0},{1,3},{3,1},{4,6},{6,4},{5,7},{7,5},{8,10},{10,8},{9,1... | collective-permute-start | bytes 1544 | tf_op jit(solution)/shard_map/ppermute | solution.py:17
  120.5 8.5 %collective-permute-done.31 = f32[128]{0:T(128)S(1)} collective-permute-done((f32[128]{0:T(128)S(1)}, f32[128]{0:T(128)S(1)}, u32[]{:S(2)}, u32[]{:S(2)}) %collective-permute-start.31) | collective-permute-done | bytes 544 | tf_op jit(solution)/shard_map/ppermute | solution.py:17
  (107 shorter events, 13.7 us)
Async XLA Ops:
  0.6 31.3 %collective-permute-start.3 = (bf16[192,768]{1,0:T(8,128)(2,1)}, bf16[192,768]{1,0:T(8,128)(2,1)S(1)}, u32[]{:S(2)}, u32[]{:S(2)}) collective-permute-start(bf16[192,768]{1,0:T(8,128)(2,1)} %param.5), channel_id=1, source_target_pairs={{0,8},{8,0},{16,24},{24,16},{1,9},{9,1},{17,25},{25,17},{2,10},{10... | collective-permute-start | bytes 884744 | tf_op jit(solution)/shard_map/ppermute | solution.py:17
  3.6 29.8 %collective-permute-start.4 = (bf16[192,768]{1,0:T(8,128)(2,1)}, bf16[192,768]{1,0:T(8,128)(2,1)S(1)}, u32[]{:S(2)}, u32[]{:S(2)}) collective-permute-start(bf16[192,768]{1,0:T(8,128)(2,1)} %param.5), channel_id=1, source_target_pairs={{0,16},{8,24},{16,0},{24,8},{1,17},{9,25},{17,1},{25,9},{2,18},{10... | collective-permute-start | bytes 884744 | tf_op jit(solution)/shard_map/ppermute | solution.py:17
  5.2 28.9 %collective-permute-start.5 = (bf16[192,768]{1,0:T(8,128)(2,1)}, bf16[192,768]{1,0:T(8,128)(2,1)S(1)}, u32[]{:S(2)}, u32[]{:S(2)}) collective-permute-start(bf16[192,768]{1,0:T(8,128)(2,1)} %param.5), channel_id=1, source_target_pairs={{0,24},{8,16},{16,8},{24,0},{1,25},{9,17},{17,9},{25,1},{2,26},{10... | collective-permute-start | bytes 884744 | tf_op jit(solution)/shard_map/ppermute | solution.py:17
  5.2 25.2 %collective-permute-start.6 = (bf16[192,768]{1,0:T(8,128)(2,1)}, bf16[192,768]{1,0:T(8,128)(2,1)S(1)}, u32[]{:S(2)}, u32[]{:S(2)}) collective-permute-start(bf16[192,768]{1,0:T(8,128)(2,1)} %param.5), channel_id=1, source_target_pairs={{0,4},{4,0},{1,5},{5,1},{2,6},{6,2},{3,7},{7,3},{8,12},{12,8},{9,1... | collective-permute-start | bytes 884744 | tf_op jit(solution)/shard_map/ppermute | solution.py:17
  8.2 21.2 %collective-permute-start = (bf16[128,768]{1,0:T(8,128)(2,1)}, bf16[128,768]{1,0:T(8,128)(2,1)S(1)}, u32[]{:S(2)}, u32[]{:S(2)}) collective-permute-start(bf16[128,768]{1,0:T(8,128)(2,1)} %param.4), channel_id=1, source_target_pairs={{0,4},{4,0},{1,5},{5,1},{2,6},{6,2},{3,7},{7,3},{8,12},{12,8},{9,1... | collective-permute-start | bytes 589832 | tf_op jit(solution)/shard_map/ppermute | solution.py:17
  29.4 10.2 %collective-permute-start.1 = (bf16[2,128,768]{2,1,0:T(8,128)(2,1)S(1)}, bf16[2,128,768]{2,1,0:T(8,128)(2,1)S(1)}, u32[]{:S(2)}, u32[]{:S(2)}) collective-permute-start(bf16[2,128,768]{2,1,0:T(8,128)(2,1)S(1)} %bitcast_dynamic-update-slice_fusion.12), channel_id=1, source_target_pairs={{0,2},{2,0},{1,3},{3,1},{4,6},{6,4},{5,7},{7,5},{8,10},{10,8},{9,1... | collective-permute-start | bytes 1179656 | tf_op jit(solution)/shard_map/ppermute | solution.py:17
  30.4 10.0 %collective-permute-start.7 = (bf16[192,768]{1,0:T(8,128)(2,1)S(1)}, bf16[192,768]{1,0:T(8,128)(2,1)S(1)}, u32[]{:S(2)}, u32[]{:S(2)}) collective-permute-start(bf16[192,768]{1,0:T(8,128)(2,1)S(1)} %collective-permute-done.6), channel_id=1, source_target_pairs={{0,8},{8,0},{16,24},{24,16},{1,9},{9,1},{17,25},{25,17},{2,10},{10... | collective-permute-start | bytes 884744 | tf_op jit(solution)/shard_map/ppermute | solution.py:17
  31.9 14.7 %collective-permute-start.8 = (bf16[192,768]{1,0:T(8,128)(2,1)S(1)}, bf16[192,768]{1,0:T(8,128)(2,1)S(1)}, u32[]{:S(2)}, u32[]{:S(2)}) collective-permute-start(bf16[192,768]{1,0:T(8,128)(2,1)S(1)} %collective-permute-done.6), channel_id=1, source_target_pairs={{0,16},{8,24},{16,0},{24,8},{1,17},{9,25},{17,1},{25,9},{2,18},{10... | collective-permute-start | bytes 884744 | tf_op jit(solution)/shard_map/ppermute | solution.py:17
  33.5 13.2 %collective-permute-start.9 = (bf16[192,768]{1,0:T(8,128)(2,1)S(1)}, bf16[192,768]{1,0:T(8,128)(2,1)S(1)}, u32[]{:S(2)}, u32[]{:S(2)}) collective-permute-start(bf16[192,768]{1,0:T(8,128)(2,1)S(1)} %collective-permute-done.6), channel_id=1, source_target_pairs={{0,24},{8,16},{16,8},{24,0},{1,25},{9,17},{17,9},{25,1},{2,26},{10... | collective-permute-start | bytes 884744 | tf_op jit(solution)/shard_map/ppermute | solution.py:17
  39.6 7.4 %collective-permute-start.2 = (bf16[2,2,128,768]{3,2,1,0:T(8,128)(2,1)S(1)}, bf16[2,2,128,768]{3,2,1,0:T(8,128)(2,1)S(1)}, u32[]{:S(2)}, u32[]{:S(2)}) collective-permute-start(bf16[2,2,128,768]{3,2,1,0:T(8,128)(2,1)S(1)} %bitcast_dynamic-update-slice_fusion.2), channel_id=1, source_target_pairs={{0,1},{1,0},{2,3},{3,2},{4,5},{5,4},{6,7},{7,6},{8,9},{9,8},{10,11... | collective-permute-start | bytes 2359304 | tf_op jit(solution)/shard_map/ppermute | solution.py:17
  46.8 3.0 %copy-start.3 = (bf16[2,4,192,768]{3,2,1,0:T(8,128)(2,1)}, bf16[2,4,192,768]{3,2,1,0:T(8,128)(2,1)S(1)}, u32[]{:S(2)}) copy-start(bf16[2,4,192,768]{3,2,1,0:T(8,128)(2,1)S(1)} %constant_dynamic-update-slice_fusion) | copy-start | bytes 7077892
  49.8 2.7 %copy-start = (f32[1024,1536]{1,0:T(8,128)}, f32[1024,1536]{1,0:T(8,128)S(1)}, u32[]{:S(2)}) copy-start(f32[1024,1536]{1,0:T(8,128)S(1)} %get-tuple-element.6) | copy-start | bytes 18874372
  49.8 2.7 %copy-start.4 = (f32[768]{0:T(1024)S(1)}, f32[768]{0:T(1024)}, u32[]{:S(2)}) copy-start(f32[768]{0:T(1024)} %param.7) | copy-start | bytes 9220
  49.8 6.4 %copy-start.5 = (f32[1024]{0:T(1024)S(1)}, f32[1024]{0:T(1024)}, u32[]{:S(2)}) copy-start(f32[1024]{0:T(1024)} %param.6) | copy-start | bytes 12292
  52.5 3.3 %collective-permute-start.11 = (f32[1024]{0:T(1024)S(1)}, f32[1024]{0:T(1024)S(1)}, u32[]{:S(2)}, u32[]{:S(2)}) collective-permute-start(f32[1024]{0:T(1024)S(1)} %multiply_add_fusion.8), channel_id=1, source_target_pairs={{0,1},{1,0},{2,3},{3,2},{4,5},{5,4},{6,7},{7,6},{8,9},{9,8},{10,11... | collective-permute-start | bytes 12296 | tf_op jit(solution)/shard_map/ppermute | solution.py:17
  52.5 4.9 %collective-permute-start.10 = (f32[768]{0:T(1024)S(1)}, f32[768]{0:T(1024)S(1)}, u32[]{:S(2)}, u32[]{:S(2)}) collective-permute-start(f32[768]{0:T(1024)S(1)} %copy-done.4), channel_id=1, source_target_pairs={{0,4},{4,0},{1,5},{5,1},{2,6},{6,2},{3,7},{7,3},{8,12},{12,8},{9,1... | collective-permute-start | bytes 9224 | tf_op jit(solution)/shard_map/ppermute | solution.py:17
  55.8 3.7 %collective-permute-start.12 = (f32[1024]{0:T(1024)S(1)}, f32[1024]{0:T(1024)S(1)}, u32[]{:S(2)}, u32[]{:S(2)}) collective-permute-start(f32[1024]{0:T(1024)S(1)} %multiply_add_fusion.7), channel_id=1, source_target_pairs={{0,2},{2,0},{1,3},{3,1},{4,6},{6,4},{5,7},{7,5},{8,10},{10,8},{9,1... | collective-permute-start | bytes 12296 | tf_op jit(solution)/shard_map/ppermute | solution.py:17
  59.5 4.6 %copy-start.1 = (f32[1024,1536]{1,0:T(8,128)S(1)}, f32[1024,1536]{1,0:T(8,128)}, u32[]{:S(2)}) copy-start(f32[1024,1536]{1,0:T(8,128)} %copy-done) | copy-start | bytes 18874372
  65.5 4.6 %collective-permute-start.15 = (f32[1536]{0:T(1024)S(1)}, f32[1536]{0:T(1024)S(1)}, u32[]{:S(2)}, u32[]{:S(2)}) collective-permute-start(f32[1536]{0:T(1024)S(1)} %multiply_add_fusion.2), channel_id=1, source_target_pairs={{0,24},{8,16},{16,8},{24,0},{1,25},{9,17},{17,9},{25,1},{2,26},{10... | collective-permute-start | bytes 18440 | tf_op jit(solution)/shard_map/ppermute | solution.py:17
  67.0 3.7 %collective-permute-start.14 = (f32[1536]{0:T(1024)S(1)}, f32[1536]{0:T(1024)S(1)}, u32[]{:S(2)}, u32[]{:S(2)}) collective-permute-start(f32[1536]{0:T(1024)S(1)} %multiply_add_fusion.2), channel_id=1, source_target_pairs={{0,16},{8,24},{16,0},{24,8},{1,17},{9,25},{17,1},{25,9},{2,18},{10... | collective-permute-start | bytes 18440 | tf_op jit(solution)/shard_map/ppermute | solution.py:17
  68.2 3.7 %collective-permute-start.13 = (f32[1536]{0:T(1024)S(1)}, f32[1536]{0:T(1024)S(1)}, u32[]{:S(2)}, u32[]{:S(2)}) collective-permute-start(f32[1536]{0:T(1024)S(1)} %multiply_add_fusion.2), channel_id=1, source_target_pairs={{0,8},{8,0},{16,24},{24,16},{1,9},{9,1},{17,25},{25,17},{2,10},{10... | collective-permute-start | bytes 18440 | tf_op jit(solution)/shard_map/ppermute | solution.py:17
  71.9 4.6 %copy-start.2 = (f32[1024,1536]{1,0:T(8,128)S(1)}, f32[1024,1536]{1,0:T(8,128)}, u32[]{:S(2)}) copy-start(f32[1024,1536]{1,0:T(8,128)} %copy-done) | copy-start | bytes 18874372
  77.8 1.2 collective-permute-start.16
  79.1 3.7 %collective-permute-start.17 = (f32[1024]{0:T(1024)S(1)}, f32[1024]{0:T(1024)S(1)}, u32[]{:S(2)}, u32[]{:S(2)}) collective-permute-start(f32[1024]{0:T(1024)S(1)} %multiply_add_fusion.5), channel_id=1, source_target_pairs={{0,2},{2,0},{1,3},{3,1},{4,6},{6,4},{5,7},{7,5},{8,10},{10,8},{9,1... | collective-permute-start | bytes 12296 | tf_op jit(solution)/shard_map/ppermute | solution.py:17
  84.6 4.6 %collective-permute-start.20 = (f32[1536]{0:T(1024)S(1)}, f32[1536]{0:T(1024)S(1)}, u32[]{:S(2)}, u32[]{:S(2)}) collective-permute-start(f32[1536]{0:T(1024)S(1)} %multiply_add_fusion.1), channel_id=1, source_target_pairs={{0,24},{8,16},{16,8},{24,0},{1,25},{9,17},{17,9},{25,1},{2,26},{10... | collective-permute-start | bytes 18440 | tf_op jit(solution)/shard_map/ppermute | solution.py:17
  86.5 3.7 %collective-permute-start.19 = (f32[1536]{0:T(1024)S(1)}, f32[1536]{0:T(1024)S(1)}, u32[]{:S(2)}, u32[]{:S(2)}) collective-permute-start(f32[1536]{0:T(1024)S(1)} %multiply_add_fusion.1), channel_id=1, source_target_pairs={{0,16},{8,24},{16,0},{24,8},{1,17},{9,25},{17,1},{25,9},{2,18},{10... | collective-permute-start | bytes 18440 | tf_op jit(solution)/shard_map/ppermute | solution.py:17
  87.0 3.7 %collective-permute-start.18 = (f32[1536]{0:T(1024)S(1)}, f32[1536]{0:T(1024)S(1)}, u32[]{:S(2)}, u32[]{:S(2)}) collective-permute-start(f32[1536]{0:T(1024)S(1)} %multiply_add_fusion.1), channel_id=1, source_target_pairs={{0,8},{8,0},{16,24},{24,16},{1,9},{9,1},{17,25},{25,17},{2,10},{10... | collective-permute-start | bytes 18440 | tf_op jit(solution)/shard_map/ppermute | solution.py:17
  92.5 1.2 collective-permute-start.21
  93.7 3.7 %collective-permute-start.22 = (f32[1024]{0:T(1024)S(1)}, f32[1024]{0:T(1024)S(1)}, u32[]{:S(2)}, u32[]{:S(2)}) collective-permute-start(f32[1024]{0:T(1024)S(1)} %multiply_add_fusion.3), channel_id=1, source_target_pairs={{0,2},{2,0},{1,3},{3,1},{4,6},{6,4},{5,7},{7,5},{8,10},{10,8},{9,1... | collective-permute-start | bytes 12296 | tf_op jit(solution)/shard_map/ppermute | solution.py:17
  99.3 4.6 %collective-permute-start.25 = (f32[1536]{0:T(1024)S(1)}, f32[1536]{0:T(1024)S(1)}, u32[]{:S(2)}, u32[]{:S(2)}) collective-permute-start(f32[1536]{0:T(1024)S(1)} %multiply_add_fusion), channel_id=1, source_target_pairs={{0,24},{8,16},{16,8},{24,0},{1,25},{9,17},{17,9},{25,1},{2,26},{10... | collective-permute-start | bytes 18440 | tf_op jit(solution)/shard_map/ppermute | solution.py:17
  100.8 3.7 %collective-permute-start.24 = (f32[1536]{0:T(1024)S(1)}, f32[1536]{0:T(1024)S(1)}, u32[]{:S(2)}, u32[]{:S(2)}) collective-permute-start(f32[1536]{0:T(1024)S(1)} %multiply_add_fusion), channel_id=1, source_target_pairs={{0,16},{8,24},{16,0},{24,8},{1,17},{9,25},{17,1},{25,9},{2,18},{10... | collective-permute-start | bytes 18440 | tf_op jit(solution)/shard_map/ppermute | solution.py:17
  102.0 3.7 %collective-permute-start.23 = (f32[1536]{0:T(1024)S(1)}, f32[1536]{0:T(1024)S(1)}, u32[]{:S(2)}, u32[]{:S(2)}) collective-permute-start(f32[1536]{0:T(1024)S(1)} %multiply_add_fusion), channel_id=1, source_target_pairs={{0,8},{8,0},{16,24},{24,16},{1,9},{9,1},{17,25},{25,17},{2,10},{10... | collective-permute-start | bytes 18440 | tf_op jit(solution)/shard_map/ppermute | solution.py:17
  105.7 10.2 %slice-start = ((s8[6291456]{0:T(1024)(128)(4,1)}), s8[2097152]{0:T(1024)(128)(4,1)S(1)}, s32[]{:S(2)}) async-start(s8[6291456]{0:T(1024)(128)(4,1)} %bitcast.90), calls=%async_computation | async-start | bytes 4194304
  106.0 1.2 collective-permute-start.26
  107.2 3.6 %collective-permute-start.27 = (f32[512]{0:T(512)S(1)}, f32[512]{0:T(512)S(1)}, u32[]{:S(2)}, u32[]{:S(2)}) collective-permute-start(f32[512]{0:T(512)S(1)} %max.66), channel_id=1, source_target_pairs={{0,2},{2,0},{1,3},{3,1},{4,6},{6,4},{5,7},{7,5},{8,10},{10,8},{9,1... | collective-permute-start | bytes 6152 | tf_op jit(solution)/shard_map/ppermute | solution.py:17
  110.8 5.1 %slice-start.1 = ((s8[6291456]{0:T(1024)(128)(4,1)}), s8[4194304]{0:T(1024)(128)(4,1)S(1)}, s32[]{:S(2)}) async-start(s8[6291456]{0:T(1024)(128)(4,1)} %bitcast.90), calls=%async_computation.1 | async-start | bytes 8388608
  115.2 2.4 %collective-permute-start.28 = (f32[2,128,768]{2,1,0:T(8,128)S(1)}, f32[2,128,768]{2,1,0:T(8,128)S(1)}, u32[]{:S(2)}, u32[]{:S(2)}) collective-permute-start(f32[2,128,768]{2,1,0:T(8,128)S(1)} %dynamic-slice_bitcast_fusion), channel_id=1, source_target_pairs={{0,1},{1,0},{2,3},{3,2},{4,5},{5,4},{6,7},{7,6},{8,9},{9,8},{10,11... | collective-permute-start | bytes 2359304 | tf_op jit(solution)/shard_map/ppermute | solution.py:17
  116.6 1.4 %collective-permute-start.30 = (f32[2,128]{1,0:T(2,128)S(1)}, f32[2,128]{1,0:T(2,128)S(1)}, u32[]{:S(2)}, u32[]{:S(2)}) collective-permute-start(f32[2,128]{1,0:T(2,128)S(1)} %fusion.28), channel_id=1, source_target_pairs={{0,1},{1,0},{2,3},{3,2},{4,5},{5,4},{6,7},{7,6},{8,9},{9,8},{10,11... | collective-permute-start | bytes 3080 | tf_op jit(solution)/shard_map/ppermute | solution.py:17
  117.7 11.3 %collective-permute-start.29 = (f32[128,768]{1,0:T(8,128)S(1)}, f32[128,768]{1,0:T(8,128)S(1)}, u32[]{:S(2)}, u32[]{:S(2)}) collective-permute-start(f32[128,768]{1,0:T(8,128)S(1)} %dynamic-slice_bitcast_fusion.1), channel_id=1, source_target_pairs={{0,2},{2,0},{1,3},{3,1},{4,6},{6,4},{5,7},{7,5},{8,10},{10,8},{9,1... | collective-permute-start | bytes 1179656 | tf_op jit(solution)/shard_map/ppermute | solution.py:17
  118.1 10.9 %collective-permute-start.31 = (f32[128]{0:T(128)S(1)}, f32[128]{0:T(128)S(1)}, u32[]{:S(2)}, u32[]{:S(2)}) collective-permute-start(f32[128]{0:T(128)S(1)} %fusion.31), channel_id=1, source_target_pairs={{0,2},{2,0},{1,3},{3,1},{4,6},{6,4},{5,7},{7,5},{8,10},{10,8},{9,1... | collective-permute-start | bytes 1544 | tf_op jit(solution)/shard_map/ppermute | solution.py:17

commit v3 on v2

--- a/solution.py
+++ b/solution.py
@@ -52,35 +52,57 @@
     return lax.dot_general(a, b, (((1,), (1,)), ((), ())), preferred_element_type=jnp.float32)
 
 
+def pairs(x, axes):
+    return [x, swap(x, axes, 1)]
+
+
+def by_place(pair, index):
+    first = index == 0
+    return jnp.stack([jnp.where(first, pair[0], pair[1]), jnp.where(first, pair[1], pair[0])])
+
+
 def local(queries, tools, query_mass, tool_mass):
     rows = lax.axis_size("row")
-    nh, nl = lax.axis_size("zh"), lax.axis_size("zl")
+    nl = lax.axis_size("zl")
     ri, hi, li, core = (lax.axis_index(a) for a in ("row", "zh", "zl", "core"))
     bq, features = queries.shape
     bt = tools.shape[0]
     scaling = LOG2E / (math.sqrt(features) * EPSILON)
 
-    tile_tools = place([place(swaps(t, "row"), ri) for t in swaps(tools, "zh")], hi).reshape(-1, features)
-    log_tool = jnp.log2(place(swaps(tool_mass, "zh"), hi)).reshape(-1)
-    tile_queries = place(swaps(place(swaps(queries, "zh"), hi), "zl"), li)
-    tile_queries = place(swaps(tile_queries, "core"), core).reshape(-1, features)
-    log_query = jnp.log2(query_mass).reshape(nh, nl, 2, bq).transpose(2, 1, 0, 3).reshape(-1)
+    other_tools = swap(tools, "zh", 1)
+    own = swaps(tools, "row")
+    held, held_mass, own[1] = lax.optimization_barrier((queries, tool_mass, own[1]))
+    tile_tools = [place(t, ri).reshape(-1, features) for t in (own, swaps(other_tools, "row"))]
+    far = swap(held, "zh", 1)
+    near_queries = place(swaps(queries, "zl"), li)
+    far_queries = place(swaps(far, "zl"), li)
+    tile_queries = jnp.stack([near_queries, far_queries])
+    tile_queries = jnp.moveaxis(place(pairs(tile_queries, "core"), core), 0, 1).reshape(-1, features)
+    log_tools = [jnp.log2(t) for t in (tool_mass, swap(held_mass, "zh", 1))]
+    tile_queries, log_tools = lax.optimization_barrier((tile_queries, log_tools))
+    log_query = jnp.log2(query_mass).reshape(2, nl, 2, bq).transpose(0, 2, 1, 3)
+    log_query = by_place([log_query[0], log_query[1]], hi).reshape(-1)
 
-    tile = dot_t(tile_queries, tile_tools) * scaling
-    tool_side = jnp.zeros((tile.shape[1],), jnp.float32)
+    tiles = [dot_t(tile_queries, t) * scaling for t in tile_tools]
+    tool_sides = [jnp.zeros((t.shape[1],), jnp.float32) for t in tiles]
     for sweep in range(ITERS):
-        part = lse_of(swaps(local_lse(tile + tool_side[None, :], 1), "core"))
+        part = lse_of([local_lse(t + s[None, :], 1) for t, s in zip(tiles, tool_sides)])
+        part = lse_of(swaps(part, "core"))
         query_side = log_query - lse_of(swaps(part, "zl"))
-        part = local_lse(tile + query_side[:, None], 0)
-        tool_side = log_tool - lse_of(swaps(part, "row"))
+        part = jnp.concatenate([local_lse(t + query_side[:, None], 0) for t in tiles])
+        got = lse_of(swaps(part, "row"))
+        tool_sides = [m - g for m, g in zip(log_tools, jnp.split(got, 2))]
 
-    scores = pick(tile.reshape(2, nl, nh, bq, -1), hi, 2).reshape(2 * nl * bq, -1) + tool_side[None, :]
-    peak = jnp.max(scores, axis=1)
+    half = 2 * nl * bq
+    scores = [t[:half] + s[None, :] for t, s in zip(tiles, tool_sides)]
+    peak = jnp.maximum(jnp.max(scores[0], axis=1), jnp.max(scores[1], axis=1))
     peak = functools.reduce(jnp.maximum, swaps(peak, "core"))
     peak = functools.reduce(jnp.maximum, swaps(peak, "zl"))
-    exps = jnp.exp2(scores - peak[:, None])
-    total = jnp.sum(exps, axis=1).reshape(2, nl, bq)
-    summed = jnp.dot(exps.astype(jnp.bfloat16), tile_tools, preferred_element_type=jnp.float32)
+    exps = [jnp.exp2(s - peak[:, None]) for s in scores]
+    total = sum(jnp.sum(e, axis=1) for e in exps).reshape(2, nl, bq)
+    summed = sum(
+        jnp.dot(e.astype(jnp.bfloat16), t, preferred_element_type=jnp.float32) for e, t in zip(exps, tile_tools)
+    )
     summed = summed.reshape(2, nl, bq, features)
     summed, total = (pick(x, core, 0) + swap(pick(x, 1 - core, 0), "core", 1) for x in (summed, total))
     summed, total = (
@@ -89,9 +111,9 @@
     mapped = (summed / total[:, None]).astype(jnp.bfloat16)
 
     unit = EPSILON / LOG2E
-    query_potential = unit * query_side.reshape(2, nl, nh, bq).transpose(2, 1, 0, 3).reshape(-1)
-    tool_potential = unit * pick(tool_side.reshape(nh, -1), hi, 0)
-    return (mapped, query_potential, tool_potential)
+    query_potential = query_side.reshape(2, 2, nl, bq).transpose(0, 2, 1, 3)
+    query_potential = unit * by_place([query_potential[0], query_potential[1]], hi).reshape(-1)
+    return (mapped, query_potential, unit * tool_sides[0])
 
 
 def solution(mesh):

time: 130 us -> 114 us (0.88)
  waiting for transfers between devices: 64.3 us -> 47.6 us
  starting transfers between devices: 30.6 us -> 37.4 us
  local copies, waits for them, and re-layouts: 7.87 us -> 4 us
  other arithmetic: 18.9 us -> 16.1 us
    ppermute x32 -> x33, waiting for transfers between devices: 64.3 us -> 47.6 us  [swap(): return lax.ppermute(x, axes, [(i, i ^ k) for i in range(n)])]
    ppermute x32 -> x33, starting transfers between devices: 30.6 us -> 37.4 us  [swap(): return lax.ppermute(x, axes, [(i, i ^ k) for i in range(n)])]
    reduce_max x5 -> x7, other arithmetic: 8.34 us -> 1.96 us  [local_lse(): highest = jnp.max(scores, axis=axis, keepdims=True)]
    unnamed x16 -> x12, local copies, waits for them, and re-layouts: 3.83 us -> 0.74 us
    reduce_sum x6 -> x11, other arithmetic: 7.77 us -> 9.65 us  [local_lse(): total = jnp.sum(jnp.exp2(scores - highest), axis=axis)]
    another operation x2 -> x5, other arithmetic: 0.01 us -> 1.47 us  [the longest x2 0.7 us: local(): log_tools = [jnp.log2(t) for t in (tool_mass, swap(held_mass, 'zh', 1))]]
    dot_general x1 -> x2, matrix products: 4.33 us -> 3.71 us  [local(): jnp.dot(e.astype(jnp.bfloat16), t, preferred_element_type=jnp.float32)]
    dynamic_update_slice x18 -> x13, local copies, waits for them, and re-layouts: 2.79 us -> 2.23 us  [place(): whole = lax.dynamic_update_index_in_dim(whole, block, index ^ k, 0)]
  transfers between devices with their start and end apart: 32 -> 33, of which waited for: 23 -> 24; matrix products, arithmetic and copies ran while one was open for 4% -> 5% of each run, Pallas kernels for 0% -> 0%
where the time goes in v3:
time: 114 us; the launch traced here: 113 us
  waiting for transfers between devices  47.6 us (42%)
  starting transfers between devices  37.4 us (33%)
  other arithmetic  16.1 us (14%)
  matrix products  6.56 us (6%)
  local copies, waits for them, and re-layouts  4 us (4%)
  between operations  1.26 us (1%)
    ppermute x33, waiting for transfers between devices, swap(): return lax.ppermute(x, axes, [(i, i ^ k) for i in range(n)])  47.6 us
    ppermute x33, starting transfers between devices, swap(): return lax.ppermute(x, axes, [(i, i ^ k) for i in range(n)])  37.4 us
    reduce_sum x11, other arithmetic, local_lse(): total = jnp.sum(jnp.exp2(scores - highest), axis=axis)  9.65 us
    dot_general x2, matrix products, local(): jnp.dot(e.astype(jnp.bfloat16), t, preferred_element_type=jnp.float32)  3.71 us
    dot_general x2, matrix products, dot_t(): lax.dot_general(a, b, (((1,), (1,)), ((), ())), preferred_element_type=jn...  2.84 us
  transfers between devices with their start and end apart: 33, of which 24 were waited for; matrix products, arithmetic and copies ran while one was open for 5% of the time, Pallas kernels for 0%

profile of v3, /device:TPU:0, one launch (start us, length us, event | category | flops | bytes accessed | tf_op | source)
XLA Modules:
  0.0 112.9 jit_solution(3946275049524651079)
XLA Ops:
  0.6 3.0 %collective-permute-start.1 = (bf16[192,768]{1,0:T(8,128)(2,1)}, bf16[192,768]{1,0:T(8,128)(2,1)S(1)}, u32[]{:S(2)}, u32[]{:S(2)}) collective-permute-start(bf16[192,768]{1,0:T(8,128)(2,1)} %param.5), channel_id=1, source_target_pairs={{0,8},{8,0},{16,24},{24,16},{1,9},{9,1},{17,25},{25,17},{2,10},{10... | collective-permute-start | bytes 884744 | tf_op jit(solution)/shard_map/ppermute | solution.py:17
  3.6 2.6 %collective-permute-start.8 = (bf16[192,768]{1,0:T(8,128)(2,1)}, bf16[192,768]{1,0:T(8,128)(2,1)S(1)}, u32[]{:S(2)}, u32[]{:S(2)}) collective-permute-start(bf16[192,768]{1,0:T(8,128)(2,1)} %param.5), channel_id=1, source_target_pairs={{0,4},{4,0},{1,5},{5,1},{2,6},{6,2},{3,7},{7,3},{8,12},{12,8},{9,1... | collective-permute-start | bytes 884744 | tf_op jit(solution)/shard_map/ppermute | solution.py:17
  6.2 1.5 %collective-permute-start.6 = (bf16[192,768]{1,0:T(8,128)(2,1)}, bf16[192,768]{1,0:T(8,128)(2,1)S(1)}, u32[]{:S(2)}, u32[]{:S(2)}) collective-permute-start(bf16[192,768]{1,0:T(8,128)(2,1)} %param.5), channel_id=1, source_target_pairs={{0,16},{8,24},{16,0},{24,8},{1,17},{9,25},{17,1},{25,9},{2,18},{10... | collective-permute-start | bytes 884744 | tf_op jit(solution)/shard_map/ppermute | solution.py:17
  8.2 1.6 %collective-permute-start = (bf16[128,768]{1,0:T(8,128)(2,1)}, bf16[128,768]{1,0:T(8,128)(2,1)S(1)}, u32[]{:S(2)}, u32[]{:S(2)}) collective-permute-start(bf16[128,768]{1,0:T(8,128)(2,1)} %param.4), channel_id=1, source_target_pairs={{0,2},{2,0},{1,3},{3,1},{4,6},{6,4},{5,7},{7,5},{8,10},{10,8},{9,1... | collective-permute-start | bytes 589832 | tf_op jit(solution)/shard_map/ppermute | solution.py:17
  10.5 0.9 bitcast_dynamic-update-slice_fusion.13
  11.6 1.0 bitcast_dynamic-update-slice_fusion.9
  13.2 3.5 %collective-permute-done = bf16[128,768]{1,0:T(8,128)(2,1)S(1)} collective-permute-done((bf16[128,768]{1,0:T(8,128)(2,1)}, bf16[128,768]{1,0:T(8,128)(2,1)S(1)}, u32[]{:S(2)}, u32[]{:S(2)}) %collective-permute-start) | collective-permute-done | bytes 196640 | tf_op jit(solution)/shard_map/ppermute | solution.py:17
  16.8 2.3 %collective-permute-start.2 = (bf16[128,768]{1,0:T(8,128)(2,1)}, bf16[128,768]{1,0:T(8,128)(2,1)S(1)}, u32[]{:S(2)}, u32[]{:S(2)}) collective-permute-start(bf16[128,768]{1,0:T(8,128)(2,1)} %param.4), channel_id=1, source_target_pairs={{0,4},{4,0},{1,5},{5,1},{2,6},{6,2},{3,7},{7,3},{8,12},{12,8},{9,1... | collective-permute-start | bytes 589832 | tf_op jit(solution)/shard_map/ppermute | solution.py:17
  19.8 5.6 %collective-permute-start.9 = (bf16[192,768]{1,0:T(8,128)(2,1)S(1)}, bf16[192,768]{1,0:T(8,128)(2,1)S(1)}, u32[]{:S(2)}, u32[]{:S(2)}) collective-permute-start(bf16[192,768]{1,0:T(8,128)(2,1)S(1)} %collective-permute-done.8), channel_id=1, source_target_pairs={{0,8},{8,0},{16,24},{24,16},{1,9},{9,1},{17,25},{25,17},{2,10},{10... | collective-permute-start | bytes 884744 | tf_op jit(solution)/shard_map/ppermute | solution.py:17
  25.6 1.6 %collective-permute-start.10 = (bf16[192,768]{1,0:T(8,128)(2,1)S(1)}, bf16[192,768]{1,0:T(8,128)(2,1)S(1)}, u32[]{:S(2)}, u32[]{:S(2)}) collective-permute-start(bf16[192,768]{1,0:T(8,128)(2,1)S(1)} %collective-permute-done.8), channel_id=1, source_target_pairs={{0,16},{8,24},{16,0},{24,8},{1,17},{9,25},{17,1},{25,9},{2,18},{10... | collective-permute-start | bytes 884744 | tf_op jit(solution)/shard_map/ppermute | solution.py:17
  27.3 0.8 collective-permute-done.5
  28.9 5.0 %collective-permute-done.3 = bf16[128,768]{1,0:T(8,128)(2,1)S(1)} collective-permute-done((bf16[128,768]{1,0:T(8,128)(2,1)S(1)}, bf16[128,768]{1,0:T(8,128)(2,1)S(1)}, u32[]{:S(2)}, u32[]{:S(2)}) %collective-permute-start.3) | collective-permute-done | bytes 196640 | tf_op jit(solution)/shard_map/ppermute | solution.py:17
  34.1 1.4 %collective-permute-done.10 = bf16[192,768]{1,0:T(8,128)(2,1)S(1)} collective-permute-done((bf16[192,768]{1,0:T(8,128)(2,1)S(1)}, bf16[192,768]{1,0:T(8,128)(2,1)S(1)}, u32[]{:S(2)}, u32[]{:S(2)}) %collective-permute-start.10) | collective-permute-done | bytes 294944 | tf_op jit(solution)/shard_map/ppermute | solution.py:17
  36.4 1.4 %fusion.43 = (f32[1024]{0:T(1024)S(1)}, f32[1024,768]{0,1:T(8,128)S(1)}) fusion(bf16[1024,768]{1,0:T(8,128)(2,1)S(1)} %bitcast.77, bf16[768,768]{1,0:T(8,128)(2,1)S(1)} %bitcast.79), kind=kOutput, calls=%fused_computation.139 | convolution fusion | flops 1209531392 | bytes 5902336 | tf_op jit(solution)/shard_map/dot_general | solution.py:52
  37.9 1.4 %fusion.44 = (f32[1024]{0:T(1024)S(1)}, f32[1024,768]{0,1:T(8,128)S(1)}) fusion(bf16[1024,768]{1,0:T(8,128)(2,1)S(1)} %bitcast.78, bf16[768,768]{1,0:T(8,128)(2,1)S(1)} %bitcast.82), kind=kOutput, calls=%fused_computation.140 | convolution fusion | flops 1209531392 | bytes 5902336 | tf_op jit(solution)/shard_map/dot_general | solution.py:52
  39.3 1.0 exponential_reduce_fusion.10
  40.6 1.0 collective-permute-done.12
  41.6 1.8 %collective-permute-start.13 = (f32[1024]{0:T(1024)S(1)}, f32[1024]{0:T(1024)S(1)}, u32[]{:S(2)}, u32[]{:S(2)}) collective-permute-start(f32[1024]{0:T(1024)S(1)} %multiply_add_fusion.13), channel_id=1, source_target_pairs={{0,2},{2,0},{1,3},{3,1},{4,6},{6,4},{5,7},{7,5},{8,10},{10,8},{9,1... | collective-permute-start | bytes 12296 | tf_op jit(solution)/shard_map/ppermute | solution.py:17
  43.5 1.9 %collective-permute-done.13 = f32[1024]{0:T(1024)S(1)} collective-permute-done((f32[1024]{0:T(1024)S(1)}, f32[1024]{0:T(1024)S(1)}, u32[]{:S(2)}, u32[]{:S(2)}) %collective-permute-start.13) | collective-permute-done | bytes 4128 | tf_op jit(solution)/shard_map/ppermute | solution.py:17
  45.6 1.1 exponential_reduce_fusion.9
  46.7 0.9 exponential_reduce_fusion.8
  47.6 2.5 %collective-permute-start.14 = (f32[1536]{0:T(1024)S(1)}, f32[1536]{0:T(1024)S(1)}, u32[]{:S(2)}, u32[]{:S(2)}) collective-permute-start(f32[1536]{0:T(1024)S(1)} %pad_maximum_fusion.1), channel_id=1, source_target_pairs={{0,8},{8,0},{16,24},{24,16},{1,9},{9,1},{17,25},{25,17},{2,10},{10... | collective-permute-start | bytes 18440 | tf_op jit(solution)/shard_map/ppermute | solution.py:17
  50.2 1.5 %collective-permute-start.15 = (f32[1536]{0:T(1024)S(1)}, f32[1536]{0:T(1024)S(1)}, u32[]{:S(2)}, u32[]{:S(2)}) collective-permute-start(f32[1536]{0:T(1024)S(1)} %pad_maximum_fusion.1), channel_id=1, source_target_pairs={{0,16},{8,24},{16,0},{24,8},{1,17},{9,25},{17,1},{25,9},{2,18},{10... | collective-permute-start | bytes 18440 | tf_op jit(solution)/shard_map/ppermute | solution.py:17
  51.8 2.0 %collective-permute-done.15 = f32[1536]{0:T(1024)S(1)} collective-permute-done((f32[1536]{0:T(1024)S(1)}, f32[1536]{0:T(1024)S(1)}, u32[]{:S(2)}, u32[]{:S(2)}) %collective-permute-start.15) | collective-permute-done | bytes 6176 | tf_op jit(solution)/shard_map/ppermute | solution.py:17
  53.8 2.4 %collective-permute-done.16 = f32[1536]{0:T(1024)S(1)} collective-permute-done((f32[1536]{0:T(1024)S(1)}, f32[1536]{0:T(1024)S(1)}, u32[]{:S(2)}, u32[]{:S(2)}) %collective-permute-start.16) | collective-permute-done | bytes 6176 | tf_op jit(solution)/shard_map/ppermute | solution.py:17
  58.3 1.2 %collective-permute-done.17 = f32[1024]{0:T(1024)S(1)} collective-permute-done((f32[1024]{0:T(1024)S(1)}, f32[1024]{0:T(1024)S(1)}, u32[]{:S(2)}, u32[]{:S(2)}) %collective-permute-start.17) | collective-permute-done | bytes 4128 | tf_op jit(solution)/shard_map/ppermute | solution.py:17
  59.6 3.6 %collective-permute-done.18 = f32[1024]{0:T(1024)S(1)} collective-permute-done((f32[1024]{0:T(1024)S(1)}, f32[1024]{0:T(1024)S(1)}, u32[]{:S(2)}, u32[]{:S(2)}) %collective-permute-start.18) | collective-permute-done | bytes 4128 | tf_op jit(solution)/shard_map/ppermute | solution.py:17
  63.5 1.1 exponential_reduce_fusion.5
  64.6 0.9 exponential_reduce_fusion.4
  66.3 2.9 %collective-permute-start.21 = (f32[1536]{0:T(1024)S(1)}, f32[1536]{0:T(1024)S(1)}, u32[]{:S(2)}, u32[]{:S(2)}) collective-permute-start(f32[1536]{0:T(1024)S(1)} %pad_maximum_fusion.2), channel_id=1, source_target_pairs={{0,24},{8,16},{16,8},{24,0},{1,25},{9,17},{17,9},{25,1},{2,26},{10... | collective-permute-start | bytes 18440 | tf_op jit(solution)/shard_map/ppermute | solution.py:17
  69.5 1.4 %collective-permute-done.21 = f32[1536]{0:T(1024)S(1)} collective-permute-done((f32[1536]{0:T(1024)S(1)}, f32[1536]{0:T(1024)S(1)}, u32[]{:S(2)}, u32[]{:S(2)}) %collective-permute-start.21) | collective-permute-done | bytes 6176 | tf_op jit(solution)/shard_map/ppermute | solution.py:17
  73.0 1.2 %collective-permute-done.22 = f32[1024]{0:T(1024)S(1)} collective-permute-done((f32[1024]{0:T(1024)S(1)}, f32[1024]{0:T(1024)S(1)}, u32[]{:S(2)}, u32[]{:S(2)}) %collective-permute-start.22) | collective-permute-done | bytes 4128 | tf_op jit(solution)/shard_map/ppermute | solution.py:17
  74.1 1.3 %collective-permute-start.23 = (f32[1024]{0:T(1024)S(1)}, f32[1024]{0:T(1024)S(1)}, u32[]{:S(2)}, u32[]{:S(2)}) collective-permute-start(f32[1024]{0:T(1024)S(1)} %multiply_add_fusion.5), channel_id=1, source_target_pairs={{0,2},{2,0},{1,3},{3,1},{4,6},{6,4},{5,7},{7,5},{8,10},{10,8},{9,1... | collective-permute-start | bytes 12296 | tf_op jit(solution)/shard_map/ppermute | solution.py:17
  75.4 2.4 %collective-permute-done.23 = f32[1024]{0:T(1024)S(1)} collective-permute-done((f32[1024]{0:T(1024)S(1)}, f32[1024]{0:T(1024)S(1)}, u32[]{:S(2)}, u32[]{:S(2)}) %collective-permute-start.23) | collective-permute-done | bytes 4128 | tf_op jit(solution)/shard_map/ppermute | solution.py:17
  78.1 1.1 exponential_reduce_fusion.1
  79.2 0.9 exponential_reduce_fusion
  80.1 2.0 %collective-permute-start.24 = (f32[1536]{0:T(1024)S(1)}, f32[1536]{0:T(1024)S(1)}, u32[]{:S(2)}, u32[]{:S(2)}) collective-permute-start(f32[1536]{0:T(1024)S(1)} %pad_maximum_fusion.3), channel_id=1, source_target_pairs={{0,8},{8,0},{16,24},{24,16},{1,9},{9,1},{17,25},{25,17},{2,10},{10... | collective-permute-start | bytes 18440 | tf_op jit(solution)/shard_map/ppermute | solution.py:17
  82.1 1.5 %collective-permute-start.25 = (f32[1536]{0:T(1024)S(1)}, f32[1536]{0:T(1024)S(1)}, u32[]{:S(2)}, u32[]{:S(2)}) collective-permute-start(f32[1536]{0:T(1024)S(1)} %pad_maximum_fusion.3), channel_id=1, source_target_pairs={{0,16},{8,24},{16,0},{24,8},{1,17},{9,25},{17,1},{25,9},{2,18},{10... | collective-permute-start | bytes 18440 | tf_op jit(solution)/shard_map/ppermute | solution.py:17
  83.8 1.9 %collective-permute-done.25 = f32[1536]{0:T(1024)S(1)} collective-permute-done((f32[1536]{0:T(1024)S(1)}, f32[1536]{0:T(1024)S(1)}, u32[]{:S(2)}, u32[]{:S(2)}) %collective-permute-start.25) | collective-permute-done | bytes 6176 | tf_op jit(solution)/shard_map/ppermute | solution.py:17
  85.8 2.4 %collective-permute-done.26 = f32[1536]{0:T(1024)S(1)} collective-permute-done((f32[1536]{0:T(1024)S(1)}, f32[1536]{0:T(1024)S(1)}, u32[]{:S(2)}, u32[]{:S(2)}) %collective-permute-start.26) | collective-permute-done | bytes 6176 | tf_op jit(solution)/shard_map/ppermute | solution.py:17
  89.3 1.1 %collective-permute-done.27 = f32[512]{0:T(512)S(1)} collective-permute-done((f32[512]{0:T(512)S(1)}, f32[512]{0:T(512)S(1)}, u32[]{:S(2)}, u32[]{:S(2)}) %collective-permute-start.27) | collective-permute-done | bytes 2080 | tf_op jit(solution)/shard_map/ppermute | solution.py:17
  90.5 3.6 %collective-permute-done.28 = f32[512]{0:T(512)S(1)} collective-permute-done((f32[512]{0:T(512)S(1)}, f32[512]{0:T(512)S(1)}, u32[]{:S(2)}, u32[]{:S(2)}) %collective-permute-start.28) | collective-permute-done | bytes 2080 | tf_op jit(solution)/shard_map/ppermute | solution.py:17
  94.1 2.7 %fusion.7 = f32[512,768]{1,0:T(8,128)S(1)} fusion(bf16[768,768]{1,0:T(8,128)(2,1)} %bitcast.81, f32[1024,768]{0,1:T(8,128)} %copy-done, f32[512]{0:T(512)S(1)} %max.83, f32[768]{0:T(1024)S(1)} %get-tuple-element.24), kind=kOutput, calls=%fused_computation.35 | convolution fusion | flops 605552640 | bytes 4330496 | tf_op jit(solution)/shard_map/dot_general | solution.py:104
  96.8 1.0 convolution_add_fusion
  99.5 1.1 collective-permute-done.31
  100.8 2.0 %collective-permute-start.32 = (f32[128]{0:T(128)S(1)}, f32[128]{0:T(128)S(1)}, u32[]{:S(2)}, u32[]{:S(2)}) collective-permute-start(f32[128]{0:T(128)S(1)} %fusion.40), channel_id=1, source_target_pairs={{0,2},{2,0},{1,3},{3,1},{4,6},{6,4},{5,7},{7,5},{8,10},{10,8},{9,1... | collective-permute-start | bytes 1544 | tf_op jit(solution)/shard_map/ppermute | solution.py:17
  103.4 8.6 %collective-permute-done.32 = f32[128]{0:T(128)S(1)} collective-permute-done((f32[128]{0:T(128)S(1)}, f32[128]{0:T(128)S(1)}, u32[]{:S(2)}, u32[]{:S(2)}) %collective-permute-start.32) | collective-permute-done | bytes 544 | tf_op jit(solution)/shard_map/ppermute | solution.py:17
  112.1 0.8 fusion.16
  (120 shorter events, 15.1 us)
Async XLA Ops:
  0.6 16.2 %collective-permute-start.1 = (bf16[192,768]{1,0:T(8,128)(2,1)}, bf16[192,768]{1,0:T(8,128)(2,1)S(1)}, u32[]{:S(2)}, u32[]{:S(2)}) collective-permute-start(bf16[192,768]{1,0:T(8,128)(2,1)} %param.5), channel_id=1, source_target_pairs={{0,8},{8,0},{16,24},{24,16},{1,9},{9,1},{17,25},{25,17},{2,10},{10... | collective-permute-start | bytes 884744 | tf_op jit(solution)/shard_map/ppermute | solution.py:17
  3.6 16.2 %collective-permute-start.8 = (bf16[192,768]{1,0:T(8,128)(2,1)}, bf16[192,768]{1,0:T(8,128)(2,1)S(1)}, u32[]{:S(2)}, u32[]{:S(2)}) collective-permute-start(bf16[192,768]{1,0:T(8,128)(2,1)} %param.5), channel_id=1, source_target_pairs={{0,4},{4,0},{1,5},{5,1},{2,6},{6,2},{3,7},{7,3},{8,12},{12,8},{9,1... | collective-permute-start | bytes 884744 | tf_op jit(solution)/shard_map/ppermute | solution.py:17
  6.2 19.4 %collective-permute-start.6 = (bf16[192,768]{1,0:T(8,128)(2,1)}, bf16[192,768]{1,0:T(8,128)(2,1)S(1)}, u32[]{:S(2)}, u32[]{:S(2)}) collective-permute-start(bf16[192,768]{1,0:T(8,128)(2,1)} %param.5), channel_id=1, source_target_pairs={{0,16},{8,24},{16,0},{24,8},{1,17},{9,25},{17,1},{25,9},{2,18},{10... | collective-permute-start | bytes 884744 | tf_op jit(solution)/shard_map/ppermute | solution.py:17
  7.7 19.5 %collective-permute-start.7 = (bf16[192,768]{1,0:T(8,128)(2,1)}, bf16[192,768]{1,0:T(8,128)(2,1)S(1)}, u32[]{:S(2)}, u32[]{:S(2)}) collective-permute-start(bf16[192,768]{1,0:T(8,128)(2,1)} %param.5), channel_id=1, source_target_pairs={{0,24},{8,16},{16,8},{24,0},{1,25},{9,17},{17,9},{25,1},{2,26},{10... | collective-permute-start | bytes 884744 | tf_op jit(solution)/shard_map/ppermute | solution.py:17
  8.2 8.6 %collective-permute-start = (bf16[128,768]{1,0:T(8,128)(2,1)}, bf16[128,768]{1,0:T(8,128)(2,1)S(1)}, u32[]{:S(2)}, u32[]{:S(2)}) collective-permute-start(bf16[128,768]{1,0:T(8,128)(2,1)} %param.4), channel_id=1, source_target_pairs={{0,2},{2,0},{1,3},{3,1},{4,6},{6,4},{5,7},{7,5},{8,10},{10,8},{9,1... | collective-permute-start | bytes 589832 | tf_op jit(solution)/shard_map/ppermute | solution.py:17
  16.8 11.3 %collective-permute-start.2 = (bf16[128,768]{1,0:T(8,128)(2,1)}, bf16[128,768]{1,0:T(8,128)(2,1)S(1)}, u32[]{:S(2)}, u32[]{:S(2)}) collective-permute-start(bf16[128,768]{1,0:T(8,128)(2,1)} %param.4), channel_id=1, source_target_pairs={{0,4},{4,0},{1,5},{5,1},{2,6},{6,2},{3,7},{7,3},{8,12},{12,8},{9,1... | collective-permute-start | bytes 589832 | tf_op jit(solution)/shard_map/ppermute | solution.py:17
  19.2 9.0 %collective-permute-start.5 = (f32[768]{0:T(1024)}, f32[768]{0:T(1024)S(1)}, u32[]{:S(2)}, u32[]{:S(2)}) collective-permute-start(f32[768]{0:T(1024)} %param.7), channel_id=1, source_target_pairs={{0,4},{4,0},{1,5},{5,1},{2,6},{6,2},{3,7},{7,3},{8,12},{12,8},{9,1... | collective-permute-start | bytes 9224 | tf_op jit(solution)/shard_map/ppermute | solution.py:17
  19.8 14.3 %collective-permute-start.9 = (bf16[192,768]{1,0:T(8,128)(2,1)S(1)}, bf16[192,768]{1,0:T(8,128)(2,1)S(1)}, u32[]{:S(2)}, u32[]{:S(2)}) collective-permute-start(bf16[192,768]{1,0:T(8,128)(2,1)S(1)} %collective-permute-done.8), channel_id=1, source_target_pairs={{0,8},{8,0},{16,24},{24,16},{1,9},{9,1},{17,25},{25,17},{2,10},{10... | collective-permute-start | bytes 884744 | tf_op jit(solution)/shard_map/ppermute | solution.py:17
  25.6 9.9 %collective-permute-start.10 = (bf16[192,768]{1,0:T(8,128)(2,1)S(1)}, bf16[192,768]{1,0:T(8,128)(2,1)S(1)}, u32[]{:S(2)}, u32[]{:S(2)}) collective-permute-start(bf16[192,768]{1,0:T(8,128)(2,1)S(1)} %collective-permute-done.8), channel_id=1, source_target_pairs={{0,16},{8,24},{16,0},{24,8},{1,17},{9,25},{17,1},{25,9},{2,18},{10... | collective-permute-start | bytes 884744 | tf_op jit(solution)/shard_map/ppermute | solution.py:17
  27.2 8.4 %collective-permute-start.11 = (bf16[192,768]{1,0:T(8,128)(2,1)S(1)}, bf16[192,768]{1,0:T(8,128)(2,1)S(1)}, u32[]{:S(2)}, u32[]{:S(2)}) collective-permute-start(bf16[192,768]{1,0:T(8,128)(2,1)S(1)} %collective-permute-done.8), channel_id=1, source_target_pairs={{0,24},{8,16},{16,8},{24,0},{1,25},{9,17},{17,9},{25,1},{2,26},{10... | collective-permute-start | bytes 884744 | tf_op jit(solution)/shard_map/ppermute | solution.py:17
  27.3 8.5 %copy-start.4 = (bf16[4,192,768]{2,1,0:T(8,128)(2,1)}, bf16[4,192,768]{2,1,0:T(8,128)(2,1)S(1)}, u32[]{:S(2)}) copy-start(bf16[4,192,768]{2,1,0:T(8,128)(2,1)S(1)} %bitcast_dynamic-update-slice_fusion.6) | copy-start | bytes 3538948
  28.2 5.8 %collective-permute-start.3 = (bf16[128,768]{1,0:T(8,128)(2,1)S(1)}, bf16[128,768]{1,0:T(8,128)(2,1)S(1)}, u32[]{:S(2)}, u32[]{:S(2)}) collective-permute-start(bf16[128,768]{1,0:T(8,128)(2,1)S(1)} %collective-permute-done.2), channel_id=1, source_target_pairs={{0,2},{2,0},{1,3},{3,1},{4,6},{6,4},{5,7},{7,5},{8,10},{10,8},{9,1... | collective-permute-start | bytes 589832 | tf_op jit(solution)/shard_map/ppermute | solution.py:17
  34.0 2.4 %collective-permute-start.4 = (bf16[2,2,128,768]{3,2,1,0:T(8,128)(2,1)S(1)}, bf16[2,2,128,768]{3,2,1,0:T(8,128)(2,1)S(1)}, u32[]{:S(2)}, u32[]{:S(2)}) collective-permute-start(bf16[2,2,128,768]{3,2,1,0:T(8,128)(2,1)S(1)} %pad_maximum_fusion), channel_id=1, source_target_pairs={{0,1},{1,0},{2,3},{3,2},{4,5},{5,4},{6,7},{7,6},{8,9},{9,8},{10,11... | collective-permute-start | bytes 2359304 | tf_op jit(solution)/shard_map/ppermute | solution.py:17
  35.6 2.3 %copy-start.2 = (bf16[4,192,768]{2,1,0:T(8,128)(2,1)}, bf16[4,192,768]{2,1,0:T(8,128)(2,1)S(1)}, u32[]{:S(2)}) copy-start(bf16[4,192,768]{2,1,0:T(8,128)(2,1)S(1)} %bitcast_dynamic-update-slice_fusion.2) | copy-start | bytes 3538948
  36.4 1.4 %copy-start.5 = (bf16[4,192,768]{2,1,0:T(8,128)(2,1)S(1)}, bf16[4,192,768]{2,1,0:T(8,128)(2,1)}, u32[]{:S(2)}) copy-start(bf16[4,192,768]{2,1,0:T(8,128)(2,1)} %copy-done.4) | copy-start | bytes 3538948
  39.3 49.7 %copy-start = (f32[1024,768]{0,1:T(8,128)}, f32[1024,768]{0,1:T(8,128)S(1)}, u32[]{:S(2)}) copy-start(f32[1024,768]{0,1:T(8,128)S(1)} %get-tuple-element.37) | copy-start | bytes 9437188
  40.4 1.2 %collective-permute-start.12 = (f32[1024]{0:T(1024)S(1)}, f32[1024]{0:T(1024)S(1)}, u32[]{:S(2)}, u32[]{:S(2)}) collective-permute-start(f32[1024]{0:T(1024)S(1)} %multiply_add_fusion.14), channel_id=1, source_target_pairs={{0,1},{1,0},{2,3},{3,2},{4,5},{5,4},{6,7},{7,6},{8,9},{9,8},{10,11... | collective-permute-start | bytes 12296 | tf_op jit(solution)/shard_map/ppermute | solution.py:17
  41.6 3.7 %collective-permute-start.13 = (f32[1024]{0:T(1024)S(1)}, f32[1024]{0:T(1024)S(1)}, u32[]{:S(2)}, u32[]{:S(2)}) collective-permute-start(f32[1024]{0:T(1024)S(1)} %multiply_add_fusion.13), channel_id=1, source_target_pairs={{0,2},{2,0},{1,3},{3,1},{4,6},{6,4},{5,7},{7,5},{8,10},{10,8},{9,1... | collective-permute-start | bytes 12296 | tf_op jit(solution)/shard_map/ppermute | solution.py:17
  47.6 4.2 %collective-permute-start.14 = (f32[1536]{0:T(1024)S(1)}, f32[1536]{0:T(1024)S(1)}, u32[]{:S(2)}, u32[]{:S(2)}) collective-permute-start(f32[1536]{0:T(1024)S(1)} %pad_maximum_fusion.1), channel_id=1, source_target_pairs={{0,8},{8,0},{16,24},{24,16},{1,9},{9,1},{17,25},{25,17},{2,10},{10... | collective-permute-start | bytes 18440 | tf_op jit(solution)/shard_map/ppermute | solution.py:17
  50.2 3.7 %collective-permute-start.15 = (f32[1536]{0:T(1024)S(1)}, f32[1536]{0:T(1024)S(1)}, u32[]{:S(2)}, u32[]{:S(2)}) collective-permute-start(f32[1536]{0:T(1024)S(1)} %pad_maximum_fusion.1), channel_id=1, source_target_pairs={{0,16},{8,24},{16,0},{24,8},{1,17},{9,25},{17,1},{25,9},{2,18},{10... | collective-permute-start | bytes 18440 | tf_op jit(solution)/shard_map/ppermute | solution.py:17
  51.7 4.5 %collective-permute-start.16 = (f32[1536]{0:T(1024)S(1)}, f32[1536]{0:T(1024)S(1)}, u32[]{:S(2)}, u32[]{:S(2)}) collective-permute-start(f32[1536]{0:T(1024)S(1)} %pad_maximum_fusion.1), channel_id=1, source_target_pairs={{0,24},{8,16},{16,8},{24,0},{1,25},{9,17},{17,9},{25,1},{2,26},{10... | collective-permute-start | bytes 18440 | tf_op jit(solution)/shard_map/ppermute | solution.py:17
  58.3 1.2 %collective-permute-start.17 = (f32[1024]{0:T(1024)S(1)}, f32[1024]{0:T(1024)S(1)}, u32[]{:S(2)}, u32[]{:S(2)}) collective-permute-start(f32[1024]{0:T(1024)S(1)} %multiply_add_fusion.10), channel_id=1, source_target_pairs={{0,1},{1,0},{2,3},{3,2},{4,5},{5,4},{6,7},{7,6},{8,9},{9,8},{10,11... | collective-permute-start | bytes 12296 | tf_op jit(solution)/shard_map/ppermute | solution.py:17
  59.5 3.7 %collective-permute-start.18 = (f32[1024]{0:T(1024)S(1)}, f32[1024]{0:T(1024)S(1)}, u32[]{:S(2)}, u32[]{:S(2)}) collective-permute-start(f32[1024]{0:T(1024)S(1)} %multiply_add_fusion.9), channel_id=1, source_target_pairs={{0,2},{2,0},{1,3},{3,1},{4,6},{6,4},{5,7},{7,5},{8,10},{10,8},{9,1... | collective-permute-start | bytes 12296 | tf_op jit(solution)/shard_map/ppermute | solution.py:17
  65.5 3.9 %collective-permute-start.19 = (f32[1536]{0:T(1024)S(1)}, f32[1536]{0:T(1024)S(1)}, u32[]{:S(2)}, u32[]{:S(2)}) collective-permute-start(f32[1536]{0:T(1024)S(1)} %pad_maximum_fusion.2), channel_id=1, source_target_pairs={{0,8},{8,0},{16,24},{24,16},{1,9},{9,1},{17,25},{25,17},{2,10},{10... | collective-permute-start | bytes 18440 | tf_op jit(solution)/shard_map/ppermute | solution.py:17
  65.8 3.7 %collective-permute-start.20 = (f32[1536]{0:T(1024)S(1)}, f32[1536]{0:T(1024)S(1)}, u32[]{:S(2)}, u32[]{:S(2)}) collective-permute-start(f32[1536]{0:T(1024)S(1)} %pad_maximum_fusion.2), channel_id=1, source_target_pairs={{0,16},{8,24},{16,0},{24,8},{1,17},{9,25},{17,1},{25,9},{2,18},{10... | collective-permute-start | bytes 18440 | tf_op jit(solution)/shard_map/ppermute | solution.py:17
  66.3 4.5 %collective-permute-start.21 = (f32[1536]{0:T(1024)S(1)}, f32[1536]{0:T(1024)S(1)}, u32[]{:S(2)}, u32[]{:S(2)}) collective-permute-start(f32[1536]{0:T(1024)S(1)} %pad_maximum_fusion.2), channel_id=1, source_target_pairs={{0,24},{8,16},{16,8},{24,0},{1,25},{9,17},{17,9},{25,1},{2,26},{10... | collective-permute-start | bytes 18440 | tf_op jit(solution)/shard_map/ppermute | solution.py:17
  72.9 1.2 %collective-permute-start.22 = (f32[1024]{0:T(1024)S(1)}, f32[1024]{0:T(1024)S(1)}, u32[]{:S(2)}, u32[]{:S(2)}) collective-permute-start(f32[1024]{0:T(1024)S(1)} %multiply_add_fusion.6), channel_id=1, source_target_pairs={{0,1},{1,0},{2,3},{3,2},{4,5},{5,4},{6,7},{7,6},{8,9},{9,8},{10,11... | collective-permute-start | bytes 12296 | tf_op jit(solution)/shard_map/ppermute | solution.py:17
  74.1 3.7 %collective-permute-start.23 = (f32[1024]{0:T(1024)S(1)}, f32[1024]{0:T(1024)S(1)}, u32[]{:S(2)}, u32[]{:S(2)}) collective-permute-start(f32[1024]{0:T(1024)S(1)} %multiply_add_fusion.5), channel_id=1, source_target_pairs={{0,2},{2,0},{1,3},{3,1},{4,6},{6,4},{5,7},{7,5},{8,10},{10,8},{9,1... | collective-permute-start | bytes 12296 | tf_op jit(solution)/shard_map/ppermute | solution.py:17
  80.1 3.7 %collective-permute-start.24 = (f32[1536]{0:T(1024)S(1)}, f32[1536]{0:T(1024)S(1)}, u32[]{:S(2)}, u32[]{:S(2)}) collective-permute-start(f32[1536]{0:T(1024)S(1)} %pad_maximum_fusion.3), channel_id=1, source_target_pairs={{0,8},{8,0},{16,24},{24,16},{1,9},{9,1},{17,25},{25,17},{2,10},{10... | collective-permute-start | bytes 18440 | tf_op jit(solution)/shard_map/ppermute | solution.py:17
  82.1 3.7 %collective-permute-start.25 = (f32[1536]{0:T(1024)S(1)}, f32[1536]{0:T(1024)S(1)}, u32[]{:S(2)}, u32[]{:S(2)}) collective-permute-start(f32[1536]{0:T(1024)S(1)} %pad_maximum_fusion.3), channel_id=1, source_target_pairs={{0,16},{8,24},{16,0},{24,8},{1,17},{9,25},{17,1},{25,9},{2,18},{10... | collective-permute-start | bytes 18440 | tf_op jit(solution)/shard_map/ppermute | solution.py:17
  83.7 4.5 %collective-permute-start.26 = (f32[1536]{0:T(1024)S(1)}, f32[1536]{0:T(1024)S(1)}, u32[]{:S(2)}, u32[]{:S(2)}) collective-permute-start(f32[1536]{0:T(1024)S(1)} %pad_maximum_fusion.3), channel_id=1, source_target_pairs={{0,24},{8,16},{16,8},{24,0},{1,25},{9,17},{17,9},{25,1},{2,26},{10... | collective-permute-start | bytes 18440 | tf_op jit(solution)/shard_map/ppermute | solution.py:17
  89.2 1.2 %collective-permute-start.27 = (f32[512]{0:T(512)S(1)}, f32[512]{0:T(512)S(1)}, u32[]{:S(2)}, u32[]{:S(2)}) collective-permute-start(f32[512]{0:T(512)S(1)} %max.81), channel_id=1, source_target_pairs={{0,1},{1,0},{2,3},{3,2},{4,5},{5,4},{6,7},{7,6},{8,9},{9,8},{10,11... | collective-permute-start | bytes 6152 | tf_op jit(solution)/shard_map/ppermute | solution.py:17
  90.5 3.6 %collective-permute-start.28 = (f32[512]{0:T(512)S(1)}, f32[512]{0:T(512)S(1)}, u32[]{:S(2)}, u32[]{:S(2)}) collective-permute-start(f32[512]{0:T(512)S(1)} %max.82), channel_id=1, source_target_pairs={{0,2},{2,0},{1,3},{3,1},{4,6},{6,4},{5,7},{7,5},{8,10},{10,8},{9,1... | collective-permute-start | bytes 6152 | tf_op jit(solution)/shard_map/ppermute | solution.py:17
  90.5 6.3 %copy-start.3 = (bf16[4,192,768]{2,1,0:T(8,128)(2,1)S(1)}, bf16[4,192,768]{2,1,0:T(8,128)(2,1)}, u32[]{:S(2)}) copy-start(bf16[4,192,768]{2,1,0:T(8,128)(2,1)} %copy-done.2) | copy-start | bytes 3538948
  96.8 1.9 %copy-start.1 = (f32[1024,768]{0,1:T(8,128)S(1)}, f32[1024,768]{0,1:T(8,128)}, u32[]{:S(2)}) copy-start(f32[1024,768]{0,1:T(8,128)} %copy-done) | copy-start | bytes 9437188
  97.9 2.7 %collective-permute-start.29 = (f32[2,128,768]{2,1,0:T(8,128)S(1)}, f32[2,128,768]{2,1,0:T(8,128)S(1)}, u32[]{:S(2)}, u32[]{:S(2)}) collective-permute-start(f32[2,128,768]{2,1,0:T(8,128)S(1)} %dynamic-slice_bitcast_fusion), channel_id=1, source_target_pairs={{0,1},{1,0},{2,3},{3,2},{4,5},{5,4},{6,7},{7,6},{8,9},{9,8},{10,11... | collective-permute-start | bytes 2359304 | tf_op jit(solution)/shard_map/ppermute | solution.py:17
  99.4 1.2 %collective-permute-start.31 = (f32[2,128]{1,0:T(2,128)S(1)}, f32[2,128]{1,0:T(2,128)S(1)}, u32[]{:S(2)}, u32[]{:S(2)}) collective-permute-start(f32[2,128]{1,0:T(2,128)S(1)} %fusion.37), channel_id=1, source_target_pairs={{0,1},{1,0},{2,3},{3,2},{4,5},{5,4},{6,7},{7,6},{8,9},{9,8},{10,11... | collective-permute-start | bytes 3080 | tf_op jit(solution)/shard_map/ppermute | solution.py:17
  100.7 11.4 %collective-permute-start.30 = (f32[128,768]{1,0:T(8,128)S(1)}, f32[128,768]{1,0:T(8,128)S(1)}, u32[]{:S(2)}, u32[]{:S(2)}) collective-permute-start(f32[128,768]{1,0:T(8,128)S(1)} %dynamic-slice_bitcast_fusion.1), channel_id=1, source_target_pairs={{0,2},{2,0},{1,3},{3,1},{4,6},{6,4},{5,7},{7,5},{8,10},{10,8},{9,1... | collective-permute-start | bytes 1179656 | tf_op jit(solution)/shard_map/ppermute | solution.py:17
  100.8 11.2 %collective-permute-start.32 = (f32[128]{0:T(128)S(1)}, f32[128]{0:T(128)S(1)}, u32[]{:S(2)}, u32[]{:S(2)}) collective-permute-start(f32[128]{0:T(128)S(1)} %fusion.40), channel_id=1, source_target_pairs={{0,2},{2,0},{1,3},{3,1},{4,6},{6,4},{5,7},{7,5},{8,10},{10,8},{9,1... | collective-permute-start | bytes 1544 | tf_op jit(solution)/shard_map/ppermute | solution.py:17

commit v4 on v3

v4 whole, which is shorter than its diff:
```python
import functools
import math

import jax
import jax.numpy as jnp
from jax import lax
from jax.experimental import pallas as pl
from jax.experimental.pallas import tpu as pltpu
from jax.sharding import Mesh
from jax.sharding import PartitionSpec as P

ITERS = 3
EPSILON = 0.5
LOG2E = 1.0 / math.log(2.0)
LANES = 128


def swap(x, axes, k):
    n = lax.axis_size(axes)
    return lax.ppermute(x, axes, [(i, i ^ k) for i in range(n)])


def swaps(x, axes):
    return [x] + [swap(x, axes, k) for k in range(1, lax.axis_size(axes))]


def place(blocks, index):
    whole = jnp.zeros((len(blocks),) + blocks[0].shape, blocks[0].dtype)
    for k, block in enumerate(blocks):
        whole = lax.dynamic_update_index_in_dim(whole, block, index ^ k, 0)
    return whole


def pick(x, index, axis):
    return lax.dynamic_index_in_dim(x, index, axis, False)


def lse_of(parts):
    highest = parts[0]
    for part in parts[1:]:
        highest = jnp.maximum(highest, part)
    total = jnp.exp2(parts[0] - highest)
    for part in parts[1:]:
        total = total + jnp.exp2(part - highest)
    return highest + jnp.log2(total)


def groups(x):
    return x.reshape(x.shape[0] // 8, 8, LANES)


def row_kernel(n, *refs):
    tiles, (side, out, *peak) = refs[:n], refs[n:]
    for at in range(out.shape[0]):
        rows = pl.ds(at * LANES, LANES)

        def blocks():
            c = 0
            for t in tiles:
                for k in range(0, t.shape[1], LANES):
                    yield t[rows, k : k + LANES] + side[c : c + 1, :]
                    c += 1

        m = functools.reduce(jnp.maximum, blocks())
        s = sum(jnp.exp2(x - m) for x in blocks())
        m, s = m.T, s.T
        high = jnp.max(m, axis=0, keepdims=True)
        s = jnp.sum(s * jnp.exp2(m - high), axis=0, keepdims=True)
        out[at : at + 1, :] = high + jnp.log2(s)
        if peak:
            peak[0][at : at + 1, :] = high


def col_kernel(n, *refs):
    tiles, (side, out, wide) = refs[:n], refs[n:]
    for at in range(side.shape[0]):
        wide[at * LANES : (at + 1) * LANES, :] = jnp.broadcast_to(side[at : at + 1, :], (LANES, LANES)).T
    c = 0
    for t in tiles:
        for k in range(0, t.shape[1], LANES):

            def blocks():
                for r in range(0, t.shape[0], LANES):
                    yield groups(t[r : r + LANES, k : k + LANES] + wide[r : r + LANES, :])

            m = functools.reduce(jnp.maximum, (jnp.max(x, axis=0) for x in blocks()))
            s = sum(jnp.sum(jnp.exp2(x - m[None]), axis=0) for x in blocks())
            high = jnp.max(m, axis=0, keepdims=True)
            s = jnp.sum(s * jnp.exp2(m - high), axis=0, keepdims=True)
            out[c : c + 1, :] = high + jnp.log2(s)
            c += 1


def map_kernel(tile0, tile1, tools0, tools1, side, peak, lse, first, out):
    start = first[0]
    for r in range(0, out.shape[0], LANES):
        at = pl.multiple_of(start * LANES + r, LANES)
        which = start + r // LANES

        def wide(ref):
            return jnp.broadcast_to(ref[pl.ds(which, 1), :], (LANES, LANES)).T

        high = wide(peak)
        total = None
        c = 0
        for tile, tools in ((tile0, tools0), (tile1, tools1)):
            weights = []
            for k in range(0, tile.shape[1], LANES):
                x = tile[pl.ds(at, LANES), k : k + LANES] + side[c : c + 1, :]
                weights.append(jnp.exp2(x - high).astype(jnp.bfloat16))
                c += 1
            part = jnp.dot(jnp.concatenate(weights, axis=1), tools[...], preferred_element_type=jnp.float32)
            total = part if total is None else total + part
        scale = jnp.exp2(high - wide(lse))
        for k in range(0, out.shape[1], LANES):
            out[r : r + LANES, k : k + LANES] = total[:, k : k + LANES] * scale


def call(kernel, out_shape, args, scratch=(), flops=0, scalars=0):
    vmem, smem = (pl.BlockSpec(memory_space=m) for m in (pltpu.VMEM, pltpu.SMEM))
    size = sum(a.size for a in args)
    return pl.pallas_call(
        kernel,
        out_shape=out_shape,
        in_specs=[vmem] * (len(args) - scalars) + [smem] * scalars,
        out_specs=jax.tree.map(lambda _: vmem, out_shape),
        scratch_shapes=scratch,
        compiler_params=pltpu.CompilerParams(vmem_limit_bytes=32 << 20),
        cost_estimate=pl.CostEstimate(flops=flops or 6 * size, bytes_accessed=4 * size, transcendentals=size),
    )(*args)


def vector(n):
    return jax.ShapeDtypeStruct((n // LANES, LANES), jnp.float32)


def row_pass(tiles, side, n, peaks=False):
    return call(functools.partial(row_kernel, len(tiles)), [vector(n)] * (2 if peaks else 1), tiles + [side])


def col_pass(tiles, side):
    scratch = [pltpu.VMEM((tiles[0].shape[0], LANES), jnp.float32)]
    return call(functools.partial(col_kernel, len(tiles)), vector(sum(t.shape[1] for t in tiles)), tiles + [side], scratch)


def dot_kernel(scaling, a, b, out):
    for r in range(0, out.shape[0], 256):
        part = lax.dot_general(
            a[r : r + 256, :], b[...], (((1,), (1,)), ((), ())), preferred_element_type=jnp.float32
        )
        out[r : r + 256, :] = part * scaling


def scaled_dot(a, b, scaling):
    out_shape = jax.ShapeDtypeStruct((a.shape[0], b.shape[0]), jnp.float32)
    return call(functools.partial(dot_kernel, scaling), out_shape, [a, b], flops=2 * a.size * b.shape[0])


def pairs(x, axes):
    return [x, swap(x, axes, 1)]


def by_place(pair, index):
    first = index == 0
    return jnp.stack([jnp.where(first, pair[0], pair[1]), jnp.where(first, pair[1], pair[0])])


def local(queries, tools, query_mass, tool_mass):
    rows = lax.axis_size("row")
    nl = lax.axis_size("zl")
    ri, hi, li, core = (lax.axis_index(a) for a in ("row", "zh", "zl", "core"))
    bq, features = queries.shape
    bt = tools.shape[0]
    scaling = LOG2E / (math.sqrt(features) * EPSILON)

    other_tools = swap(tools, "zh", 1)
    own = swaps(tools, "row")
    half = nl * bq
    firsts = [jnp.full((1,), c * (half // LANES), jnp.int32) for c in (core, 1 - core)]
    held, held_mass, firsts, own[1] = lax.optimization_barrier((queries, tool_mass, firsts, own[1]))
    tile_tools = [place(t, ri).reshape(-1, features) for t in (own, swaps(other_tools, "row"))]
    far, other_mass = swap(held, "zh", 1), swap(held_mass, "zh", 1)
    near_queries = place(swaps(queries, "zl"), li)
    far_queries = place(swaps(far, "zl"), li)
    far_queries, other_mass = lax.optimization_barrier((far_queries, other_mass))
    tile_queries = jnp.stack([near_queries, far_queries])
    tile_queries = jnp.moveaxis(place(pairs(tile_queries, "core"), core), 0, 1).reshape(-1, features)
    log_tool = jnp.concatenate([jnp.log2(tool_mass), jnp.log2(other_mass)]).reshape(-1, LANES)
    log_query = jnp.log2(query_mass).reshape(2, nl, 2, bq).transpose(0, 2, 1, 3)
    log_query = by_place([log_query[0], log_query[1]], hi).reshape(-1, LANES)

    tiles = [scaled_dot(tile_queries, t, scaling) for t in tile_tools]
    tool_side = jnp.zeros_like(log_tool)
    for sweep in range(ITERS):
        (part,) = row_pass(tiles, tool_side, log_query.size)
        part = lse_of(swaps(part, "core"))
        query_side = log_query - lse_of(swaps(part, "zl"))
        tool_side = log_tool - lse_of(swaps(col_pass(tiles, query_side), "row"))

    ends = jnp.stack(row_pass(tiles, tool_side, log_query.size // 2, True))
    for axis in ("core", "zl"):
        got = swaps(ends, axis)
        ends = jnp.stack([lse_of([g[0] for g in got]), functools.reduce(jnp.maximum, [g[1] for g in got])])
    lse, peak = ends

    def mapped_rows(first):
        args = tiles + tile_tools + [tool_side, peak, lse, first]
        flops = 2 * half * tool_side.size * features
        return call(map_kernel, jax.ShapeDtypeStruct((half, features), jnp.float32), args, (), flops, 1)

    others = swap(mapped_rows(firsts[1]), "core", 1).reshape(nl, bq, features)
    own = mapped_rows(firsts[0]).reshape(nl, bq, features)
    summed = [pick(own, li ^ k, 0) + pick(others, li ^ k, 0) for k in range(nl)]
    summed = sum([summed[0]] + [swap(summed[k].astype(jnp.float16), "zl", k).astype(jnp.float32) for k in range(1, nl)])
    mapped = summed.astype(jnp.bfloat16)

    unit = EPSILON / LOG2E
    query_potential = query_side.reshape(2, 2, nl, bq).transpose(0, 2, 1, 3)
    query_potential = unit * by_place([query_potential[0], query_potential[1]], hi).reshape(-1)
    return (mapped, query_potential, unit * tool_side.reshape(-1)[: tool_mass.shape[0]])


def solution(mesh):
    rows, cols = mesh.shape["row"], mesh.shape["col"]
    fine = Mesh(mesh.devices.reshape(rows, 2, cols // 4, 2), ("row", "zh", "zl", "core"))
    col = ("zh", "zl", "core")
    in_specs = (P(("row",) + col, None), P(col + ("row",), None), P("row"), P(col))
    out_specs = (P(("row",) + col, None), P("row"), P(col))
    return jax.shard_map(local, mesh=fine, in_specs=in_specs, out_specs=out_specs, check_vma=False)
```

time: 114 us -> 103 us (0.904)
  Pallas kernels: 0 us -> 13.7 us
  other arithmetic: 16.1 us -> 2.49 us
  waiting for transfers between devices: 47.6 us -> 39.1 us
  starting transfers between devices: 37.4 us -> 44 us
  matrix products: 6.56 us -> 0 us
  local copies, waits for them, and re-layouts: 4 us -> 2.21 us
    pallas_call x0 -> x11, Pallas kernels: none -> 13.7 us  [call(): pl.pallas_call(kernel, out_shape=out_shape, in_specs=[vmem] * (len(args)...]
    reduce_sum x12 -> x0, other arithmetic: 10.4 us -> none  [the longest x11 9.65 us: local_lse(): total = jnp.sum(jnp.exp2(scores - highest), axis=axis)]
    ppermute x33 -> x31, waiting for transfers between devices: 47.6 us -> 39.1 us  [swap(): return lax.ppermute(x, axes, [(i, i ^ k) for i in range(n)])]
    ppermute x33 -> x31, starting transfers between devices: 37.4 us -> 44 us  [swap(): return lax.ppermute(x, axes, [(i, i ^ k) for i in range(n)])]
    dot_general x4 -> x0, matrix products: 6.56 us -> none  [the longest x2 3.71 us: local(): jnp.dot(e.astype(jnp.bfloat16), t, preferred_element_type=jnp.float32)]
    reduce_max x9 -> x0, other arithmetic: 2.33 us -> none  [the longest x7 1.96 us: local_lse(): highest = jnp.max(scores, axis=axis, keepdims=True)]
  transfers between devices with their start and end apart: 33 -> 31, of which waited for: 24 -> 25; matrix products, arithmetic and copies ran while one was open for 5% -> 3% of each run, Pallas kernels for 0% -> 1%
where the time goes in v4:
time: 103 us
  starting transfers between devices  44 us (43%)
  waiting for transfers between devices  39.1 us (38%)
  Pallas kernels  13.7 us (13%)
  other arithmetic  2.49 us (2%)
  local copies, waits for them, and re-layouts  2.21 us (2%)
  between operations  1.05 us (1%)
    ppermute x31, starting transfers between devices, swap(): return lax.ppermute(x, axes, [(i, i ^ k) for i in range(n)])  44 us
    ppermute x31, waiting for transfers between devices, swap(): return lax.ppermute(x, axes, [(i, i ^ k) for i in range(n)])  39.1 us
    pallas_call x11, Pallas kernels, call(): pl.pallas_call(kernel, out_shape=out_shape, in_specs=[vmem] * (len(args)...  13.7 us
  transfers between devices with their start and end apart: 31, of which 25 were waited for; matrix products, arithmetic and copies ran while one was open for 3% of the time, Pallas kernels for 1%

profile of v4, /device:TPU:0, one launch (start us, length us, event | category | flops | bytes accessed | tf_op | source)
XLA Modules:
  0.0 102.6 jit_solution(10505890407316410893)
XLA Ops:
  0.6 3.0 %collective-permute-start.1 = (bf16[192,768]{1,0:T(8,128)(2,1)}, bf16[192,768]{1,0:T(8,128)(2,1)S(1)}, u32[]{:S(2)}, u32[]{:S(2)}) collective-permute-start(bf16[192,768]{1,0:T(8,128)(2,1)} %param.5), channel_id=1, source_target_pairs={{0,8},{8,0},{16,24},{24,16},{1,9},{9,1},{17,25},{25,17},{2,10},{10... | collective-permute-start | bytes 884744 | tf_op jit(solution)/shard_map/ppermute | solution.py:20
  3.6 2.6 %collective-permute-start.8 = (bf16[192,768]{1,0:T(8,128)(2,1)}, bf16[192,768]{1,0:T(8,128)(2,1)S(1)}, u32[]{:S(2)}, u32[]{:S(2)}) collective-permute-start(bf16[192,768]{1,0:T(8,128)(2,1)} %param.5), channel_id=1, source_target_pairs={{0,4},{4,0},{1,5},{5,1},{2,6},{6,2},{3,7},{7,3},{8,12},{12,8},{9,1... | collective-permute-start | bytes 884744 | tf_op jit(solution)/shard_map/ppermute | solution.py:20
  6.2 1.5 %collective-permute-start.6 = (bf16[192,768]{1,0:T(8,128)(2,1)}, bf16[192,768]{1,0:T(8,128)(2,1)S(1)}, u32[]{:S(2)}, u32[]{:S(2)}) collective-permute-start(bf16[192,768]{1,0:T(8,128)(2,1)} %param.5), channel_id=1, source_target_pairs={{0,16},{8,24},{16,0},{24,8},{1,17},{9,25},{17,1},{25,9},{2,18},{10... | collective-permute-start | bytes 884744 | tf_op jit(solution)/shard_map/ppermute | solution.py:20
  8.2 1.6 %collective-permute-start = (bf16[128,768]{1,0:T(8,128)(2,1)}, bf16[128,768]{1,0:T(8,128)(2,1)S(1)}, u32[]{:S(2)}, u32[]{:S(2)}) collective-permute-start(bf16[128,768]{1,0:T(8,128)(2,1)} %param.4), channel_id=1, source_target_pairs={{0,2},{2,0},{1,3},{3,1},{4,6},{6,4},{5,7},{7,5},{8,10},{10,8},{9,1... | collective-permute-start | bytes 589832 | tf_op jit(solution)/shard_map/ppermute | solution.py:20
  10.5 0.9 bitcast_dynamic-update-slice_fusion.13
  11.7 5.1 %collective-permute-done = bf16[128,768]{1,0:T(8,128)(2,1)S(1)} collective-permute-done((bf16[128,768]{1,0:T(8,128)(2,1)}, bf16[128,768]{1,0:T(8,128)(2,1)S(1)}, u32[]{:S(2)}, u32[]{:S(2)}) %collective-permute-start) | collective-permute-done | bytes 196640 | tf_op jit(solution)/shard_map/ppermute | solution.py:20
  16.8 2.3 %collective-permute-start.2 = (bf16[128,768]{1,0:T(8,128)(2,1)S(1)}, bf16[128,768]{1,0:T(8,128)(2,1)S(1)}, u32[]{:S(2)}, u32[]{:S(2)}) collective-permute-start(bf16[128,768]{1,0:T(8,128)(2,1)S(1)} %copy-done.1), channel_id=1, source_target_pairs={{0,4},{4,0},{1,5},{5,1},{2,6},{6,2},{3,7},{7,3},{8,12},{12,8},{9,1... | collective-permute-start | bytes 589832 | tf_op jit(solution)/shard_map/ppermute | solution.py:20
  20.0 5.3 %collective-permute-start.9 = (bf16[192,768]{1,0:T(8,128)(2,1)S(1)}, bf16[192,768]{1,0:T(8,128)(2,1)S(1)}, u32[]{:S(2)}, u32[]{:S(2)}) collective-permute-start(bf16[192,768]{1,0:T(8,128)(2,1)S(1)} %collective-permute-done.8), channel_id=1, source_target_pairs={{0,8},{8,0},{16,24},{24,16},{1,9},{9,1},{17,25},{25,17},{2,10},{10... | collective-permute-start | bytes 884744 | tf_op jit(solution)/shard_map/ppermute | solution.py:20
  25.4 1.6 %collective-permute-start.10 = (bf16[192,768]{1,0:T(8,128)(2,1)S(1)}, bf16[192,768]{1,0:T(8,128)(2,1)S(1)}, u32[]{:S(2)}, u32[]{:S(2)}) collective-permute-start(bf16[192,768]{1,0:T(8,128)(2,1)S(1)} %collective-permute-done.8), channel_id=1, source_target_pairs={{0,16},{8,24},{16,0},{24,8},{1,17},{9,25},{17,1},{25,9},{2,18},{10... | collective-permute-start | bytes 884744 | tf_op jit(solution)/shard_map/ppermute | solution.py:20
  27.2 1.0 collective-permute-done.2
  28.9 4.9 %collective-permute-done.3 = bf16[128,768]{1,0:T(8,128)(2,1)S(1)} collective-permute-done((bf16[128,768]{1,0:T(8,128)(2,1)S(1)}, bf16[128,768]{1,0:T(8,128)(2,1)S(1)}, u32[]{:S(2)}, u32[]{:S(2)}) %collective-permute-start.3) | collective-permute-done | bytes 196640 | tf_op jit(solution)/shard_map/ppermute | solution.py:20
  34.0 1.3 %collective-permute-done.10 = bf16[192,768]{1,0:T(8,128)(2,1)S(1)} collective-permute-done((bf16[192,768]{1,0:T(8,128)(2,1)S(1)}, bf16[192,768]{1,0:T(8,128)(2,1)S(1)}, u32[]{:S(2)}, u32[]{:S(2)}) %collective-permute-start.10) | collective-permute-done | bytes 294944 | tf_op jit(solution)/shard_map/ppermute | solution.py:20
  36.3 1.4 %shard_map.68.refs_1_.tile1 = f32[1024,768]{1,0:T(8,128)S(1)} custom-call(bf16[1024,768]{1,0:T(8,128)(2,1)S(1)} %bitcast.96, bf16[768,768]{1,0:T(8,128)(2,1)S(1)} %bitcast.90), custom_call_target="tpu_custom_call" | custom-call | flops 1207959552 | bytes 5505024 | tf_op jit(solution)/shard_map/pallas_call | solution.py:122
  37.8 1.4 %shard_map.67.refs_0_.tile0 = f32[1024,768]{1,0:T(8,128)S(1)} custom-call(bf16[1024,768]{1,0:T(8,128)(2,1)S(1)} %bitcast.97, bf16[768,768]{1,0:T(8,128)(2,1)S(1)} %bitcast.93), custom_call_target="tpu_custom_call" | custom-call | flops 1207959552 | bytes 5505024 | tf_op jit(solution)/shard_map/pallas_call | solution.py:122
  39.2 1.3 %shard_map.69 = f32[8,128]{1,0:T(8,128)S(1)} custom-call(f32[1024,768]{1,0:T(8,128)S(1)} %shard_map.67.refs_0_.tile0, f32[1024,768]{1,0:T(8,128)S(1)} %shard_map.68.refs_1_.tile1, f32[12,128]{1,0:T(8,128)S(1)} %broadcast_in_dim.68.refs_2_), custom_call_target="tpu_custom_call" | custom-call | flops 9446400 | bytes 6297600 | tf_op jit(solution)/shard_map/pallas_call | solution.py:122
  40.7 1.0 collective-permute-done.12
  41.8 4.7 %collective-permute-start.13 = (f32[8,128]{1,0:T(8,128)S(1)}, f32[8,128]{1,0:T(8,128)S(1)}, u32[]{:S(2)}, u32[]{:S(2)}) collective-permute-start(f32[8,128]{1,0:T(8,128)S(1)} %multiply_add_fusion.2), channel_id=1, source_target_pairs={{0,2},{2,0},{1,3},{3,1},{4,6},{6,4},{5,7},{7,5},{8,10},{10,8},{9,1... | collective-permute-start | bytes 12296 | tf_op jit(solution)/shard_map/ppermute | solution.py:20
  46.5 1.6 %collective-permute-done.13 = f32[8,128]{1,0:T(8,128)S(1)} collective-permute-done((f32[8,128]{1,0:T(8,128)S(1)}, f32[8,128]{1,0:T(8,128)S(1)}, u32[]{:S(2)}, u32[]{:S(2)}) %collective-permute-start.13) | collective-permute-done | bytes 4128 | tf_op jit(solution)/shard_map/ppermute | solution.py:20
  48.1 1.4 %shard_map.70 = f32[12,128]{1,0:T(8,128)S(1)} custom-call(f32[1024,768]{1,0:T(8,128)S(1)} %shard_map.67.refs_0_.tile0, f32[1024,768]{1,0:T(8,128)S(1)} %shard_map.68.refs_1_.tile1, f32[8,128]{1,0:T(8,128)S(1)} %add_subtract_fusion.5.refs_2_), custom_call_target="tpu_custom_call" | custom-call | flops 9443328 | bytes 6295552 | tf_op jit(solution)/shard_map/pallas_call | solution.py:122
  49.5 1.1 %collective-permute-start.14 = (f32[12,128]{1,0:T(8,128)S(1)}, f32[12,128]{1,0:T(8,128)S(1)}, u32[]{:S(2)}, u32[]{:S(2)}) collective-permute-start(f32[12,128]{1,0:T(8,128)S(1)} %shard_map.70), channel_id=1, source_target_pairs={{0,8},{8,0},{16,24},{24,16},{1,9},{9,1},{17,25},{25,17},{2,10},{10... | collective-permute-start | bytes 18440 | tf_op jit(solution)/shard_map/ppermute | solution.py:20
  50.6 1.5 %collective-permute-start.15 = (f32[12,128]{1,0:T(8,128)S(1)}, f32[12,128]{1,0:T(8,128)S(1)}, u32[]{:S(2)}, u32[]{:S(2)}) collective-permute-start(f32[12,128]{1,0:T(8,128)S(1)} %shard_map.70), channel_id=1, source_target_pairs={{0,16},{8,24},{16,0},{24,8},{1,17},{9,25},{17,1},{25,9},{2,18},{10... | collective-permute-start | bytes 18440 | tf_op jit(solution)/shard_map/ppermute | solution.py:20
  52.1 0.9 collective-permute-start.16
  53.2 1.0 %collective-permute-done.15 = f32[12,128]{1,0:T(8,128)S(1)} collective-permute-done((f32[12,128]{1,0:T(8,128)S(1)}, f32[12,128]{1,0:T(8,128)S(1)}, u32[]{:S(2)}, u32[]{:S(2)}) %collective-permute-start.15) | collective-permute-done | bytes 6176 | tf_op jit(solution)/shard_map/ppermute | solution.py:20
  54.2 2.4 %collective-permute-done.16 = f32[12,128]{1,0:T(8,128)S(1)} collective-permute-done((f32[12,128]{1,0:T(8,128)S(1)}, f32[12,128]{1,0:T(8,128)S(1)}, u32[]{:S(2)}, u32[]{:S(2)}) %collective-permute-start.16) | collective-permute-done | bytes 6176 | tf_op jit(solution)/shard_map/ppermute | solution.py:20
  56.7 1.3 %shard_map.71 = f32[8,128]{1,0:T(8,128)S(1)} custom-call(f32[1024,768]{1,0:T(8,128)S(1)} %shard_map.67.refs_0_.tile0, f32[1024,768]{1,0:T(8,128)S(1)} %shard_map.68.refs_1_.tile1, f32[12,128]{1,0:T(8,128)S(1)} %add_subtract_fusion.2.refs_2_), custom_call_target="tpu_custom_call" | custom-call | flops 9446400 | bytes 6297600 | tf_op jit(solution)/shard_map/pallas_call | solution.py:122
  58.1 1.2 %collective-permute-done.17 = f32[8,128]{1,0:T(8,128)S(1)} collective-permute-done((f32[8,128]{1,0:T(8,128)S(1)}, f32[8,128]{1,0:T(8,128)S(1)}, u32[]{:S(2)}, u32[]{:S(2)}) %collective-permute-start.17) | collective-permute-done | bytes 4128 | tf_op jit(solution)/shard_map/ppermute | solution.py:20
  59.3 2.1 %collective-permute-start.18 = (f32[8,128]{1,0:T(8,128)S(1)}, f32[8,128]{1,0:T(8,128)S(1)}, u32[]{:S(2)}, u32[]{:S(2)}) collective-permute-start(f32[8,128]{1,0:T(8,128)S(1)} %multiply_add_fusion.1), channel_id=1, source_target_pairs={{0,2},{2,0},{1,3},{3,1},{4,6},{6,4},{5,7},{7,5},{8,10},{10,8},{9,1... | collective-permute-start | bytes 12296 | tf_op jit(solution)/shard_map/ppermute | solution.py:20
  61.3 1.6 %collective-permute-done.18 = f32[8,128]{1,0:T(8,128)S(1)} collective-permute-done((f32[8,128]{1,0:T(8,128)S(1)}, f32[8,128]{1,0:T(8,128)S(1)}, u32[]{:S(2)}, u32[]{:S(2)}) %collective-permute-start.18) | collective-permute-done | bytes 4128 | tf_op jit(solution)/shard_map/ppermute | solution.py:20
  62.9 1.4 %shard_map.72 = f32[12,128]{1,0:T(8,128)S(1)} custom-call(f32[1024,768]{1,0:T(8,128)S(1)} %shard_map.67.refs_0_.tile0, f32[1024,768]{1,0:T(8,128)S(1)} %shard_map.68.refs_1_.tile1, f32[8,128]{1,0:T(8,128)S(1)} %add_subtract_fusion.4.refs_2_), custom_call_target="tpu_custom_call" | custom-call | flops 9443328 | bytes 6295552 | tf_op jit(solution)/shard_map/pallas_call | solution.py:122
  64.7 1.2 %collective-permute-start.20 = (f32[12,128]{1,0:T(8,128)S(1)}, f32[12,128]{1,0:T(8,128)S(1)}, u32[]{:S(2)}, u32[]{:S(2)}) collective-permute-start(f32[12,128]{1,0:T(8,128)S(1)} %shard_map.72), channel_id=1, source_target_pairs={{0,16},{8,24},{16,0},{24,8},{1,17},{9,25},{17,1},{25,9},{2,18},{10... | collective-permute-start | bytes 18440 | tf_op jit(solution)/shard_map/ppermute | solution.py:20
  65.9 2.0 %collective-permute-start.21 = (f32[12,128]{1,0:T(8,128)S(1)}, f32[12,128]{1,0:T(8,128)S(1)}, u32[]{:S(2)}, u32[]{:S(2)}) collective-permute-start(f32[12,128]{1,0:T(8,128)S(1)} %shard_map.72), channel_id=1, source_target_pairs={{0,24},{8,16},{16,8},{24,0},{1,25},{9,17},{17,9},{25,1},{2,26},{10... | collective-permute-start | bytes 18440 | tf_op jit(solution)/shard_map/ppermute | solution.py:20
  68.4 2.1 %collective-permute-done.21 = f32[12,128]{1,0:T(8,128)S(1)} collective-permute-done((f32[12,128]{1,0:T(8,128)S(1)}, f32[12,128]{1,0:T(8,128)S(1)}, u32[]{:S(2)}, u32[]{:S(2)}) %collective-permute-start.21) | collective-permute-done | bytes 6176 | tf_op jit(solution)/shard_map/ppermute | solution.py:20
  70.5 1.3 %shard_map.73 = f32[8,128]{1,0:T(8,128)S(1)} custom-call(f32[1024,768]{1,0:T(8,128)S(1)} %shard_map.67.refs_0_.tile0, f32[1024,768]{1,0:T(8,128)S(1)} %shard_map.68.refs_1_.tile1, f32[12,128]{1,0:T(8,128)S(1)} %add_subtract_fusion.1.refs_2_), custom_call_target="tpu_custom_call" | custom-call | flops 9446400 | bytes 6297600 | tf_op jit(solution)/shard_map/pallas_call | solution.py:122
  71.9 1.2 %collective-permute-done.22 = f32[8,128]{1,0:T(8,128)S(1)} collective-permute-done((f32[8,128]{1,0:T(8,128)S(1)}, f32[8,128]{1,0:T(8,128)S(1)}, u32[]{:S(2)}, u32[]{:S(2)}) %collective-permute-start.22) | collective-permute-done | bytes 4128 | tf_op jit(solution)/shard_map/ppermute | solution.py:20
  73.1 2.1 %collective-permute-start.23 = (f32[8,128]{1,0:T(8,128)S(1)}, f32[8,128]{1,0:T(8,128)S(1)}, u32[]{:S(2)}, u32[]{:S(2)}) collective-permute-start(f32[8,128]{1,0:T(8,128)S(1)} %multiply_add_fusion), channel_id=1, source_target_pairs={{0,2},{2,0},{1,3},{3,1},{4,6},{6,4},{5,7},{7,5},{8,10},{10,8},{9,1... | collective-permute-start | bytes 12296 | tf_op jit(solution)/shard_map/ppermute | solution.py:20
  75.2 1.6 %collective-permute-done.23 = f32[8,128]{1,0:T(8,128)S(1)} collective-permute-done((f32[8,128]{1,0:T(8,128)S(1)}, f32[8,128]{1,0:T(8,128)S(1)}, u32[]{:S(2)}, u32[]{:S(2)}) %collective-permute-start.23) | collective-permute-done | bytes 4128 | tf_op jit(solution)/shard_map/ppermute | solution.py:20
  76.8 1.6 %shard_map.74 = f32[12,128]{1,0:T(8,128)S(1)} custom-call(f32[1024,768]{1,0:T(8,128)S(1)} %shard_map.67.refs_0_.tile0, f32[1024,768]{1,0:T(8,128)S(1)} %shard_map.68.refs_1_.tile1, f32[8,128]{1,0:T(8,128)S(1)} %add_subtract_fusion.3.refs_2_), custom_call_target="tpu_custom_call" | custom-call | flops 9443328 | bytes 6295552 | tf_op jit(solution)/shard_map/pallas_call | solution.py:122
  78.4 1.1 %collective-permute-start.24 = (f32[12,128]{1,0:T(8,128)S(1)}, f32[12,128]{1,0:T(8,128)S(1)}, u32[]{:S(2)}, u32[]{:S(2)}) collective-permute-start(f32[12,128]{1,0:T(8,128)S(1)} %shard_map.74), channel_id=1, source_target_pairs={{0,8},{8,0},{16,24},{24,16},{1,9},{9,1},{17,25},{25,17},{2,10},{10... | collective-permute-start | bytes 18440 | tf_op jit(solution)/shard_map/ppermute | solution.py:20
  79.5 1.5 %collective-permute-start.25 = (f32[12,128]{1,0:T(8,128)S(1)}, f32[12,128]{1,0:T(8,128)S(1)}, u32[]{:S(2)}, u32[]{:S(2)}) collective-permute-start(f32[12,128]{1,0:T(8,128)S(1)} %shard_map.74), channel_id=1, source_target_pairs={{0,16},{8,24},{16,0},{24,8},{1,17},{9,25},{17,1},{25,9},{2,18},{10... | collective-permute-start | bytes 18440 | tf_op jit(solution)/shard_map/ppermute | solution.py:20
  81.0 0.9 collective-permute-start.26
  82.1 1.0 %collective-permute-done.25 = f32[12,128]{1,0:T(8,128)S(1)} collective-permute-done((f32[12,128]{1,0:T(8,128)S(1)}, f32[12,128]{1,0:T(8,128)S(1)}, u32[]{:S(2)}, u32[]{:S(2)}) %collective-permute-start.25) | collective-permute-done | bytes 6176 | tf_op jit(solution)/shard_map/ppermute | solution.py:20
  83.1 2.4 %collective-permute-done.26 = f32[12,128]{1,0:T(8,128)S(1)} collective-permute-done((f32[12,128]{1,0:T(8,128)S(1)}, f32[12,128]{1,0:T(8,128)S(1)}, u32[]{:S(2)}, u32[]{:S(2)}) %collective-permute-start.26) | collective-permute-done | bytes 6176 | tf_op jit(solution)/shard_map/ppermute | solution.py:20
  86.4 1.2 %collective-permute-done.27 = f32[2,4,128]{2,1,0:T(4,128)S(1)} collective-permute-done((f32[2,4,128]{2,1,0:T(4,128)S(1)}, f32[2,4,128]{2,1,0:T(4,128)S(1)}, u32[]{:S(2)}, u32[]{:S(2)}) %collective-permute-start.27) | collective-permute-done | bytes 4128 | tf_op jit(solution)/shard_map/ppermute | solution.py:20
  87.5 2.1 %collective-permute-start.28 = (f32[2,4,128]{2,1,0:T(4,128)S(1)}, f32[2,4,128]{2,1,0:T(4,128)S(1)}, u32[]{:S(2)}, u32[]{:S(2)}) collective-permute-start(f32[2,4,128]{2,1,0:T(4,128)S(1)} %pad_maximum_fusion.4), channel_id=1, source_target_pairs={{0,2},{2,0},{1,3},{3,1},{4,6},{6,4},{5,7},{7,5},{8,10},{10,8},{9,1... | collective-permute-start | bytes 12296 | tf_op jit(solution)/shard_map/ppermute | solution.py:20
  89.6 1.6 %collective-permute-done.28 = f32[2,4,128]{2,1,0:T(4,128)S(1)} collective-permute-done((f32[2,4,128]{2,1,0:T(4,128)S(1)}, f32[2,4,128]{2,1,0:T(4,128)S(1)}, u32[]{:S(2)}, u32[]{:S(2)}) %collective-permute-start.28) | collective-permute-done | bytes 4128 | tf_op jit(solution)/shard_map/ppermute | solution.py:20
  92.8 0.9 shard_map.76
  94.5 2.1 %collective-permute-start.30 = (f16[128,768]{1,0:T(8,128)(2,1)S(1)}, f16[128,768]{1,0:T(8,128)(2,1)S(1)}, u32[]{:S(2)}, u32[]{:S(2)}) collective-permute-start(f16[128,768]{1,0:T(8,128)(2,1)S(1)} %fusion.1), channel_id=1, source_target_pairs={{0,2},{2,0},{1,3},{3,1},{4,6},{6,4},{5,7},{7,5},{8,10},{10,8},{9,1... | collective-permute-start | bytes 589832 | tf_op jit(solution)/shard_map/ppermute | solution.py:20
  97.2 4.6 %collective-permute-done.30 = f16[128,768]{1,0:T(8,128)(2,1)S(1)} collective-permute-done((f16[128,768]{1,0:T(8,128)(2,1)S(1)}, f16[128,768]{1,0:T(8,128)(2,1)S(1)}, u32[]{:S(2)}, u32[]{:S(2)}) %collective-permute-start.30) | collective-permute-done | bytes 196640 | tf_op jit(solution)/shard_map/ppermute | solution.py:20
  (77 shorter events, 10.5 us)
Async XLA Ops:
  0.6 11.0 %copy-start = (bf16[192,768]{1,0:T(8,128)(2,1)S(1)}, bf16[192,768]{1,0:T(8,128)(2,1)}, u32[]{:S(2)}) copy-start(bf16[192,768]{1,0:T(8,128)(2,1)} %param.5) | copy-start | bytes 884740
  0.6 16.2 %collective-permute-start.1 = (bf16[192,768]{1,0:T(8,128)(2,1)}, bf16[192,768]{1,0:T(8,128)(2,1)S(1)}, u32[]{:S(2)}, u32[]{:S(2)}) collective-permute-start(bf16[192,768]{1,0:T(8,128)(2,1)} %param.5), channel_id=1, source_target_pairs={{0,8},{8,0},{16,24},{24,16},{1,9},{9,1},{17,25},{25,17},{2,10},{10... | collective-permute-start | bytes 884744 | tf_op jit(solution)/shard_map/ppermute | solution.py:20
  3.6 16.4 %collective-permute-start.8 = (bf16[192,768]{1,0:T(8,128)(2,1)}, bf16[192,768]{1,0:T(8,128)(2,1)S(1)}, u32[]{:S(2)}, u32[]{:S(2)}) collective-permute-start(bf16[192,768]{1,0:T(8,128)(2,1)} %param.5), channel_id=1, source_target_pairs={{0,4},{4,0},{1,5},{5,1},{2,6},{6,2},{3,7},{7,3},{8,12},{12,8},{9,1... | collective-permute-start | bytes 884744 | tf_op jit(solution)/shard_map/ppermute | solution.py:20
  6.2 19.2 %collective-permute-start.6 = (bf16[192,768]{1,0:T(8,128)(2,1)}, bf16[192,768]{1,0:T(8,128)(2,1)S(1)}, u32[]{:S(2)}, u32[]{:S(2)}) collective-permute-start(bf16[192,768]{1,0:T(8,128)(2,1)} %param.5), channel_id=1, source_target_pairs={{0,16},{8,24},{16,0},{24,8},{1,17},{9,25},{17,1},{25,9},{2,18},{10... | collective-permute-start | bytes 884744 | tf_op jit(solution)/shard_map/ppermute | solution.py:20
  7.8 19.3 %collective-permute-start.7 = (bf16[192,768]{1,0:T(8,128)(2,1)}, bf16[192,768]{1,0:T(8,128)(2,1)S(1)}, u32[]{:S(2)}, u32[]{:S(2)}) collective-permute-start(bf16[192,768]{1,0:T(8,128)(2,1)} %param.5), channel_id=1, source_target_pairs={{0,24},{8,16},{16,8},{24,0},{1,25},{9,17},{17,9},{25,1},{2,26},{10... | collective-permute-start | bytes 884744 | tf_op jit(solution)/shard_map/ppermute | solution.py:20
  8.2 8.6 %collective-permute-start = (bf16[128,768]{1,0:T(8,128)(2,1)}, bf16[128,768]{1,0:T(8,128)(2,1)S(1)}, u32[]{:S(2)}, u32[]{:S(2)}) collective-permute-start(bf16[128,768]{1,0:T(8,128)(2,1)} %param.4), channel_id=1, source_target_pairs={{0,2},{2,0},{1,3},{3,1},{4,6},{6,4},{5,7},{7,5},{8,10},{10,8},{9,1... | collective-permute-start | bytes 589832 | tf_op jit(solution)/shard_map/ppermute | solution.py:20
  10.5 1.1 %copy-start.2 = (f32[768]{0:T(1024)S(1)}, f32[768]{0:T(1024)}, u32[]{:S(2)}) copy-start(f32[768]{0:T(1024)} %param.7) | copy-start | bytes 9220
  11.5 5.3 %copy-start.1 = (bf16[128,768]{1,0:T(8,128)(2,1)S(1)}, bf16[128,768]{1,0:T(8,128)(2,1)}, u32[]{:S(2)}) copy-start(bf16[128,768]{1,0:T(8,128)(2,1)} %param.4) | copy-start | bytes 589828
  16.8 11.3 %collective-permute-start.2 = (bf16[128,768]{1,0:T(8,128)(2,1)S(1)}, bf16[128,768]{1,0:T(8,128)(2,1)S(1)}, u32[]{:S(2)}, u32[]{:S(2)}) collective-permute-start(bf16[128,768]{1,0:T(8,128)(2,1)S(1)} %copy-done.1), channel_id=1, source_target_pairs={{0,4},{4,0},{1,5},{5,1},{2,6},{6,2},{3,7},{7,3},{8,12},{12,8},{9,1... | collective-permute-start | bytes 589832 | tf_op jit(solution)/shard_map/ppermute | solution.py:20
  19.2 14.7 %collective-permute-start.4 = (f32[768]{0:T(1024)S(1)}, f32[768]{0:T(1024)S(1)}, u32[]{:S(2)}, u32[]{:S(2)}) collective-permute-start(f32[768]{0:T(1024)S(1)} %copy-done.2), channel_id=1, source_target_pairs={{0,4},{4,0},{1,5},{5,1},{2,6},{6,2},{3,7},{7,3},{8,12},{12,8},{9,1... | collective-permute-start | bytes 9224 | tf_op jit(solution)/shard_map/ppermute | solution.py:20
  20.0 14.0 %collective-permute-start.9 = (bf16[192,768]{1,0:T(8,128)(2,1)S(1)}, bf16[192,768]{1,0:T(8,128)(2,1)S(1)}, u32[]{:S(2)}, u32[]{:S(2)}) collective-permute-start(bf16[192,768]{1,0:T(8,128)(2,1)S(1)} %collective-permute-done.8), channel_id=1, source_target_pairs={{0,8},{8,0},{16,24},{24,16},{1,9},{9,1},{17,25},{25,17},{2,10},{10... | collective-permute-start | bytes 884744 | tf_op jit(solution)/shard_map/ppermute | solution.py:20
  25.4 9.9 %collective-permute-start.10 = (bf16[192,768]{1,0:T(8,128)(2,1)S(1)}, bf16[192,768]{1,0:T(8,128)(2,1)S(1)}, u32[]{:S(2)}, u32[]{:S(2)}) collective-permute-start(bf16[192,768]{1,0:T(8,128)(2,1)S(1)} %collective-permute-done.8), channel_id=1, source_target_pairs={{0,16},{8,24},{16,0},{24,8},{1,17},{9,25},{17,1},{25,9},{2,18},{10... | collective-permute-start | bytes 884744 | tf_op jit(solution)/shard_map/ppermute | solution.py:20
  27.0 8.4 %collective-permute-start.11 = (bf16[192,768]{1,0:T(8,128)(2,1)S(1)}, bf16[192,768]{1,0:T(8,128)(2,1)S(1)}, u32[]{:S(2)}, u32[]{:S(2)}) collective-permute-start(bf16[192,768]{1,0:T(8,128)(2,1)S(1)} %collective-permute-done.8), channel_id=1, source_target_pairs={{0,24},{8,16},{16,8},{24,0},{1,25},{9,17},{17,9},{25,1},{2,26},{10... | collective-permute-start | bytes 884744 | tf_op jit(solution)/shard_map/ppermute | solution.py:20
  28.1 5.7 %collective-permute-start.3 = (bf16[128,768]{1,0:T(8,128)(2,1)S(1)}, bf16[128,768]{1,0:T(8,128)(2,1)S(1)}, u32[]{:S(2)}, u32[]{:S(2)}) collective-permute-start(bf16[128,768]{1,0:T(8,128)(2,1)S(1)} %collective-permute-done.2), channel_id=1, source_target_pairs={{0,2},{2,0},{1,3},{3,1},{4,6},{6,4},{5,7},{7,5},{8,10},{10,8},{9,1... | collective-permute-start | bytes 589832 | tf_op jit(solution)/shard_map/ppermute | solution.py:20
  33.9 2.4 %collective-permute-start.5 = (bf16[2,2,128,768]{3,2,1,0:T(8,128)(2,1)S(1)}, bf16[2,2,128,768]{3,2,1,0:T(8,128)(2,1)S(1)}, u32[]{:S(2)}, u32[]{:S(2)}) collective-permute-start(bf16[2,2,128,768]{3,2,1,0:T(8,128)(2,1)S(1)} %pad_maximum_fusion), channel_id=1, source_target_pairs={{0,1},{1,0},{2,3},{3,2},{4,5},{5,4},{6,7},{7,6},{8,9},{9,8},{10,11... | collective-permute-start | bytes 2359304 | tf_op jit(solution)/shard_map/ppermute | solution.py:20
  40.5 1.2 %collective-permute-start.12 = (f32[8,128]{1,0:T(8,128)S(1)}, f32[8,128]{1,0:T(8,128)S(1)}, u32[]{:S(2)}, u32[]{:S(2)}) collective-permute-start(f32[8,128]{1,0:T(8,128)S(1)} %shard_map.69), channel_id=1, source_target_pairs={{0,1},{1,0},{2,3},{3,2},{4,5},{5,4},{6,7},{7,6},{8,9},{9,8},{10,11... | collective-permute-start | bytes 12296 | tf_op jit(solution)/shard_map/ppermute | solution.py:20
  41.8 6.3 %collective-permute-start.13 = (f32[8,128]{1,0:T(8,128)S(1)}, f32[8,128]{1,0:T(8,128)S(1)}, u32[]{:S(2)}, u32[]{:S(2)}) collective-permute-start(f32[8,128]{1,0:T(8,128)S(1)} %multiply_add_fusion.2), channel_id=1, source_target_pairs={{0,2},{2,0},{1,3},{3,1},{4,6},{6,4},{5,7},{7,5},{8,10},{10,8},{9,1... | collective-permute-start | bytes 12296 | tf_op jit(solution)/shard_map/ppermute | solution.py:20
  49.5 3.7 %collective-permute-start.14 = (f32[12,128]{1,0:T(8,128)S(1)}, f32[12,128]{1,0:T(8,128)S(1)}, u32[]{:S(2)}, u32[]{:S(2)}) collective-permute-start(f32[12,128]{1,0:T(8,128)S(1)} %shard_map.70), channel_id=1, source_target_pairs={{0,8},{8,0},{16,24},{24,16},{1,9},{9,1},{17,25},{25,17},{2,10},{10... | collective-permute-start | bytes 18440 | tf_op jit(solution)/shard_map/ppermute | solution.py:20
  50.6 3.7 %collective-permute-start.15 = (f32[12,128]{1,0:T(8,128)S(1)}, f32[12,128]{1,0:T(8,128)S(1)}, u32[]{:S(2)}, u32[]{:S(2)}) collective-permute-start(f32[12,128]{1,0:T(8,128)S(1)} %shard_map.70), channel_id=1, source_target_pairs={{0,16},{8,24},{16,0},{24,8},{1,17},{9,25},{17,1},{25,9},{2,18},{10... | collective-permute-start | bytes 18440 | tf_op jit(solution)/shard_map/ppermute | solution.py:20
  52.1 4.5 %collective-permute-start.16 = (f32[12,128]{1,0:T(8,128)S(1)}, f32[12,128]{1,0:T(8,128)S(1)}, u32[]{:S(2)}, u32[]{:S(2)}) collective-permute-start(f32[12,128]{1,0:T(8,128)S(1)} %shard_map.70), channel_id=1, source_target_pairs={{0,24},{8,16},{16,8},{24,0},{1,25},{9,17},{17,9},{25,1},{2,26},{10... | collective-permute-start | bytes 18440 | tf_op jit(solution)/shard_map/ppermute | solution.py:20
  58.0 1.2 %collective-permute-start.17 = (f32[8,128]{1,0:T(8,128)S(1)}, f32[8,128]{1,0:T(8,128)S(1)}, u32[]{:S(2)}, u32[]{:S(2)}) collective-permute-start(f32[8,128]{1,0:T(8,128)S(1)} %shard_map.71), channel_id=1, source_target_pairs={{0,1},{1,0},{2,3},{3,2},{4,5},{5,4},{6,7},{7,6},{8,9},{9,8},{10,11... | collective-permute-start | bytes 12296 | tf_op jit(solution)/shard_map/ppermute | solution.py:20
  59.3 3.7 %collective-permute-start.18 = (f32[8,128]{1,0:T(8,128)S(1)}, f32[8,128]{1,0:T(8,128)S(1)}, u32[]{:S(2)}, u32[]{:S(2)}) collective-permute-start(f32[8,128]{1,0:T(8,128)S(1)} %multiply_add_fusion.1), channel_id=1, source_target_pairs={{0,2},{2,0},{1,3},{3,1},{4,6},{6,4},{5,7},{7,5},{8,10},{10,8},{9,1... | collective-permute-start | bytes 12296 | tf_op jit(solution)/shard_map/ppermute | solution.py:20
  64.4 3.7 %collective-permute-start.19 = (f32[12,128]{1,0:T(8,128)S(1)}, f32[12,128]{1,0:T(8,128)S(1)}, u32[]{:S(2)}, u32[]{:S(2)}) collective-permute-start(f32[12,128]{1,0:T(8,128)S(1)} %shard_map.72), channel_id=1, source_target_pairs={{0,8},{8,0},{16,24},{24,16},{1,9},{9,1},{17,25},{25,17},{2,10},{10... | collective-permute-start | bytes 18440 | tf_op jit(solution)/shard_map/ppermute | solution.py:20
  64.7 3.7 %collective-permute-start.20 = (f32[12,128]{1,0:T(8,128)S(1)}, f32[12,128]{1,0:T(8,128)S(1)}, u32[]{:S(2)}, u32[]{:S(2)}) collective-permute-start(f32[12,128]{1,0:T(8,128)S(1)} %shard_map.72), channel_id=1, source_target_pairs={{0,16},{8,24},{16,0},{24,8},{1,17},{9,25},{17,1},{25,9},{2,18},{10... | collective-permute-start | bytes 18440 | tf_op jit(solution)/shard_map/ppermute | solution.py:20
  65.9 4.5 %collective-permute-start.21 = (f32[12,128]{1,0:T(8,128)S(1)}, f32[12,128]{1,0:T(8,128)S(1)}, u32[]{:S(2)}, u32[]{:S(2)}) collective-permute-start(f32[12,128]{1,0:T(8,128)S(1)} %shard_map.72), channel_id=1, source_target_pairs={{0,24},{8,16},{16,8},{24,0},{1,25},{9,17},{17,9},{25,1},{2,26},{10... | collective-permute-start | bytes 18440 | tf_op jit(solution)/shard_map/ppermute | solution.py:20
  71.8 1.2 %collective-permute-start.22 = (f32[8,128]{1,0:T(8,128)S(1)}, f32[8,128]{1,0:T(8,128)S(1)}, u32[]{:S(2)}, u32[]{:S(2)}) collective-permute-start(f32[8,128]{1,0:T(8,128)S(1)} %shard_map.73), channel_id=1, source_target_pairs={{0,1},{1,0},{2,3},{3,2},{4,5},{5,4},{6,7},{7,6},{8,9},{9,8},{10,11... | collective-permute-start | bytes 12296 | tf_op jit(solution)/shard_map/ppermute | solution.py:20
  73.1 3.7 %collective-permute-start.23 = (f32[8,128]{1,0:T(8,128)S(1)}, f32[8,128]{1,0:T(8,128)S(1)}, u32[]{:S(2)}, u32[]{:S(2)}) collective-permute-start(f32[8,128]{1,0:T(8,128)S(1)} %multiply_add_fusion), channel_id=1, source_target_pairs={{0,2},{2,0},{1,3},{3,1},{4,6},{6,4},{5,7},{7,5},{8,10},{10,8},{9,1... | collective-permute-start | bytes 12296 | tf_op jit(solution)/shard_map/ppermute | solution.py:20
  78.4 3.7 %collective-permute-start.24 = (f32[12,128]{1,0:T(8,128)S(1)}, f32[12,128]{1,0:T(8,128)S(1)}, u32[]{:S(2)}, u32[]{:S(2)}) collective-permute-start(f32[12,128]{1,0:T(8,128)S(1)} %shard_map.74), channel_id=1, source_target_pairs={{0,8},{8,0},{16,24},{24,16},{1,9},{9,1},{17,25},{25,17},{2,10},{10... | collective-permute-start | bytes 18440 | tf_op jit(solution)/shard_map/ppermute | solution.py:20
  79.5 3.7 %collective-permute-start.25 = (f32[12,128]{1,0:T(8,128)S(1)}, f32[12,128]{1,0:T(8,128)S(1)}, u32[]{:S(2)}, u32[]{:S(2)}) collective-permute-start(f32[12,128]{1,0:T(8,128)S(1)} %shard_map.74), channel_id=1, source_target_pairs={{0,16},{8,24},{16,0},{24,8},{1,17},{9,25},{17,1},{25,9},{2,18},{10... | collective-permute-start | bytes 18440 | tf_op jit(solution)/shard_map/ppermute | solution.py:20
  81.0 4.5 %collective-permute-start.26 = (f32[12,128]{1,0:T(8,128)S(1)}, f32[12,128]{1,0:T(8,128)S(1)}, u32[]{:S(2)}, u32[]{:S(2)}) collective-permute-start(f32[12,128]{1,0:T(8,128)S(1)} %shard_map.74), channel_id=1, source_target_pairs={{0,24},{8,16},{16,8},{24,0},{1,25},{9,17},{17,9},{25,1},{2,26},{10... | collective-permute-start | bytes 18440 | tf_op jit(solution)/shard_map/ppermute | solution.py:20
  86.3 1.2 %collective-permute-start.27 = (f32[2,4,128]{2,1,0:T(4,128)S(1)}, f32[2,4,128]{2,1,0:T(4,128)S(1)}, u32[]{:S(2)}, u32[]{:S(2)}) collective-permute-start(f32[2,4,128]{2,1,0:T(4,128)S(1)} %pad_maximum_fusion.3), channel_id=1, source_target_pairs={{0,1},{1,0},{2,3},{3,2},{4,5},{5,4},{6,7},{7,6},{8,9},{9,8},{10,11... | collective-permute-start | bytes 12296 | tf_op jit(solution)/shard_map/ppermute | solution.py:20
  87.5 3.7 %collective-permute-start.28 = (f32[2,4,128]{2,1,0:T(4,128)S(1)}, f32[2,4,128]{2,1,0:T(4,128)S(1)}, u32[]{:S(2)}, u32[]{:S(2)}) collective-permute-start(f32[2,4,128]{2,1,0:T(4,128)S(1)} %pad_maximum_fusion.4), channel_id=1, source_target_pairs={{0,2},{2,0},{1,3},{3,1},{4,6},{6,4},{5,7},{7,5},{8,10},{10,8},{9,1... | collective-permute-start | bytes 12296 | tf_op jit(solution)/shard_map/ppermute | solution.py:20
  92.1 2.4 %collective-permute-start.29 = (f32[256,768]{1,0:T(8,128)S(1)}, f32[256,768]{1,0:T(8,128)S(1)}, u32[]{:S(2)}, u32[]{:S(2)}) collective-permute-start(f32[256,768]{1,0:T(8,128)S(1)} %shard_map.77), channel_id=1, source_target_pairs={{0,1},{1,0},{2,3},{3,2},{4,5},{5,4},{6,7},{7,6},{8,9},{9,8},{10,11... | collective-permute-start | bytes 2359304 | tf_op jit(solution)/shard_map/ppermute | solution.py:20
  94.5 7.3 %collective-permute-start.30 = (f16[128,768]{1,0:T(8,128)(2,1)S(1)}, f16[128,768]{1,0:T(8,128)(2,1)S(1)}, u32[]{:S(2)}, u32[]{:S(2)}) collective-permute-start(f16[128,768]{1,0:T(8,128)(2,1)S(1)} %fusion.1), channel_id=1, source_target_pairs={{0,2},{2,0},{1,3},{3,1},{4,6},{6,4},{5,7},{7,5},{8,10},{10,8},{9,1... | collective-permute-start | bytes 589832 | tf_op jit(solution)/shard_map/ppermute | solution.py:20

commit v5 on v4

--- a/solution.py
+++ b/solution.py
@@ -193,12 +193,11 @@
     tool_side = jnp.zeros_like(log_tool)
     for sweep in range(ITERS):
         (part,) = row_pass(tiles, tool_side, log_query.size)
-        part = lse_of(swaps(part, "core"))
-        query_side = log_query - lse_of(swaps(part, "zl"))
+        query_side = log_query - lse_of(swaps(part, ("zl", "core")))
         tool_side = log_tool - lse_of(swaps(col_pass(tiles, query_side), "row"))
 
     ends = jnp.stack(row_pass(tiles, tool_side, log_query.size // 2, True))
-    for axis in ("core", "zl"):
+    for axis in (("zl", "core"),):
         got = swaps(ends, axis)
         ends = jnp.stack([lse_of([g[0] for g in got]), functools.reduce(jnp.maximum, [g[1] for g in got])])
     lse, peak = ends
@@ -210,6 +209,7 @@
 
     others = swap(mapped_rows(firsts[1]), "core", 1).reshape(nl, bq, features)
     own = mapped_rows(firsts[0]).reshape(nl, bq, features)
+    own, query_side, tool_side = lax.optimization_barrier((own, query_side, tool_side))
     summed = [pick(own, li ^ k, 0) + pick(others, li ^ k, 0) for k in range(nl)]
     summed = sum([summed[0]] + [swap(summed[k].astype(jnp.float16), "zl", k).astype(jnp.float32) for k in range(1, nl)])
     mapped = summed.astype(jnp.bfloat16)

time: 103 us -> 100 us (0.971)
  waiting for transfers between devices: 39.1 us -> 37.1 us
  starting transfers between devices: 44 us -> 42.8 us
    ppermute x31 -> x35, waiting for transfers between devices: 39.1 us -> 37.1 us  [swap(): return lax.ppermute(x, axes, [(i, i ^ k) for i in range(n)])]
    ppermute x31 -> x35, starting transfers between devices: 44 us -> 42.8 us  [swap(): return lax.ppermute(x, axes, [(i, i ^ k) for i in range(n)])]
  transfers between devices with their start and end apart: 31 -> 35, of which waited for: 25 -> 23; matrix products, arithmetic and copies ran while one was open for 3% -> 4% of each run, Pallas kernels for 1% -> 1%
where the time goes in v5:
time: 100 us
  starting transfers between devices  42.8 us (43%)
  waiting for transfers between devices  37.1 us (37%)
  Pallas kernels  13.7 us (14%)
  other arithmetic  3.11 us (3%)
  local copies, waits for them, and re-layouts  2.21 us (2%)
  between operations  1.03 us (1%)
    ppermute x35, starting transfers between devices, swap(): return lax.ppermute(x, axes, [(i, i ^ k) for i in range(n)])  42.8 us
    ppermute x35, waiting for transfers between devices, swap(): return lax.ppermute(x, axes, [(i, i ^ k) for i in range(n)])  37.1 us
    pallas_call x11, Pallas kernels, call(): pl.pallas_call(kernel, out_shape=out_shape, in_specs=[vmem] * (len(args)...  13.7 us
  transfers between devices with their start and end apart: 35, of which 23 were waited for; matrix products, arithmetic and copies ran while one was open for 4% of the time, Pallas kernels for 1%

profile of v5, /device:TPU:0, one launch (start us, length us, event | category | flops | bytes accessed | tf_op | source)
XLA Modules:
  0.0 100.0 jit_solution(5574181592508965317)
XLA Ops:
  0.6 3.0 %collective-permute-start.1 = (bf16[192,768]{1,0:T(8,128)(2,1)}, bf16[192,768]{1,0:T(8,128)(2,1)S(1)}, u32[]{:S(2)}, u32[]{:S(2)}) collective-permute-start(bf16[192,768]{1,0:T(8,128)(2,1)} %param.5), channel_id=1, source_target_pairs={{0,8},{8,0},{16,24},{24,16},{1,9},{9,1},{17,25},{25,17},{2,10},{10... | collective-permute-start | bytes 884744 | tf_op jit(solution)/shard_map/ppermute | solution.py:20
  3.6 2.6 %collective-permute-start.8 = (bf16[192,768]{1,0:T(8,128)(2,1)}, bf16[192,768]{1,0:T(8,128)(2,1)S(1)}, u32[]{:S(2)}, u32[]{:S(2)}) collective-permute-start(bf16[192,768]{1,0:T(8,128)(2,1)} %param.5), channel_id=1, source_target_pairs={{0,4},{4,0},{1,5},{5,1},{2,6},{6,2},{3,7},{7,3},{8,12},{12,8},{9,1... | collective-permute-start | bytes 884744 | tf_op jit(solution)/shard_map/ppermute | solution.py:20
  6.2 1.5 %collective-permute-start.6 = (bf16[192,768]{1,0:T(8,128)(2,1)}, bf16[192,768]{1,0:T(8,128)(2,1)S(1)}, u32[]{:S(2)}, u32[]{:S(2)}) collective-permute-start(bf16[192,768]{1,0:T(8,128)(2,1)} %param.5), channel_id=1, source_target_pairs={{0,16},{8,24},{16,0},{24,8},{1,17},{9,25},{17,1},{25,9},{2,18},{10... | collective-permute-start | bytes 884744 | tf_op jit(solution)/shard_map/ppermute | solution.py:20
  8.2 1.6 %collective-permute-start = (bf16[128,768]{1,0:T(8,128)(2,1)}, bf16[128,768]{1,0:T(8,128)(2,1)S(1)}, u32[]{:S(2)}, u32[]{:S(2)}) collective-permute-start(bf16[128,768]{1,0:T(8,128)(2,1)} %param.4), channel_id=1, source_target_pairs={{0,2},{2,0},{1,3},{3,1},{4,6},{6,4},{5,7},{7,5},{8,10},{10,8},{9,1... | collective-permute-start | bytes 589832 | tf_op jit(solution)/shard_map/ppermute | solution.py:20
  11.2 0.9 bitcast_dynamic-update-slice_fusion.13
  12.4 4.4 %collective-permute-done = bf16[128,768]{1,0:T(8,128)(2,1)S(1)} collective-permute-done((bf16[128,768]{1,0:T(8,128)(2,1)}, bf16[128,768]{1,0:T(8,128)(2,1)S(1)}, u32[]{:S(2)}, u32[]{:S(2)}) %collective-permute-start) | collective-permute-done | bytes 196640 | tf_op jit(solution)/shard_map/ppermute | solution.py:20
  16.8 2.3 %collective-permute-start.2 = (bf16[128,768]{1,0:T(8,128)(2,1)S(1)}, bf16[128,768]{1,0:T(8,128)(2,1)S(1)}, u32[]{:S(2)}, u32[]{:S(2)}) collective-permute-start(bf16[128,768]{1,0:T(8,128)(2,1)S(1)} %copy-done.1), channel_id=1, source_target_pairs={{0,4},{4,0},{1,5},{5,1},{2,6},{6,2},{3,7},{7,3},{8,12},{12,8},{9,1... | collective-permute-start | bytes 589832 | tf_op jit(solution)/shard_map/ppermute | solution.py:20
  20.0 5.3 %collective-permute-start.9 = (bf16[192,768]{1,0:T(8,128)(2,1)S(1)}, bf16[192,768]{1,0:T(8,128)(2,1)S(1)}, u32[]{:S(2)}, u32[]{:S(2)}) collective-permute-start(bf16[192,768]{1,0:T(8,128)(2,1)S(1)} %collective-permute-done.8), channel_id=1, source_target_pairs={{0,8},{8,0},{16,24},{24,16},{1,9},{9,1},{17,25},{25,17},{2,10},{10... | collective-permute-start | bytes 884744 | tf_op jit(solution)/shard_map/ppermute | solution.py:20
  25.4 1.6 %collective-permute-start.10 = (bf16[192,768]{1,0:T(8,128)(2,1)S(1)}, bf16[192,768]{1,0:T(8,128)(2,1)S(1)}, u32[]{:S(2)}, u32[]{:S(2)}) collective-permute-start(bf16[192,768]{1,0:T(8,128)(2,1)S(1)} %collective-permute-done.8), channel_id=1, source_target_pairs={{0,16},{8,24},{16,0},{24,8},{1,17},{9,25},{17,1},{25,9},{2,18},{10... | collective-permute-start | bytes 884744 | tf_op jit(solution)/shard_map/ppermute | solution.py:20
  27.2 1.0 collective-permute-done.2
  28.9 4.9 %collective-permute-done.3 = bf16[128,768]{1,0:T(8,128)(2,1)S(1)} collective-permute-done((bf16[128,768]{1,0:T(8,128)(2,1)S(1)}, bf16[128,768]{1,0:T(8,128)(2,1)S(1)}, u32[]{:S(2)}, u32[]{:S(2)}) %collective-permute-start.3) | collective-permute-done | bytes 196640 | tf_op jit(solution)/shard_map/ppermute | solution.py:20
  34.0 1.3 %collective-permute-done.10 = bf16[192,768]{1,0:T(8,128)(2,1)S(1)} collective-permute-done((bf16[192,768]{1,0:T(8,128)(2,1)S(1)}, bf16[192,768]{1,0:T(8,128)(2,1)S(1)}, u32[]{:S(2)}, u32[]{:S(2)}) %collective-permute-start.10) | collective-permute-done | bytes 294944 | tf_op jit(solution)/shard_map/ppermute | solution.py:20
  36.3 1.4 %shard_map.68.refs_1_.tile1 = f32[1024,768]{1,0:T(8,128)S(1)} custom-call(bf16[1024,768]{1,0:T(8,128)(2,1)S(1)} %bitcast.96, bf16[768,768]{1,0:T(8,128)(2,1)S(1)} %bitcast.90), custom_call_target="tpu_custom_call" | custom-call | flops 1207959552 | bytes 5505024 | tf_op jit(solution)/shard_map/pallas_call | solution.py:122
  37.8 1.4 %shard_map.67.refs_0_.tile0 = f32[1024,768]{1,0:T(8,128)S(1)} custom-call(bf16[1024,768]{1,0:T(8,128)(2,1)S(1)} %bitcast.97, bf16[768,768]{1,0:T(8,128)(2,1)S(1)} %bitcast.93), custom_call_target="tpu_custom_call" | custom-call | flops 1207959552 | bytes 5505024 | tf_op jit(solution)/shard_map/pallas_call | solution.py:122
  39.2 1.3 %shard_map.69 = f32[8,128]{1,0:T(8,128)S(1)} custom-call(f32[1024,768]{1,0:T(8,128)S(1)} %shard_map.67.refs_0_.tile0, f32[1024,768]{1,0:T(8,128)S(1)} %shard_map.68.refs_1_.tile1, f32[12,128]{1,0:T(8,128)S(1)} %broadcast_in_dim.68.refs_2_), custom_call_target="tpu_custom_call" | custom-call | flops 9446400 | bytes 6297600 | tf_op jit(solution)/shard_map/pallas_call | solution.py:122
  40.7 4.6 %collective-permute-start.13 = (f32[8,128]{1,0:T(8,128)S(1)}, f32[8,128]{1,0:T(8,128)S(1)}, u32[]{:S(2)}, u32[]{:S(2)}) collective-permute-start(f32[8,128]{1,0:T(8,128)S(1)} %shard_map.69), channel_id=1, source_target_pairs={{0,2},{1,3},{2,0},{3,1},{4,6},{5,7},{6,4},{7,5},{8,10},{9,11},{10,... | collective-permute-start | bytes 12296 | tf_op jit(solution)/shard_map/ppermute | solution.py:20
  45.4 1.5 %collective-permute-done.13 = f32[8,128]{1,0:T(8,128)S(1)} collective-permute-done((f32[8,128]{1,0:T(8,128)S(1)}, f32[8,128]{1,0:T(8,128)S(1)}, u32[]{:S(2)}, u32[]{:S(2)}) %collective-permute-start.13) | collective-permute-done | bytes 4128 | tf_op jit(solution)/shard_map/ppermute | solution.py:20
  46.9 1.4 %collective-permute-done.14 = f32[8,128]{1,0:T(8,128)S(1)} collective-permute-done((f32[8,128]{1,0:T(8,128)S(1)}, f32[8,128]{1,0:T(8,128)S(1)}, u32[]{:S(2)}, u32[]{:S(2)}) %collective-permute-start.14) | collective-permute-done | bytes 4128 | tf_op jit(solution)/shard_map/ppermute | solution.py:20
  48.4 1.4 %shard_map.70 = f32[12,128]{1,0:T(8,128)S(1)} custom-call(f32[1024,768]{1,0:T(8,128)S(1)} %shard_map.67.refs_0_.tile0, f32[1024,768]{1,0:T(8,128)S(1)} %shard_map.68.refs_1_.tile1, f32[8,128]{1,0:T(8,128)S(1)} %add_subtract_fusion.5.refs_2_), custom_call_target="tpu_custom_call" | custom-call | flops 9443328 | bytes 6295552 | tf_op jit(solution)/shard_map/pallas_call | solution.py:122
  49.8 1.1 %collective-permute-start.15 = (f32[12,128]{1,0:T(8,128)S(1)}, f32[12,128]{1,0:T(8,128)S(1)}, u32[]{:S(2)}, u32[]{:S(2)}) collective-permute-start(f32[12,128]{1,0:T(8,128)S(1)} %shard_map.70), channel_id=1, source_target_pairs={{0,8},{8,0},{16,24},{24,16},{1,9},{9,1},{17,25},{25,17},{2,10},{10... | collective-permute-start | bytes 18440 | tf_op jit(solution)/shard_map/ppermute | solution.py:20
  50.9 1.5 %collective-permute-start.16 = (f32[12,128]{1,0:T(8,128)S(1)}, f32[12,128]{1,0:T(8,128)S(1)}, u32[]{:S(2)}, u32[]{:S(2)}) collective-permute-start(f32[12,128]{1,0:T(8,128)S(1)} %shard_map.70), channel_id=1, source_target_pairs={{0,16},{8,24},{16,0},{24,8},{1,17},{9,25},{17,1},{25,9},{2,18},{10... | collective-permute-start | bytes 18440 | tf_op jit(solution)/shard_map/ppermute | solution.py:20
  52.4 0.9 collective-permute-start.17
  53.5 1.0 %collective-permute-done.16 = f32[12,128]{1,0:T(8,128)S(1)} collective-permute-done((f32[12,128]{1,0:T(8,128)S(1)}, f32[12,128]{1,0:T(8,128)S(1)}, u32[]{:S(2)}, u32[]{:S(2)}) %collective-permute-start.16) | collective-permute-done | bytes 6176 | tf_op jit(solution)/shard_map/ppermute | solution.py:20
  54.5 2.4 %collective-permute-done.17 = f32[12,128]{1,0:T(8,128)S(1)} collective-permute-done((f32[12,128]{1,0:T(8,128)S(1)}, f32[12,128]{1,0:T(8,128)S(1)}, u32[]{:S(2)}, u32[]{:S(2)}) %collective-permute-start.17) | collective-permute-done | bytes 6176 | tf_op jit(solution)/shard_map/ppermute | solution.py:20
  57.0 1.3 %shard_map.71 = f32[8,128]{1,0:T(8,128)S(1)} custom-call(f32[1024,768]{1,0:T(8,128)S(1)} %shard_map.67.refs_0_.tile0, f32[1024,768]{1,0:T(8,128)S(1)} %shard_map.68.refs_1_.tile1, f32[12,128]{1,0:T(8,128)S(1)} %add_subtract_fusion.2.refs_2_), custom_call_target="tpu_custom_call" | custom-call | flops 9446400 | bytes 6297600 | tf_op jit(solution)/shard_map/pallas_call | solution.py:122
  59.0 1.2 %collective-permute-start.20 = (f32[8,128]{1,0:T(8,128)S(1)}, f32[8,128]{1,0:T(8,128)S(1)}, u32[]{:S(2)}, u32[]{:S(2)}) collective-permute-start(f32[8,128]{1,0:T(8,128)S(1)} %shard_map.71), channel_id=1, source_target_pairs={{0,3},{1,2},{2,1},{3,0},{4,7},{5,6},{6,5},{7,4},{8,11},{9,10},{10,... | collective-permute-start | bytes 12296 | tf_op jit(solution)/shard_map/ppermute | solution.py:20
  60.2 1.8 %collective-permute-done.19 = f32[8,128]{1,0:T(8,128)S(1)} collective-permute-done((f32[8,128]{1,0:T(8,128)S(1)}, f32[8,128]{1,0:T(8,128)S(1)}, u32[]{:S(2)}, u32[]{:S(2)}) %collective-permute-start.19) | collective-permute-done | bytes 4128 | tf_op jit(solution)/shard_map/ppermute | solution.py:20
  62.1 1.4 %shard_map.72 = f32[12,128]{1,0:T(8,128)S(1)} custom-call(f32[1024,768]{1,0:T(8,128)S(1)} %shard_map.67.refs_0_.tile0, f32[1024,768]{1,0:T(8,128)S(1)} %shard_map.68.refs_1_.tile1, f32[8,128]{1,0:T(8,128)S(1)} %add_subtract_fusion.4.refs_2_), custom_call_target="tpu_custom_call" | custom-call | flops 9443328 | bytes 6295552 | tf_op jit(solution)/shard_map/pallas_call | solution.py:122
  63.9 1.2 %collective-permute-start.22 = (f32[12,128]{1,0:T(8,128)S(1)}, f32[12,128]{1,0:T(8,128)S(1)}, u32[]{:S(2)}, u32[]{:S(2)}) collective-permute-start(f32[12,128]{1,0:T(8,128)S(1)} %shard_map.72), channel_id=1, source_target_pairs={{0,16},{8,24},{16,0},{24,8},{1,17},{9,25},{17,1},{25,9},{2,18},{10... | collective-permute-start | bytes 18440 | tf_op jit(solution)/shard_map/ppermute | solution.py:20
  65.1 2.0 %collective-permute-start.23 = (f32[12,128]{1,0:T(8,128)S(1)}, f32[12,128]{1,0:T(8,128)S(1)}, u32[]{:S(2)}, u32[]{:S(2)}) collective-permute-start(f32[12,128]{1,0:T(8,128)S(1)} %shard_map.72), channel_id=1, source_target_pairs={{0,24},{8,16},{16,8},{24,0},{1,25},{9,17},{17,9},{25,1},{2,26},{10... | collective-permute-start | bytes 18440 | tf_op jit(solution)/shard_map/ppermute | solution.py:20
  67.5 2.1 %collective-permute-done.23 = f32[12,128]{1,0:T(8,128)S(1)} collective-permute-done((f32[12,128]{1,0:T(8,128)S(1)}, f32[12,128]{1,0:T(8,128)S(1)}, u32[]{:S(2)}, u32[]{:S(2)}) %collective-permute-start.23) | collective-permute-done | bytes 6176 | tf_op jit(solution)/shard_map/ppermute | solution.py:20
  69.7 1.3 %shard_map.73 = f32[8,128]{1,0:T(8,128)S(1)} custom-call(f32[1024,768]{1,0:T(8,128)S(1)} %shard_map.67.refs_0_.tile0, f32[1024,768]{1,0:T(8,128)S(1)} %shard_map.68.refs_1_.tile1, f32[12,128]{1,0:T(8,128)S(1)} %add_subtract_fusion.1.refs_2_), custom_call_target="tpu_custom_call" | custom-call | flops 9446400 | bytes 6297600 | tf_op jit(solution)/shard_map/pallas_call | solution.py:122
  71.1 1.5 %collective-permute-start.25 = (f32[8,128]{1,0:T(8,128)S(1)}, f32[8,128]{1,0:T(8,128)S(1)}, u32[]{:S(2)}, u32[]{:S(2)}) collective-permute-start(f32[8,128]{1,0:T(8,128)S(1)} %shard_map.73), channel_id=1, source_target_pairs={{0,2},{1,3},{2,0},{3,1},{4,6},{5,7},{6,4},{7,5},{8,10},{9,11},{10,... | collective-permute-start | bytes 12296 | tf_op jit(solution)/shard_map/ppermute | solution.py:20
  72.9 1.8 %collective-permute-done.25 = f32[8,128]{1,0:T(8,128)S(1)} collective-permute-done((f32[8,128]{1,0:T(8,128)S(1)}, f32[8,128]{1,0:T(8,128)S(1)}, u32[]{:S(2)}, u32[]{:S(2)}) %collective-permute-start.25) | collective-permute-done | bytes 4128 | tf_op jit(solution)/shard_map/ppermute | solution.py:20
  74.7 0.8 collective-permute-done.26
  75.6 1.6 %shard_map.74 = f32[12,128]{1,0:T(8,128)S(1)} custom-call(f32[1024,768]{1,0:T(8,128)S(1)} %shard_map.67.refs_0_.tile0, f32[1024,768]{1,0:T(8,128)S(1)} %shard_map.68.refs_1_.tile1, f32[8,128]{1,0:T(8,128)S(1)} %add_subtract_fusion.3.refs_2_), custom_call_target="tpu_custom_call" | custom-call | flops 9443328 | bytes 6295552 | tf_op jit(solution)/shard_map/pallas_call | solution.py:122
  77.2 1.1 %collective-permute-start.27 = (f32[12,128]{1,0:T(8,128)S(1)}, f32[12,128]{1,0:T(8,128)S(1)}, u32[]{:S(2)}, u32[]{:S(2)}) collective-permute-start(f32[12,128]{1,0:T(8,128)S(1)} %shard_map.74), channel_id=1, source_target_pairs={{0,8},{8,0},{16,24},{24,16},{1,9},{9,1},{17,25},{25,17},{2,10},{10... | collective-permute-start | bytes 18440 | tf_op jit(solution)/shard_map/ppermute | solution.py:20
  78.3 1.5 %collective-permute-start.28 = (f32[12,128]{1,0:T(8,128)S(1)}, f32[12,128]{1,0:T(8,128)S(1)}, u32[]{:S(2)}, u32[]{:S(2)}) collective-permute-start(f32[12,128]{1,0:T(8,128)S(1)} %shard_map.74), channel_id=1, source_target_pairs={{0,16},{8,24},{16,0},{24,8},{1,17},{9,25},{17,1},{25,9},{2,18},{10... | collective-permute-start | bytes 18440 | tf_op jit(solution)/shard_map/ppermute | solution.py:20
  79.8 0.9 collective-permute-start.29
  80.9 1.0 %collective-permute-done.28 = f32[12,128]{1,0:T(8,128)S(1)} collective-permute-done((f32[12,128]{1,0:T(8,128)S(1)}, f32[12,128]{1,0:T(8,128)S(1)}, u32[]{:S(2)}, u32[]{:S(2)}) %collective-permute-start.28) | collective-permute-done | bytes 6176 | tf_op jit(solution)/shard_map/ppermute | solution.py:20
  81.9 2.4 %collective-permute-done.29 = f32[12,128]{1,0:T(8,128)S(1)} collective-permute-done((f32[12,128]{1,0:T(8,128)S(1)}, f32[12,128]{1,0:T(8,128)S(1)}, u32[]{:S(2)}, u32[]{:S(2)}) %collective-permute-start.29) | collective-permute-done | bytes 6176 | tf_op jit(solution)/shard_map/ppermute | solution.py:20
  85.9 1.2 %collective-permute-start.32 = (f32[2,4,128]{2,1,0:T(4,128)S(1)}, f32[2,4,128]{2,1,0:T(4,128)S(1)}, u32[]{:S(2)}, u32[]{:S(2)}) collective-permute-start(f32[2,4,128]{2,1,0:T(4,128)S(1)} %pad_maximum_fusion.3), channel_id=1, source_target_pairs={{0,3},{1,2},{2,1},{3,0},{4,7},{5,6},{6,5},{7,4},{8,11},{9,10},{10,... | collective-permute-start | bytes 12296 | tf_op jit(solution)/shard_map/ppermute | solution.py:20
  87.1 1.8 %collective-permute-done.31 = f32[2,4,128]{2,1,0:T(4,128)S(1)} collective-permute-done((f32[2,4,128]{2,1,0:T(4,128)S(1)}, f32[2,4,128]{2,1,0:T(4,128)S(1)}, u32[]{:S(2)}, u32[]{:S(2)}) %collective-permute-start.31) | collective-permute-done | bytes 4128 | tf_op jit(solution)/shard_map/ppermute | solution.py:20
  88.9 0.9 shard_map.77
  90.1 0.9 shard_map.76
  92.2 1.5 %collective-permute-start.34 = (f16[128,768]{1,0:T(8,128)(2,1)S(1)}, f16[128,768]{1,0:T(8,128)(2,1)S(1)}, u32[]{:S(2)}, u32[]{:S(2)}) collective-permute-start(f16[128,768]{1,0:T(8,128)(2,1)S(1)} %fusion.1), channel_id=1, source_target_pairs={{0,2},{2,0},{1,3},{3,1},{4,6},{6,4},{5,7},{7,5},{8,10},{10,8},{9,1... | collective-permute-start | bytes 589832 | tf_op jit(solution)/shard_map/ppermute | solution.py:20
  94.3 5.0 %collective-permute-done.34 = f16[128,768]{1,0:T(8,128)(2,1)S(1)} collective-permute-done((f16[128,768]{1,0:T(8,128)(2,1)S(1)}, f16[128,768]{1,0:T(8,128)(2,1)S(1)}, u32[]{:S(2)}, u32[]{:S(2)}) %collective-permute-start.34) | collective-permute-done | bytes 196640 | tf_op jit(solution)/shard_map/ppermute | solution.py:20
  99.3 0.8 fusion
  (80 shorter events, 11.3 us)
Async XLA Ops:
  0.6 11.7 %copy-start = (bf16[192,768]{1,0:T(8,128)(2,1)S(1)}, bf16[192,768]{1,0:T(8,128)(2,1)}, u32[]{:S(2)}) copy-start(bf16[192,768]{1,0:T(8,128)(2,1)} %param.5) | copy-start | bytes 884740
  0.6 16.2 %collective-permute-start.1 = (bf16[192,768]{1,0:T(8,128)(2,1)}, bf16[192,768]{1,0:T(8,128)(2,1)S(1)}, u32[]{:S(2)}, u32[]{:S(2)}) collective-permute-start(bf16[192,768]{1,0:T(8,128)(2,1)} %param.5), channel_id=1, source_target_pairs={{0,8},{8,0},{16,24},{24,16},{1,9},{9,1},{17,25},{25,17},{2,10},{10... | collective-permute-start | bytes 884744 | tf_op jit(solution)/shard_map/ppermute | solution.py:20
  3.6 16.4 %collective-permute-start.8 = (bf16[192,768]{1,0:T(8,128)(2,1)}, bf16[192,768]{1,0:T(8,128)(2,1)S(1)}, u32[]{:S(2)}, u32[]{:S(2)}) collective-permute-start(bf16[192,768]{1,0:T(8,128)(2,1)} %param.5), channel_id=1, source_target_pairs={{0,4},{4,0},{1,5},{5,1},{2,6},{6,2},{3,7},{7,3},{8,12},{12,8},{9,1... | collective-permute-start | bytes 884744 | tf_op jit(solution)/shard_map/ppermute | solution.py:20
  6.2 19.2 %collective-permute-start.6 = (bf16[192,768]{1,0:T(8,128)(2,1)}, bf16[192,768]{1,0:T(8,128)(2,1)S(1)}, u32[]{:S(2)}, u32[]{:S(2)}) collective-permute-start(bf16[192,768]{1,0:T(8,128)(2,1)} %param.5), channel_id=1, source_target_pairs={{0,16},{8,24},{16,0},{24,8},{1,17},{9,25},{17,1},{25,9},{2,18},{10... | collective-permute-start | bytes 884744 | tf_op jit(solution)/shard_map/ppermute | solution.py:20
  7.8 19.3 %collective-permute-start.7 = (bf16[192,768]{1,0:T(8,128)(2,1)}, bf16[192,768]{1,0:T(8,128)(2,1)S(1)}, u32[]{:S(2)}, u32[]{:S(2)}) collective-permute-start(bf16[192,768]{1,0:T(8,128)(2,1)} %param.5), channel_id=1, source_target_pairs={{0,24},{8,16},{16,8},{24,0},{1,25},{9,17},{17,9},{25,1},{2,26},{10... | collective-permute-start | bytes 884744 | tf_op jit(solution)/shard_map/ppermute | solution.py:20
  8.2 8.6 %collective-permute-start = (bf16[128,768]{1,0:T(8,128)(2,1)}, bf16[128,768]{1,0:T(8,128)(2,1)S(1)}, u32[]{:S(2)}, u32[]{:S(2)}) collective-permute-start(bf16[128,768]{1,0:T(8,128)(2,1)} %param.4), channel_id=1, source_target_pairs={{0,2},{2,0},{1,3},{3,1},{4,6},{6,4},{5,7},{7,5},{8,10},{10,8},{9,1... | collective-permute-start | bytes 589832 | tf_op jit(solution)/shard_map/ppermute | solution.py:20
  12.2 4.6 %copy-start.1 = (bf16[128,768]{1,0:T(8,128)(2,1)S(1)}, bf16[128,768]{1,0:T(8,128)(2,1)}, u32[]{:S(2)}) copy-start(bf16[128,768]{1,0:T(8,128)(2,1)} %param.4) | copy-start | bytes 589828
  12.2 7.0 %copy-start.2 = (f32[768]{0:T(1024)S(1)}, f32[768]{0:T(1024)}, u32[]{:S(2)}) copy-start(f32[768]{0:T(1024)} %param.7) | copy-start | bytes 9220
  16.8 11.3 %collective-permute-start.2 = (bf16[128,768]{1,0:T(8,128)(2,1)S(1)}, bf16[128,768]{1,0:T(8,128)(2,1)S(1)}, u32[]{:S(2)}, u32[]{:S(2)}) collective-permute-start(bf16[128,768]{1,0:T(8,128)(2,1)S(1)} %copy-done.1), channel_id=1, source_target_pairs={{0,4},{4,0},{1,5},{5,1},{2,6},{6,2},{3,7},{7,3},{8,12},{12,8},{9,1... | collective-permute-start | bytes 589832 | tf_op jit(solution)/shard_map/ppermute | solution.py:20
  19.2 14.6 %collective-permute-start.4 = (f32[768]{0:T(1024)S(1)}, f32[768]{0:T(1024)S(1)}, u32[]{:S(2)}, u32[]{:S(2)}) collective-permute-start(f32[768]{0:T(1024)S(1)} %copy-done.2), channel_id=1, source_target_pairs={{0,4},{4,0},{1,5},{5,1},{2,6},{6,2},{3,7},{7,3},{8,12},{12,8},{9,1... | collective-permute-start | bytes 9224 | tf_op jit(solution)/shard_map/ppermute | solution.py:20
  20.0 14.0 %collective-permute-start.9 = (bf16[192,768]{1,0:T(8,128)(2,1)S(1)}, bf16[192,768]{1,0:T(8,128)(2,1)S(1)}, u32[]{:S(2)}, u32[]{:S(2)}) collective-permute-start(bf16[192,768]{1,0:T(8,128)(2,1)S(1)} %collective-permute-done.8), channel_id=1, source_target_pairs={{0,8},{8,0},{16,24},{24,16},{1,9},{9,1},{17,25},{25,17},{2,10},{10... | collective-permute-start | bytes 884744 | tf_op jit(solution)/shard_map/ppermute | solution.py:20
  25.4 9.9 %collective-permute-start.10 = (bf16[192,768]{1,0:T(8,128)(2,1)S(1)}, bf16[192,768]{1,0:T(8,128)(2,1)S(1)}, u32[]{:S(2)}, u32[]{:S(2)}) collective-permute-start(bf16[192,768]{1,0:T(8,128)(2,1)S(1)} %collective-permute-done.8), channel_id=1, source_target_pairs={{0,16},{8,24},{16,0},{24,8},{1,17},{9,25},{17,1},{25,9},{2,18},{10... | collective-permute-start | bytes 884744 | tf_op jit(solution)/shard_map/ppermute | solution.py:20
  27.0 8.4 %collective-permute-start.11 = (bf16[192,768]{1,0:T(8,128)(2,1)S(1)}, bf16[192,768]{1,0:T(8,128)(2,1)S(1)}, u32[]{:S(2)}, u32[]{:S(2)}) collective-permute-start(bf16[192,768]{1,0:T(8,128)(2,1)S(1)} %collective-permute-done.8), channel_id=1, source_target_pairs={{0,24},{8,16},{16,8},{24,0},{1,25},{9,17},{17,9},{25,1},{2,26},{10... | collective-permute-start | bytes 884744 | tf_op jit(solution)/shard_map/ppermute | solution.py:20
  28.1 5.7 %collective-permute-start.3 = (bf16[128,768]{1,0:T(8,128)(2,1)S(1)}, bf16[128,768]{1,0:T(8,128)(2,1)S(1)}, u32[]{:S(2)}, u32[]{:S(2)}) collective-permute-start(bf16[128,768]{1,0:T(8,128)(2,1)S(1)} %collective-permute-done.2), channel_id=1, source_target_pairs={{0,2},{2,0},{1,3},{3,1},{4,6},{6,4},{5,7},{7,5},{8,10},{10,8},{9,1... | collective-permute-start | bytes 589832 | tf_op jit(solution)/shard_map/ppermute | solution.py:20
  33.9 2.4 %collective-permute-start.5 = (bf16[2,2,128,768]{3,2,1,0:T(8,128)(2,1)S(1)}, bf16[2,2,128,768]{3,2,1,0:T(8,128)(2,1)S(1)}, u32[]{:S(2)}, u32[]{:S(2)}) collective-permute-start(bf16[2,2,128,768]{3,2,1,0:T(8,128)(2,1)S(1)} %pad_maximum_fusion), channel_id=1, source_target_pairs={{0,1},{1,0},{2,3},{3,2},{4,5},{5,4},{6,7},{7,6},{8,9},{9,8},{10,11... | collective-permute-start | bytes 2359304 | tf_op jit(solution)/shard_map/ppermute | solution.py:20
  40.5 4.9 %collective-permute-start.12 = (f32[8,128]{1,0:T(8,128)S(1)}, f32[8,128]{1,0:T(8,128)S(1)}, u32[]{:S(2)}, u32[]{:S(2)}) collective-permute-start(f32[8,128]{1,0:T(8,128)S(1)} %shard_map.69), channel_id=1, source_target_pairs={{0,1},{1,0},{2,3},{3,2},{4,5},{5,4},{6,7},{7,6},{8,9},{9,8},{10,11... | collective-permute-start | bytes 12296 | tf_op jit(solution)/shard_map/ppermute | solution.py:20
  40.7 6.2 %collective-permute-start.13 = (f32[8,128]{1,0:T(8,128)S(1)}, f32[8,128]{1,0:T(8,128)S(1)}, u32[]{:S(2)}, u32[]{:S(2)}) collective-permute-start(f32[8,128]{1,0:T(8,128)S(1)} %shard_map.69), channel_id=1, source_target_pairs={{0,2},{1,3},{2,0},{3,1},{4,6},{5,7},{6,4},{7,5},{8,10},{9,11},{10,... | collective-permute-start | bytes 12296 | tf_op jit(solution)/shard_map/ppermute | solution.py:20
  45.3 3.0 %collective-permute-start.14 = (f32[8,128]{1,0:T(8,128)S(1)}, f32[8,128]{1,0:T(8,128)S(1)}, u32[]{:S(2)}, u32[]{:S(2)}) collective-permute-start(f32[8,128]{1,0:T(8,128)S(1)} %shard_map.69), channel_id=1, source_target_pairs={{0,3},{1,2},{2,1},{3,0},{4,7},{5,6},{6,5},{7,4},{8,11},{9,10},{10,... | collective-permute-start | bytes 12296 | tf_op jit(solution)/shard_map/ppermute | solution.py:20
  49.8 3.7 %collective-permute-start.15 = (f32[12,128]{1,0:T(8,128)S(1)}, f32[12,128]{1,0:T(8,128)S(1)}, u32[]{:S(2)}, u32[]{:S(2)}) collective-permute-start(f32[12,128]{1,0:T(8,128)S(1)} %shard_map.70), channel_id=1, source_target_pairs={{0,8},{8,0},{16,24},{24,16},{1,9},{9,1},{17,25},{25,17},{2,10},{10... | collective-permute-start | bytes 18440 | tf_op jit(solution)/shard_map/ppermute | solution.py:20
  50.9 3.7 %collective-permute-start.16 = (f32[12,128]{1,0:T(8,128)S(1)}, f32[12,128]{1,0:T(8,128)S(1)}, u32[]{:S(2)}, u32[]{:S(2)}) collective-permute-start(f32[12,128]{1,0:T(8,128)S(1)} %shard_map.70), channel_id=1, source_target_pairs={{0,16},{8,24},{16,0},{24,8},{1,17},{9,25},{17,1},{25,9},{2,18},{10... | collective-permute-start | bytes 18440 | tf_op jit(solution)/shard_map/ppermute | solution.py:20
  52.4 4.5 %collective-permute-start.17 = (f32[12,128]{1,0:T(8,128)S(1)}, f32[12,128]{1,0:T(8,128)S(1)}, u32[]{:S(2)}, u32[]{:S(2)}) collective-permute-start(f32[12,128]{1,0:T(8,128)S(1)} %shard_map.70), channel_id=1, source_target_pairs={{0,24},{8,16},{16,8},{24,0},{1,25},{9,17},{17,9},{25,1},{2,26},{10... | collective-permute-start | bytes 18440 | tf_op jit(solution)/shard_map/ppermute | solution.py:20
  58.3 1.9 %collective-permute-start.18 = (f32[8,128]{1,0:T(8,128)S(1)}, f32[8,128]{1,0:T(8,128)S(1)}, u32[]{:S(2)}, u32[]{:S(2)}) collective-permute-start(f32[8,128]{1,0:T(8,128)S(1)} %shard_map.71), channel_id=1, source_target_pairs={{0,1},{1,0},{2,3},{3,2},{4,5},{5,4},{6,7},{7,6},{8,9},{9,8},{10,11... | collective-permute-start | bytes 12296 | tf_op jit(solution)/shard_map/ppermute | solution.py:20
  58.4 3.7 %collective-permute-start.19 = (f32[8,128]{1,0:T(8,128)S(1)}, f32[8,128]{1,0:T(8,128)S(1)}, u32[]{:S(2)}, u32[]{:S(2)}) collective-permute-start(f32[8,128]{1,0:T(8,128)S(1)} %shard_map.71), channel_id=1, source_target_pairs={{0,2},{1,3},{2,0},{3,1},{4,6},{5,7},{6,4},{7,5},{8,10},{9,11},{10,... | collective-permute-start | bytes 12296 | tf_op jit(solution)/shard_map/ppermute | solution.py:20
  59.0 3.1 %collective-permute-start.20 = (f32[8,128]{1,0:T(8,128)S(1)}, f32[8,128]{1,0:T(8,128)S(1)}, u32[]{:S(2)}, u32[]{:S(2)}) collective-permute-start(f32[8,128]{1,0:T(8,128)S(1)} %shard_map.71), channel_id=1, source_target_pairs={{0,3},{1,2},{2,1},{3,0},{4,7},{5,6},{6,5},{7,4},{8,11},{9,10},{10,... | collective-permute-start | bytes 12296 | tf_op jit(solution)/shard_map/ppermute | solution.py:20
  63.5 3.7 %collective-permute-start.21 = (f32[12,128]{1,0:T(8,128)S(1)}, f32[12,128]{1,0:T(8,128)S(1)}, u32[]{:S(2)}, u32[]{:S(2)}) collective-permute-start(f32[12,128]{1,0:T(8,128)S(1)} %shard_map.72), channel_id=1, source_target_pairs={{0,8},{8,0},{16,24},{24,16},{1,9},{9,1},{17,25},{25,17},{2,10},{10... | collective-permute-start | bytes 18440 | tf_op jit(solution)/shard_map/ppermute | solution.py:20
  63.9 3.7 %collective-permute-start.22 = (f32[12,128]{1,0:T(8,128)S(1)}, f32[12,128]{1,0:T(8,128)S(1)}, u32[]{:S(2)}, u32[]{:S(2)}) collective-permute-start(f32[12,128]{1,0:T(8,128)S(1)} %shard_map.72), channel_id=1, source_target_pairs={{0,16},{8,24},{16,0},{24,8},{1,17},{9,25},{17,1},{25,9},{2,18},{10... | collective-permute-start | bytes 18440 | tf_op jit(solution)/shard_map/ppermute | solution.py:20
  65.1 4.5 %collective-permute-start.23 = (f32[12,128]{1,0:T(8,128)S(1)}, f32[12,128]{1,0:T(8,128)S(1)}, u32[]{:S(2)}, u32[]{:S(2)}) collective-permute-start(f32[12,128]{1,0:T(8,128)S(1)} %shard_map.72), channel_id=1, source_target_pairs={{0,24},{8,16},{16,8},{24,0},{1,25},{9,17},{17,9},{25,1},{2,26},{10... | collective-permute-start | bytes 18440 | tf_op jit(solution)/shard_map/ppermute | solution.py:20
  71.0 1.9 %collective-permute-start.24 = (f32[8,128]{1,0:T(8,128)S(1)}, f32[8,128]{1,0:T(8,128)S(1)}, u32[]{:S(2)}, u32[]{:S(2)}) collective-permute-start(f32[8,128]{1,0:T(8,128)S(1)} %shard_map.73), channel_id=1, source_target_pairs={{0,1},{1,0},{2,3},{3,2},{4,5},{5,4},{6,7},{7,6},{8,9},{9,8},{10,11... | collective-permute-start | bytes 12296 | tf_op jit(solution)/shard_map/ppermute | solution.py:20
  71.1 3.7 %collective-permute-start.25 = (f32[8,128]{1,0:T(8,128)S(1)}, f32[8,128]{1,0:T(8,128)S(1)}, u32[]{:S(2)}, u32[]{:S(2)}) collective-permute-start(f32[8,128]{1,0:T(8,128)S(1)} %shard_map.73), channel_id=1, source_target_pairs={{0,2},{1,3},{2,0},{3,1},{4,6},{5,7},{6,4},{7,5},{8,10},{9,11},{10,... | collective-permute-start | bytes 12296 | tf_op jit(solution)/shard_map/ppermute | solution.py:20
  72.5 3.0 %collective-permute-start.26 = (f32[8,128]{1,0:T(8,128)S(1)}, f32[8,128]{1,0:T(8,128)S(1)}, u32[]{:S(2)}, u32[]{:S(2)}) collective-permute-start(f32[8,128]{1,0:T(8,128)S(1)} %shard_map.73), channel_id=1, source_target_pairs={{0,3},{1,2},{2,1},{3,0},{4,7},{5,6},{6,5},{7,4},{8,11},{9,10},{10,... | collective-permute-start | bytes 12296 | tf_op jit(solution)/shard_map/ppermute | solution.py:20
  77.2 3.7 %collective-permute-start.27 = (f32[12,128]{1,0:T(8,128)S(1)}, f32[12,128]{1,0:T(8,128)S(1)}, u32[]{:S(2)}, u32[]{:S(2)}) collective-permute-start(f32[12,128]{1,0:T(8,128)S(1)} %shard_map.74), channel_id=1, source_target_pairs={{0,8},{8,0},{16,24},{24,16},{1,9},{9,1},{17,25},{25,17},{2,10},{10... | collective-permute-start | bytes 18440 | tf_op jit(solution)/shard_map/ppermute | solution.py:20
  78.3 3.7 %collective-permute-start.28 = (f32[12,128]{1,0:T(8,128)S(1)}, f32[12,128]{1,0:T(8,128)S(1)}, u32[]{:S(2)}, u32[]{:S(2)}) collective-permute-start(f32[12,128]{1,0:T(8,128)S(1)} %shard_map.74), channel_id=1, source_target_pairs={{0,16},{8,24},{16,0},{24,8},{1,17},{9,25},{17,1},{25,9},{2,18},{10... | collective-permute-start | bytes 18440 | tf_op jit(solution)/shard_map/ppermute | solution.py:20
  79.8 4.5 %collective-permute-start.29 = (f32[12,128]{1,0:T(8,128)S(1)}, f32[12,128]{1,0:T(8,128)S(1)}, u32[]{:S(2)}, u32[]{:S(2)}) collective-permute-start(f32[12,128]{1,0:T(8,128)S(1)} %shard_map.74), channel_id=1, source_target_pairs={{0,24},{8,16},{16,8},{24,0},{1,25},{9,17},{17,9},{25,1},{2,26},{10... | collective-permute-start | bytes 18440 | tf_op jit(solution)/shard_map/ppermute | solution.py:20
  85.1 1.9 %collective-permute-start.30 = (f32[2,4,128]{2,1,0:T(4,128)S(1)}, f32[2,4,128]{2,1,0:T(4,128)S(1)}, u32[]{:S(2)}, u32[]{:S(2)}) collective-permute-start(f32[2,4,128]{2,1,0:T(4,128)S(1)} %pad_maximum_fusion.3), channel_id=1, source_target_pairs={{0,1},{1,0},{2,3},{3,2},{4,5},{5,4},{6,7},{7,6},{8,9},{9,8},{10,11... | collective-permute-start | bytes 12296 | tf_op jit(solution)/shard_map/ppermute | solution.py:20
  85.2 3.7 %collective-permute-start.31 = (f32[2,4,128]{2,1,0:T(4,128)S(1)}, f32[2,4,128]{2,1,0:T(4,128)S(1)}, u32[]{:S(2)}, u32[]{:S(2)}) collective-permute-start(f32[2,4,128]{2,1,0:T(4,128)S(1)} %pad_maximum_fusion.3), channel_id=1, source_target_pairs={{0,2},{1,3},{2,0},{3,1},{4,6},{5,7},{6,4},{7,5},{8,10},{9,11},{10,... | collective-permute-start | bytes 12296 | tf_op jit(solution)/shard_map/ppermute | solution.py:20
  85.9 3.0 %collective-permute-start.32 = (f32[2,4,128]{2,1,0:T(4,128)S(1)}, f32[2,4,128]{2,1,0:T(4,128)S(1)}, u32[]{:S(2)}, u32[]{:S(2)}) collective-permute-start(f32[2,4,128]{2,1,0:T(4,128)S(1)} %pad_maximum_fusion.3), channel_id=1, source_target_pairs={{0,3},{1,2},{2,1},{3,0},{4,7},{5,6},{6,5},{7,4},{8,11},{9,10},{10,... | collective-permute-start | bytes 12296 | tf_op jit(solution)/shard_map/ppermute | solution.py:20
  89.8 2.4 %collective-permute-start.33 = (f32[256,768]{1,0:T(8,128)S(1)}, f32[256,768]{1,0:T(8,128)S(1)}, u32[]{:S(2)}, u32[]{:S(2)}) collective-permute-start(f32[256,768]{1,0:T(8,128)S(1)} %shard_map.77), channel_id=1, source_target_pairs={{0,1},{1,0},{2,3},{3,2},{4,5},{5,4},{6,7},{7,6},{8,9},{9,8},{10,11... | collective-permute-start | bytes 2359304 | tf_op jit(solution)/shard_map/ppermute | solution.py:20
  92.2 7.0 %collective-permute-start.34 = (f16[128,768]{1,0:T(8,128)(2,1)S(1)}, f16[128,768]{1,0:T(8,128)(2,1)S(1)}, u32[]{:S(2)}, u32[]{:S(2)}) collective-permute-start(f16[128,768]{1,0:T(8,128)(2,1)S(1)} %fusion.1), channel_id=1, source_target_pairs={{0,2},{2,0},{1,3},{3,1},{4,6},{6,4},{5,7},{7,5},{8,10},{10,8},{9,1... | collective-permute-start | bytes 589832 | tf_op jit(solution)/shard_map/ppermute | solution.py:20

commit v6 on v5

--- a/solution.py
+++ b/solution.py
@@ -26,7 +26,7 @@
 
 def place(blocks, index):
     whole = jnp.zeros((len(blocks),) + blocks[0].shape, blocks[0].dtype)
-    for k, block in enumerate(blocks):
+    for k, block in reversed(list(enumerate(blocks))):
         whole = lax.dynamic_update_index_in_dim(whole, block, index ^ k, 0)
     return whole
 
@@ -177,7 +177,7 @@
     own = swaps(tools, "row")
     half = nl * bq
     firsts = [jnp.full((1,), c * (half // LANES), jnp.int32) for c in (core, 1 - core)]
-    held, held_mass, firsts, own[1] = lax.optimization_barrier((queries, tool_mass, firsts, own[1]))
+    held, held_mass, firsts, own[2] = lax.optimization_barrier((queries, tool_mass, firsts, own[2]))
     tile_tools = [place(t, ri).reshape(-1, features) for t in (own, swaps(other_tools, "row"))]
     far, other_mass = swap(held, "zh", 1), swap(held_mass, "zh", 1)
     near_queries = place(swaps(queries, "zl"), li)
@@ -193,12 +193,15 @@
     tool_side = jnp.zeros_like(log_tool)
     for sweep in range(ITERS):
         (part,) = row_pass(tiles, tool_side, log_query.size)
-        query_side = log_query - lse_of(swaps(part, ("zl", "core")))
-        tool_side = log_tool - lse_of(swaps(col_pass(tiles, query_side), "row"))
+        got = swaps(part, ("zl", "core"))
+        query_side = log_query - lse_of(got[:1] + got[:0:-1])
+        got = swaps(col_pass(tiles, query_side), "row")
+        tool_side = log_tool - lse_of([got[k] for k in (0, *range(rows - 1, 0, -1))])
 
     ends = jnp.stack(row_pass(tiles, tool_side, log_query.size // 2, True))
     for axis in (("zl", "core"),):
         got = swaps(ends, axis)
+        got = got[:1] + got[:0:-1]
         ends = jnp.stack([lse_of([g[0] for g in got]), functools.reduce(jnp.maximum, [g[1] for g in got])])
     lse, peak = ends
 

time: 100 us -> 95.9 us (0.959)
  starting transfers between devices: 42.8 us -> 37.4 us
  waiting for transfers between devices: 37.1 us -> 38.2 us
    ppermute x35, starting transfers between devices: 42.8 us -> 37.4 us  [swap(): return lax.ppermute(x, axes, [(i, i ^ k) for i in range(n)])]
    ppermute x35, waiting for transfers between devices: 37.1 us -> 38.2 us  [swap(): return lax.ppermute(x, axes, [(i, i ^ k) for i in range(n)])]
  transfers between devices with their start and end apart: 35 -> 35, of which waited for: 23 -> 24; matrix products, arithmetic and copies ran while one was open for 4% -> 4% of each run, Pallas kernels for 1% -> 1%
where the time goes in v6:
time: 95.9 us; the launch traced here: 95.7 us
  waiting for transfers between devices  38.2 us (40%)
  starting transfers between devices  37.4 us (39%)
  Pallas kernels  13.7 us (14%)
  other arithmetic  3.11 us (3%)
  local copies, waits for them, and re-layouts  2.22 us (2%)
  between operations  0.98 us (1%)
    ppermute x35, waiting for transfers between devices, swap(): return lax.ppermute(x, axes, [(i, i ^ k) for i in range(n)])  38.2 us
    ppermute x35, starting transfers between devices, swap(): return lax.ppermute(x, axes, [(i, i ^ k) for i in range(n)])  37.4 us
    pallas_call x11, Pallas kernels, call(): pl.pallas_call(kernel, out_shape=out_shape, in_specs=[vmem] * (len(args)...  13.7 us
  transfers between devices with their start and end apart: 35, of which 24 were waited for; matrix products, arithmetic and copies ran while one was open for 4% of the time, Pallas kernels for 1%

profile of v6, /device:TPU:0, one launch (start us, length us, event | category | flops | bytes accessed | tf_op | source)
XLA Modules:
  0.0 95.7 jit_solution(7232059977167547208)
XLA Ops:
  0.7 3.0 %collective-permute-start.1 = (bf16[192,768]{1,0:T(8,128)(2,1)}, bf16[192,768]{1,0:T(8,128)(2,1)S(1)}, u32[]{:S(2)}, u32[]{:S(2)}) collective-permute-start(bf16[192,768]{1,0:T(8,128)(2,1)} %param.5), channel_id=1, source_target_pairs={{0,16},{8,24},{16,0},{24,8},{1,17},{9,25},{17,1},{25,9},{2,18},{10... | collective-permute-start | bytes 884744 | tf_op jit(solution)/shard_map/ppermute | solution.py:20
  3.7 2.6 %collective-permute-start.8 = (bf16[192,768]{1,0:T(8,128)(2,1)}, bf16[192,768]{1,0:T(8,128)(2,1)S(1)}, u32[]{:S(2)}, u32[]{:S(2)}) collective-permute-start(bf16[192,768]{1,0:T(8,128)(2,1)} %param.5), channel_id=1, source_target_pairs={{0,4},{4,0},{1,5},{5,1},{2,6},{6,2},{3,7},{7,3},{8,12},{12,8},{9,1... | collective-permute-start | bytes 884744 | tf_op jit(solution)/shard_map/ppermute | solution.py:20
  6.3 1.4 %collective-permute-start.6 = (bf16[192,768]{1,0:T(8,128)(2,1)}, bf16[192,768]{1,0:T(8,128)(2,1)S(1)}, u32[]{:S(2)}, u32[]{:S(2)}) collective-permute-start(bf16[192,768]{1,0:T(8,128)(2,1)} %param.5), channel_id=1, source_target_pairs={{0,24},{8,16},{16,8},{24,0},{1,25},{9,17},{17,9},{25,1},{2,26},{10... | collective-permute-start | bytes 884744 | tf_op jit(solution)/shard_map/ppermute | solution.py:20
  8.2 1.6 %collective-permute-start = (bf16[128,768]{1,0:T(8,128)(2,1)}, bf16[128,768]{1,0:T(8,128)(2,1)S(1)}, u32[]{:S(2)}, u32[]{:S(2)}) collective-permute-start(bf16[128,768]{1,0:T(8,128)(2,1)} %param.4), channel_id=1, source_target_pairs={{0,2},{2,0},{1,3},{3,1},{4,6},{6,4},{5,7},{7,5},{8,10},{10,8},{9,1... | collective-permute-start | bytes 589832 | tf_op jit(solution)/shard_map/ppermute | solution.py:20
  9.8 0.7 log_multiply_fusion
  10.5 0.7 multiply_bitcast_fusion.2
  11.2 5.6 %collective-permute-done = bf16[128,768]{1,0:T(8,128)(2,1)S(1)} collective-permute-done((bf16[128,768]{1,0:T(8,128)(2,1)}, bf16[128,768]{1,0:T(8,128)(2,1)S(1)}, u32[]{:S(2)}, u32[]{:S(2)}) %collective-permute-start) | collective-permute-done | bytes 196640 | tf_op jit(solution)/shard_map/ppermute | solution.py:20
  16.9 0.9 bitcast_dynamic-update-slice_fusion.12
  17.9 2.3 %collective-permute-start.2 = (bf16[128,768]{1,0:T(8,128)(2,1)S(1)}, bf16[128,768]{1,0:T(8,128)(2,1)S(1)}, u32[]{:S(2)}, u32[]{:S(2)}) collective-permute-start(bf16[128,768]{1,0:T(8,128)(2,1)S(1)} %copy-done.1), channel_id=1, source_target_pairs={{0,4},{4,0},{1,5},{5,1},{2,6},{6,2},{3,7},{7,3},{8,12},{12,8},{9,1... | collective-permute-start | bytes 589832 | tf_op jit(solution)/shard_map/ppermute | solution.py:20
  20.9 4.9 %collective-permute-start.9 = (bf16[192,768]{1,0:T(8,128)(2,1)S(1)}, bf16[192,768]{1,0:T(8,128)(2,1)S(1)}, u32[]{:S(2)}, u32[]{:S(2)}) collective-permute-start(bf16[192,768]{1,0:T(8,128)(2,1)S(1)} %collective-permute-done.8), channel_id=1, source_target_pairs={{0,24},{8,16},{16,8},{24,0},{1,25},{9,17},{17,9},{25,1},{2,26},{10... | collective-permute-start | bytes 884744 | tf_op jit(solution)/shard_map/ppermute | solution.py:20
  26.0 0.7 collective-permute-start.11
  26.7 1.9 %collective-permute-done.2 = bf16[128,768]{1,0:T(8,128)(2,1)S(1)} collective-permute-done((bf16[128,768]{1,0:T(8,128)(2,1)S(1)}, bf16[128,768]{1,0:T(8,128)(2,1)S(1)}, u32[]{:S(2)}, u32[]{:S(2)}) %collective-permute-start.2) | collective-permute-done | bytes 196640 | tf_op jit(solution)/shard_map/ppermute | solution.py:20
  29.2 5.1 %collective-permute-done.3 = bf16[128,768]{1,0:T(8,128)(2,1)S(1)} collective-permute-done((bf16[128,768]{1,0:T(8,128)(2,1)S(1)}, bf16[128,768]{1,0:T(8,128)(2,1)S(1)}, u32[]{:S(2)}, u32[]{:S(2)}) %collective-permute-start.3) | collective-permute-done | bytes 196640 | tf_op jit(solution)/shard_map/ppermute | solution.py:20
  35.2 1.6 %collective-permute-done.5 = bf16[2,2,128,768]{3,2,1,0:T(8,128)(2,1)S(1)} collective-permute-done((bf16[2,2,128,768]{3,2,1,0:T(8,128)(2,1)S(1)}, bf16[2,2,128,768]{3,2,1,0:T(8,128)(2,1)S(1)}, u32[]{:S(2)}, u32[]{:S(2)}) %collective-permute-start.5) | collective-permute-done | bytes 786464 | tf_op jit(solution)/shard_map/ppermute | solution.py:20
  37.1 1.4 %shard_map.68.refs_1_.tile1 = f32[1024,768]{1,0:T(8,128)S(1)} custom-call(bf16[1024,768]{1,0:T(8,128)(2,1)S(1)} %bitcast.96, bf16[768,768]{1,0:T(8,128)(2,1)S(1)} %bitcast.90), custom_call_target="tpu_custom_call" | custom-call | flops 1207959552 | bytes 5505024 | tf_op jit(solution)/shard_map/pallas_call | solution.py:122
  38.5 1.4 %shard_map.67.refs_0_.tile0 = f32[1024,768]{1,0:T(8,128)S(1)} custom-call(bf16[1024,768]{1,0:T(8,128)(2,1)S(1)} %bitcast.97, bf16[768,768]{1,0:T(8,128)(2,1)S(1)} %bitcast.93), custom_call_target="tpu_custom_call" | custom-call | flops 1207959552 | bytes 5505024 | tf_op jit(solution)/shard_map/pallas_call | solution.py:122
  39.9 1.3 %shard_map.69 = f32[8,128]{1,0:T(8,128)S(1)} custom-call(f32[1024,768]{1,0:T(8,128)S(1)} %shard_map.67.refs_0_.tile0, f32[1024,768]{1,0:T(8,128)S(1)} %shard_map.68.refs_1_.tile1, f32[12,128]{1,0:T(8,128)S(1)} %broadcast_in_dim.68.refs_2_), custom_call_target="tpu_custom_call" | custom-call | flops 9446400 | bytes 6297600 | tf_op jit(solution)/shard_map/pallas_call | solution.py:122
  41.3 1.4 %collective-permute-start.12 = (f32[8,128]{1,0:T(8,128)S(1)}, f32[8,128]{1,0:T(8,128)S(1)}, u32[]{:S(2)}, u32[]{:S(2)}) collective-permute-start(f32[8,128]{1,0:T(8,128)S(1)} %shard_map.69), channel_id=1, source_target_pairs={{0,3},{1,2},{2,1},{3,0},{4,7},{5,6},{6,5},{7,4},{8,11},{9,10},{10,... | collective-permute-start | bytes 12296 | tf_op jit(solution)/shard_map/ppermute | solution.py:20
  43.2 1.2 %collective-permute-done.12 = f32[8,128]{1,0:T(8,128)S(1)} collective-permute-done((f32[8,128]{1,0:T(8,128)S(1)}, f32[8,128]{1,0:T(8,128)S(1)}, u32[]{:S(2)}, u32[]{:S(2)}) %collective-permute-start.12) | collective-permute-done | bytes 4128 | tf_op jit(solution)/shard_map/ppermute | solution.py:20
  44.4 1.9 %collective-permute-done.13 = f32[8,128]{1,0:T(8,128)S(1)} collective-permute-done((f32[8,128]{1,0:T(8,128)S(1)}, f32[8,128]{1,0:T(8,128)S(1)}, u32[]{:S(2)}, u32[]{:S(2)}) %collective-permute-start.13) | collective-permute-done | bytes 4128 | tf_op jit(solution)/shard_map/ppermute | solution.py:20
  46.3 1.4 %shard_map.70 = f32[12,128]{1,0:T(8,128)S(1)} custom-call(f32[1024,768]{1,0:T(8,128)S(1)} %shard_map.67.refs_0_.tile0, f32[1024,768]{1,0:T(8,128)S(1)} %shard_map.68.refs_1_.tile1, f32[8,128]{1,0:T(8,128)S(1)} %add_subtract_fusion.5.refs_2_), custom_call_target="tpu_custom_call" | custom-call | flops 9443328 | bytes 6295552 | tf_op jit(solution)/shard_map/pallas_call | solution.py:122
  47.8 2.5 %collective-permute-start.15 = (f32[12,128]{1,0:T(8,128)S(1)}, f32[12,128]{1,0:T(8,128)S(1)}, u32[]{:S(2)}, u32[]{:S(2)}) collective-permute-start(f32[12,128]{1,0:T(8,128)S(1)} %shard_map.70), channel_id=1, source_target_pairs={{0,24},{8,16},{16,8},{24,0},{1,25},{9,17},{17,9},{25,1},{2,26},{10... | collective-permute-start | bytes 18440 | tf_op jit(solution)/shard_map/ppermute | solution.py:20
  51.3 1.1 %collective-permute-done.15 = f32[12,128]{1,0:T(8,128)S(1)} collective-permute-done((f32[12,128]{1,0:T(8,128)S(1)}, f32[12,128]{1,0:T(8,128)S(1)}, u32[]{:S(2)}, u32[]{:S(2)}) %collective-permute-start.15) | collective-permute-done | bytes 6176 | tf_op jit(solution)/shard_map/ppermute | solution.py:20
  52.4 1.5 %collective-permute-done.16 = f32[12,128]{1,0:T(8,128)S(1)} collective-permute-done((f32[12,128]{1,0:T(8,128)S(1)}, f32[12,128]{1,0:T(8,128)S(1)}, u32[]{:S(2)}, u32[]{:S(2)}) %collective-permute-start.16) | collective-permute-done | bytes 6176 | tf_op jit(solution)/shard_map/ppermute | solution.py:20
  54.5 1.3 %shard_map.71 = f32[8,128]{1,0:T(8,128)S(1)} custom-call(f32[1024,768]{1,0:T(8,128)S(1)} %shard_map.67.refs_0_.tile0, f32[1024,768]{1,0:T(8,128)S(1)} %shard_map.68.refs_1_.tile1, f32[12,128]{1,0:T(8,128)S(1)} %add_subtract_fusion.2.refs_2_), custom_call_target="tpu_custom_call" | custom-call | flops 9446400 | bytes 6297600 | tf_op jit(solution)/shard_map/pallas_call | solution.py:122
  56.3 1.4 %collective-permute-start.20 = (f32[8,128]{1,0:T(8,128)S(1)}, f32[8,128]{1,0:T(8,128)S(1)}, u32[]{:S(2)}, u32[]{:S(2)}) collective-permute-start(f32[8,128]{1,0:T(8,128)S(1)} %shard_map.71), channel_id=1, source_target_pairs={{0,1},{1,0},{2,3},{3,2},{4,5},{5,4},{6,7},{7,6},{8,9},{9,8},{10,11... | collective-permute-start | bytes 12296 | tf_op jit(solution)/shard_map/ppermute | solution.py:20
  57.7 1.2 %collective-permute-done.18 = f32[8,128]{1,0:T(8,128)S(1)} collective-permute-done((f32[8,128]{1,0:T(8,128)S(1)}, f32[8,128]{1,0:T(8,128)S(1)}, u32[]{:S(2)}, u32[]{:S(2)}) %collective-permute-start.18) | collective-permute-done | bytes 4128 | tf_op jit(solution)/shard_map/ppermute | solution.py:20
  58.9 0.7 collective-permute-done.19
  59.6 1.4 %shard_map.72 = f32[12,128]{1,0:T(8,128)S(1)} custom-call(f32[1024,768]{1,0:T(8,128)S(1)} %shard_map.67.refs_0_.tile0, f32[1024,768]{1,0:T(8,128)S(1)} %shard_map.68.refs_1_.tile1, f32[8,128]{1,0:T(8,128)S(1)} %add_subtract_fusion.4.refs_2_), custom_call_target="tpu_custom_call" | custom-call | flops 9443328 | bytes 6295552 | tf_op jit(solution)/shard_map/pallas_call | solution.py:122
  61.0 1.6 %collective-permute-start.21 = (f32[12,128]{1,0:T(8,128)S(1)}, f32[12,128]{1,0:T(8,128)S(1)}, u32[]{:S(2)}, u32[]{:S(2)}) collective-permute-start(f32[12,128]{1,0:T(8,128)S(1)} %shard_map.72), channel_id=1, source_target_pairs={{0,24},{8,16},{16,8},{24,0},{1,25},{9,17},{17,9},{25,1},{2,26},{10... | collective-permute-start | bytes 18440 | tf_op jit(solution)/shard_map/ppermute | solution.py:20
  63.0 1.5 %collective-permute-start.23 = (f32[12,128]{1,0:T(8,128)S(1)}, f32[12,128]{1,0:T(8,128)S(1)}, u32[]{:S(2)}, u32[]{:S(2)}) collective-permute-start(f32[12,128]{1,0:T(8,128)S(1)} %shard_map.72), channel_id=1, source_target_pairs={{0,8},{8,0},{16,24},{24,16},{1,9},{9,1},{17,25},{25,17},{2,10},{10... | collective-permute-start | bytes 18440 | tf_op jit(solution)/shard_map/ppermute | solution.py:20
  64.5 1.1 %collective-permute-done.21 = f32[12,128]{1,0:T(8,128)S(1)} collective-permute-done((f32[12,128]{1,0:T(8,128)S(1)}, f32[12,128]{1,0:T(8,128)S(1)}, u32[]{:S(2)}, u32[]{:S(2)}) %collective-permute-start.21) | collective-permute-done | bytes 6176 | tf_op jit(solution)/shard_map/ppermute | solution.py:20
  66.7 1.3 %shard_map.73 = f32[8,128]{1,0:T(8,128)S(1)} custom-call(f32[1024,768]{1,0:T(8,128)S(1)} %shard_map.67.refs_0_.tile0, f32[1024,768]{1,0:T(8,128)S(1)} %shard_map.68.refs_1_.tile1, f32[12,128]{1,0:T(8,128)S(1)} %add_subtract_fusion.1.refs_2_), custom_call_target="tpu_custom_call" | custom-call | flops 9446400 | bytes 6297600 | tf_op jit(solution)/shard_map/pallas_call | solution.py:122
  68.6 1.4 %collective-permute-start.26 = (f32[8,128]{1,0:T(8,128)S(1)}, f32[8,128]{1,0:T(8,128)S(1)}, u32[]{:S(2)}, u32[]{:S(2)}) collective-permute-start(f32[8,128]{1,0:T(8,128)S(1)} %shard_map.73), channel_id=1, source_target_pairs={{0,1},{1,0},{2,3},{3,2},{4,5},{5,4},{6,7},{7,6},{8,9},{9,8},{10,11... | collective-permute-start | bytes 12296 | tf_op jit(solution)/shard_map/ppermute | solution.py:20
  70.0 1.2 %collective-permute-done.24 = f32[8,128]{1,0:T(8,128)S(1)} collective-permute-done((f32[8,128]{1,0:T(8,128)S(1)}, f32[8,128]{1,0:T(8,128)S(1)}, u32[]{:S(2)}, u32[]{:S(2)}) %collective-permute-start.24) | collective-permute-done | bytes 4128 | tf_op jit(solution)/shard_map/ppermute | solution.py:20
  71.1 0.7 collective-permute-done.25
  71.8 1.6 %shard_map.74 = f32[12,128]{1,0:T(8,128)S(1)} custom-call(f32[1024,768]{1,0:T(8,128)S(1)} %shard_map.67.refs_0_.tile0, f32[1024,768]{1,0:T(8,128)S(1)} %shard_map.68.refs_1_.tile1, f32[8,128]{1,0:T(8,128)S(1)} %add_subtract_fusion.3.refs_2_), custom_call_target="tpu_custom_call" | custom-call | flops 9443328 | bytes 6295552 | tf_op jit(solution)/shard_map/pallas_call | solution.py:122
  73.4 2.5 %collective-permute-start.27 = (f32[12,128]{1,0:T(8,128)S(1)}, f32[12,128]{1,0:T(8,128)S(1)}, u32[]{:S(2)}, u32[]{:S(2)}) collective-permute-start(f32[12,128]{1,0:T(8,128)S(1)} %shard_map.74), channel_id=1, source_target_pairs={{0,24},{8,16},{16,8},{24,0},{1,25},{9,17},{17,9},{25,1},{2,26},{10... | collective-permute-start | bytes 18440 | tf_op jit(solution)/shard_map/ppermute | solution.py:20
  77.0 1.1 %collective-permute-done.27 = f32[12,128]{1,0:T(8,128)S(1)} collective-permute-done((f32[12,128]{1,0:T(8,128)S(1)}, f32[12,128]{1,0:T(8,128)S(1)}, u32[]{:S(2)}, u32[]{:S(2)}) %collective-permute-start.27) | collective-permute-done | bytes 6176 | tf_op jit(solution)/shard_map/ppermute | solution.py:20
  78.0 1.6 %collective-permute-done.28 = f32[12,128]{1,0:T(8,128)S(1)} collective-permute-done((f32[12,128]{1,0:T(8,128)S(1)}, f32[12,128]{1,0:T(8,128)S(1)}, u32[]{:S(2)}, u32[]{:S(2)}) %collective-permute-start.28) | collective-permute-done | bytes 6176 | tf_op jit(solution)/shard_map/ppermute | solution.py:20
  80.1 0.7 shard_map.75
  81.4 1.4 %collective-permute-start.32 = (f32[2,4,128]{2,1,0:T(4,128)S(1)}, f32[2,4,128]{2,1,0:T(4,128)S(1)}, u32[]{:S(2)}, u32[]{:S(2)}) collective-permute-start(f32[2,4,128]{2,1,0:T(4,128)S(1)} %pad_maximum_fusion.3), channel_id=1, source_target_pairs={{0,1},{1,0},{2,3},{3,2},{4,5},{5,4},{6,7},{7,6},{8,9},{9,8},{10,11... | collective-permute-start | bytes 12296 | tf_op jit(solution)/shard_map/ppermute | solution.py:20
  82.8 1.2 %collective-permute-done.30 = f32[2,4,128]{2,1,0:T(4,128)S(1)} collective-permute-done((f32[2,4,128]{2,1,0:T(4,128)S(1)}, f32[2,4,128]{2,1,0:T(4,128)S(1)}, u32[]{:S(2)}, u32[]{:S(2)}) %collective-permute-start.30) | collective-permute-done | bytes 4128 | tf_op jit(solution)/shard_map/ppermute | solution.py:20
  84.6 0.9 shard_map.77
  85.6 0.9 shard_map.76
  87.1 0.8 collective-permute-done.33
  89.1 5.8 %collective-permute-done.34 = f16[128,768]{1,0:T(8,128)(2,1)S(1)} collective-permute-done((f16[128,768]{1,0:T(8,128)(2,1)S(1)}, f16[128,768]{1,0:T(8,128)(2,1)S(1)}, u32[]{:S(2)}, u32[]{:S(2)}) %collective-permute-start.34) | collective-permute-done | bytes 196640 | tf_op jit(solution)/shard_map/ppermute | solution.py:20
  94.9 0.8 fusion
  (80 shorter events, 12.5 us)
Async XLA Ops:
  0.6 17.2 %copy-start.1 = (bf16[128,768]{1,0:T(8,128)(2,1)S(1)}, bf16[128,768]{1,0:T(8,128)(2,1)}, u32[]{:S(2)}) copy-start(bf16[128,768]{1,0:T(8,128)(2,1)} %param.4) | copy-start | bytes 589828
  0.6 19.6 %copy-start.2 = (f32[768]{0:T(1024)S(1)}, f32[768]{0:T(1024)}, u32[]{:S(2)}) copy-start(f32[768]{0:T(1024)} %param.7) | copy-start | bytes 9220
  0.7 17.2 %collective-permute-start.1 = (bf16[192,768]{1,0:T(8,128)(2,1)}, bf16[192,768]{1,0:T(8,128)(2,1)S(1)}, u32[]{:S(2)}, u32[]{:S(2)}) collective-permute-start(bf16[192,768]{1,0:T(8,128)(2,1)} %param.5), channel_id=1, source_target_pairs={{0,16},{8,24},{16,0},{24,8},{1,17},{9,25},{17,1},{25,9},{2,18},{10... | collective-permute-start | bytes 884744 | tf_op jit(solution)/shard_map/ppermute | solution.py:20
  3.7 17.2 %collective-permute-start.8 = (bf16[192,768]{1,0:T(8,128)(2,1)}, bf16[192,768]{1,0:T(8,128)(2,1)S(1)}, u32[]{:S(2)}, u32[]{:S(2)}) collective-permute-start(bf16[192,768]{1,0:T(8,128)(2,1)} %param.5), channel_id=1, source_target_pairs={{0,4},{4,0},{1,5},{5,1},{2,6},{6,2},{3,7},{7,3},{8,12},{12,8},{9,1... | collective-permute-start | bytes 884744 | tf_op jit(solution)/shard_map/ppermute | solution.py:20
  6.3 19.5 %collective-permute-start.6 = (bf16[192,768]{1,0:T(8,128)(2,1)}, bf16[192,768]{1,0:T(8,128)(2,1)S(1)}, u32[]{:S(2)}, u32[]{:S(2)}) collective-permute-start(bf16[192,768]{1,0:T(8,128)(2,1)} %param.5), channel_id=1, source_target_pairs={{0,24},{8,16},{16,8},{24,0},{1,25},{9,17},{17,9},{25,1},{2,26},{10... | collective-permute-start | bytes 884744 | tf_op jit(solution)/shard_map/ppermute | solution.py:20
  7.7 18.3 %collective-permute-start.7 = (bf16[192,768]{1,0:T(8,128)(2,1)}, bf16[192,768]{1,0:T(8,128)(2,1)S(1)}, u32[]{:S(2)}, u32[]{:S(2)}) collective-permute-start(bf16[192,768]{1,0:T(8,128)(2,1)} %param.5), channel_id=1, source_target_pairs={{0,8},{8,0},{16,24},{24,16},{1,9},{9,1},{17,25},{25,17},{2,10},{10... | collective-permute-start | bytes 884744 | tf_op jit(solution)/shard_map/ppermute | solution.py:20
  8.2 8.6 %collective-permute-start = (bf16[128,768]{1,0:T(8,128)(2,1)}, bf16[128,768]{1,0:T(8,128)(2,1)S(1)}, u32[]{:S(2)}, u32[]{:S(2)}) collective-permute-start(bf16[128,768]{1,0:T(8,128)(2,1)} %param.4), channel_id=1, source_target_pairs={{0,2},{2,0},{1,3},{3,1},{4,6},{6,4},{5,7},{7,5},{8,10},{10,8},{9,1... | collective-permute-start | bytes 589832 | tf_op jit(solution)/shard_map/ppermute | solution.py:20
  17.9 10.8 %collective-permute-start.2 = (bf16[128,768]{1,0:T(8,128)(2,1)S(1)}, bf16[128,768]{1,0:T(8,128)(2,1)S(1)}, u32[]{:S(2)}, u32[]{:S(2)}) collective-permute-start(bf16[128,768]{1,0:T(8,128)(2,1)S(1)} %copy-done.1), channel_id=1, source_target_pairs={{0,4},{4,0},{1,5},{5,1},{2,6},{6,2},{3,7},{7,3},{8,12},{12,8},{9,1... | collective-permute-start | bytes 589832 | tf_op jit(solution)/shard_map/ppermute | solution.py:20
  20.2 14.2 %collective-permute-start.4 = (f32[768]{0:T(1024)S(1)}, f32[768]{0:T(1024)S(1)}, u32[]{:S(2)}, u32[]{:S(2)}) collective-permute-start(f32[768]{0:T(1024)S(1)} %copy-done.2), channel_id=1, source_target_pairs={{0,4},{4,0},{1,5},{5,1},{2,6},{6,2},{3,7},{7,3},{8,12},{12,8},{9,1... | collective-permute-start | bytes 9224 | tf_op jit(solution)/shard_map/ppermute | solution.py:20
  20.9 13.7 %collective-permute-start.9 = (bf16[192,768]{1,0:T(8,128)(2,1)S(1)}, bf16[192,768]{1,0:T(8,128)(2,1)S(1)}, u32[]{:S(2)}, u32[]{:S(2)}) collective-permute-start(bf16[192,768]{1,0:T(8,128)(2,1)S(1)} %collective-permute-done.8), channel_id=1, source_target_pairs={{0,24},{8,16},{16,8},{24,0},{1,25},{9,17},{17,9},{25,1},{2,26},{10... | collective-permute-start | bytes 884744 | tf_op jit(solution)/shard_map/ppermute | solution.py:20
  25.8 9.3 %collective-permute-start.10 = (bf16[192,768]{1,0:T(8,128)(2,1)S(1)}, bf16[192,768]{1,0:T(8,128)(2,1)S(1)}, u32[]{:S(2)}, u32[]{:S(2)}) collective-permute-start(bf16[192,768]{1,0:T(8,128)(2,1)S(1)} %collective-permute-done.8), channel_id=1, source_target_pairs={{0,16},{8,24},{16,0},{24,8},{1,17},{9,25},{17,1},{25,9},{2,18},{10... | collective-permute-start | bytes 884744 | tf_op jit(solution)/shard_map/ppermute | solution.py:20
  25.9 3.3 %copy-start = (bf16[192,768]{1,0:T(8,128)(2,1)S(1)}, bf16[192,768]{1,0:T(8,128)(2,1)}, u32[]{:S(2)}) copy-start(bf16[192,768]{1,0:T(8,128)(2,1)} %param.5) | copy-start | bytes 884740
  26.0 9.1 %collective-permute-start.11 = (bf16[192,768]{1,0:T(8,128)(2,1)S(1)}, bf16[192,768]{1,0:T(8,128)(2,1)S(1)}, u32[]{:S(2)}, u32[]{:S(2)}) collective-permute-start(bf16[192,768]{1,0:T(8,128)(2,1)S(1)} %collective-permute-done.8), channel_id=1, source_target_pairs={{0,8},{8,0},{16,24},{24,16},{1,9},{9,1},{17,25},{25,17},{2,10},{10... | collective-permute-start | bytes 884744 | tf_op jit(solution)/shard_map/ppermute | solution.py:20
  28.6 5.7 %collective-permute-start.3 = (bf16[128,768]{1,0:T(8,128)(2,1)S(1)}, bf16[128,768]{1,0:T(8,128)(2,1)S(1)}, u32[]{:S(2)}, u32[]{:S(2)}) collective-permute-start(bf16[128,768]{1,0:T(8,128)(2,1)S(1)} %collective-permute-done.2), channel_id=1, source_target_pairs={{0,2},{2,0},{1,3},{3,1},{4,6},{6,4},{5,7},{7,5},{8,10},{10,8},{9,1... | collective-permute-start | bytes 589832 | tf_op jit(solution)/shard_map/ppermute | solution.py:20
  34.5 2.4 %collective-permute-start.5 = (bf16[2,2,128,768]{3,2,1,0:T(8,128)(2,1)S(1)}, bf16[2,2,128,768]{3,2,1,0:T(8,128)(2,1)S(1)}, u32[]{:S(2)}, u32[]{:S(2)}) collective-permute-start(bf16[2,2,128,768]{3,2,1,0:T(8,128)(2,1)S(1)} %pad_maximum_fusion), channel_id=1, source_target_pairs={{0,1},{1,0},{2,3},{3,2},{4,5},{5,4},{6,7},{7,6},{8,9},{9,8},{10,11... | collective-permute-start | bytes 2359304 | tf_op jit(solution)/shard_map/ppermute | solution.py:20
  41.3 3.1 %collective-permute-start.12 = (f32[8,128]{1,0:T(8,128)S(1)}, f32[8,128]{1,0:T(8,128)S(1)}, u32[]{:S(2)}, u32[]{:S(2)}) collective-permute-start(f32[8,128]{1,0:T(8,128)S(1)} %shard_map.69), channel_id=1, source_target_pairs={{0,3},{1,2},{2,1},{3,0},{4,7},{5,6},{6,5},{7,4},{8,11},{9,10},{10,... | collective-permute-start | bytes 12296 | tf_op jit(solution)/shard_map/ppermute | solution.py:20
  42.7 3.6 %collective-permute-start.13 = (f32[8,128]{1,0:T(8,128)S(1)}, f32[8,128]{1,0:T(8,128)S(1)}, u32[]{:S(2)}, u32[]{:S(2)}) collective-permute-start(f32[8,128]{1,0:T(8,128)S(1)} %shard_map.69), channel_id=1, source_target_pairs={{0,2},{1,3},{2,0},{3,1},{4,6},{5,7},{6,4},{7,5},{8,10},{9,11},{10,... | collective-permute-start | bytes 12296 | tf_op jit(solution)/shard_map/ppermute | solution.py:20
  43.1 3.2 %collective-permute-start.14 = (f32[8,128]{1,0:T(8,128)S(1)}, f32[8,128]{1,0:T(8,128)S(1)}, u32[]{:S(2)}, u32[]{:S(2)}) collective-permute-start(f32[8,128]{1,0:T(8,128)S(1)} %shard_map.69), channel_id=1, source_target_pairs={{0,1},{1,0},{2,3},{3,2},{4,5},{5,4},{6,7},{7,6},{8,9},{9,8},{10,11... | collective-permute-start | bytes 12296 | tf_op jit(solution)/shard_map/ppermute | solution.py:20
  47.8 4.6 %collective-permute-start.15 = (f32[12,128]{1,0:T(8,128)S(1)}, f32[12,128]{1,0:T(8,128)S(1)}, u32[]{:S(2)}, u32[]{:S(2)}) collective-permute-start(f32[12,128]{1,0:T(8,128)S(1)} %shard_map.70), channel_id=1, source_target_pairs={{0,24},{8,16},{16,8},{24,0},{1,25},{9,17},{17,9},{25,1},{2,26},{10... | collective-permute-start | bytes 18440 | tf_op jit(solution)/shard_map/ppermute | solution.py:20
  50.3 3.7 %collective-permute-start.16 = (f32[12,128]{1,0:T(8,128)S(1)}, f32[12,128]{1,0:T(8,128)S(1)}, u32[]{:S(2)}, u32[]{:S(2)}) collective-permute-start(f32[12,128]{1,0:T(8,128)S(1)} %shard_map.70), channel_id=1, source_target_pairs={{0,16},{8,24},{16,0},{24,8},{1,17},{9,25},{17,1},{25,9},{2,18},{10... | collective-permute-start | bytes 18440 | tf_op jit(solution)/shard_map/ppermute | solution.py:20
  50.8 3.7 %collective-permute-start.17 = (f32[12,128]{1,0:T(8,128)S(1)}, f32[12,128]{1,0:T(8,128)S(1)}, u32[]{:S(2)}, u32[]{:S(2)}) collective-permute-start(f32[12,128]{1,0:T(8,128)S(1)} %shard_map.70), channel_id=1, source_target_pairs={{0,8},{8,0},{16,24},{24,16},{1,9},{9,1},{17,25},{25,17},{2,10},{10... | collective-permute-start | bytes 18440 | tf_op jit(solution)/shard_map/ppermute | solution.py:20
  55.8 3.1 %collective-permute-start.18 = (f32[8,128]{1,0:T(8,128)S(1)}, f32[8,128]{1,0:T(8,128)S(1)}, u32[]{:S(2)}, u32[]{:S(2)}) collective-permute-start(f32[8,128]{1,0:T(8,128)S(1)} %shard_map.71), channel_id=1, source_target_pairs={{0,3},{1,2},{2,1},{3,0},{4,7},{5,6},{6,5},{7,4},{8,11},{9,10},{10,... | collective-permute-start | bytes 12296 | tf_op jit(solution)/shard_map/ppermute | solution.py:20
  55.9 3.7 %collective-permute-start.19 = (f32[8,128]{1,0:T(8,128)S(1)}, f32[8,128]{1,0:T(8,128)S(1)}, u32[]{:S(2)}, u32[]{:S(2)}) collective-permute-start(f32[8,128]{1,0:T(8,128)S(1)} %shard_map.71), channel_id=1, source_target_pairs={{0,2},{1,3},{2,0},{3,1},{4,6},{5,7},{6,4},{7,5},{8,10},{9,11},{10,... | collective-permute-start | bytes 12296 | tf_op jit(solution)/shard_map/ppermute | solution.py:20
  56.3 3.2 %collective-permute-start.20 = (f32[8,128]{1,0:T(8,128)S(1)}, f32[8,128]{1,0:T(8,128)S(1)}, u32[]{:S(2)}, u32[]{:S(2)}) collective-permute-start(f32[8,128]{1,0:T(8,128)S(1)} %shard_map.71), channel_id=1, source_target_pairs={{0,1},{1,0},{2,3},{3,2},{4,5},{5,4},{6,7},{7,6},{8,9},{9,8},{10,11... | collective-permute-start | bytes 12296 | tf_op jit(solution)/shard_map/ppermute | solution.py:20
  61.0 4.7 %collective-permute-start.21 = (f32[12,128]{1,0:T(8,128)S(1)}, f32[12,128]{1,0:T(8,128)S(1)}, u32[]{:S(2)}, u32[]{:S(2)}) collective-permute-start(f32[12,128]{1,0:T(8,128)S(1)} %shard_map.72), channel_id=1, source_target_pairs={{0,24},{8,16},{16,8},{24,0},{1,25},{9,17},{17,9},{25,1},{2,26},{10... | collective-permute-start | bytes 18440 | tf_op jit(solution)/shard_map/ppermute | solution.py:20
  62.6 3.7 %collective-permute-start.22 = (f32[12,128]{1,0:T(8,128)S(1)}, f32[12,128]{1,0:T(8,128)S(1)}, u32[]{:S(2)}, u32[]{:S(2)}) collective-permute-start(f32[12,128]{1,0:T(8,128)S(1)} %shard_map.72), channel_id=1, source_target_pairs={{0,16},{8,24},{16,0},{24,8},{1,17},{9,25},{17,1},{25,9},{2,18},{10... | collective-permute-start | bytes 18440 | tf_op jit(solution)/shard_map/ppermute | solution.py:20
  63.0 3.7 %collective-permute-start.23 = (f32[12,128]{1,0:T(8,128)S(1)}, f32[12,128]{1,0:T(8,128)S(1)}, u32[]{:S(2)}, u32[]{:S(2)}) collective-permute-start(f32[12,128]{1,0:T(8,128)S(1)} %shard_map.72), channel_id=1, source_target_pairs={{0,8},{8,0},{16,24},{24,16},{1,9},{9,1},{17,25},{25,17},{2,10},{10... | collective-permute-start | bytes 18440 | tf_op jit(solution)/shard_map/ppermute | solution.py:20
  68.0 3.1 %collective-permute-start.24 = (f32[8,128]{1,0:T(8,128)S(1)}, f32[8,128]{1,0:T(8,128)S(1)}, u32[]{:S(2)}, u32[]{:S(2)}) collective-permute-start(f32[8,128]{1,0:T(8,128)S(1)} %shard_map.73), channel_id=1, source_target_pairs={{0,3},{1,2},{2,1},{3,0},{4,7},{5,6},{6,5},{7,4},{8,11},{9,10},{10,... | collective-permute-start | bytes 12296 | tf_op jit(solution)/shard_map/ppermute | solution.py:20
  68.1 3.7 %collective-permute-start.25 = (f32[8,128]{1,0:T(8,128)S(1)}, f32[8,128]{1,0:T(8,128)S(1)}, u32[]{:S(2)}, u32[]{:S(2)}) collective-permute-start(f32[8,128]{1,0:T(8,128)S(1)} %shard_map.73), channel_id=1, source_target_pairs={{0,2},{1,3},{2,0},{3,1},{4,6},{5,7},{6,4},{7,5},{8,10},{9,11},{10,... | collective-permute-start | bytes 12296 | tf_op jit(solution)/shard_map/ppermute | solution.py:20
  68.6 3.2 %collective-permute-start.26 = (f32[8,128]{1,0:T(8,128)S(1)}, f32[8,128]{1,0:T(8,128)S(1)}, u32[]{:S(2)}, u32[]{:S(2)}) collective-permute-start(f32[8,128]{1,0:T(8,128)S(1)} %shard_map.73), channel_id=1, source_target_pairs={{0,1},{1,0},{2,3},{3,2},{4,5},{5,4},{6,7},{7,6},{8,9},{9,8},{10,11... | collective-permute-start | bytes 12296 | tf_op jit(solution)/shard_map/ppermute | solution.py:20
  73.4 4.6 %collective-permute-start.27 = (f32[12,128]{1,0:T(8,128)S(1)}, f32[12,128]{1,0:T(8,128)S(1)}, u32[]{:S(2)}, u32[]{:S(2)}) collective-permute-start(f32[12,128]{1,0:T(8,128)S(1)} %shard_map.74), channel_id=1, source_target_pairs={{0,24},{8,16},{16,8},{24,0},{1,25},{9,17},{17,9},{25,1},{2,26},{10... | collective-permute-start | bytes 18440 | tf_op jit(solution)/shard_map/ppermute | solution.py:20
  75.9 3.7 %collective-permute-start.28 = (f32[12,128]{1,0:T(8,128)S(1)}, f32[12,128]{1,0:T(8,128)S(1)}, u32[]{:S(2)}, u32[]{:S(2)}) collective-permute-start(f32[12,128]{1,0:T(8,128)S(1)} %shard_map.74), channel_id=1, source_target_pairs={{0,16},{8,24},{16,0},{24,8},{1,17},{9,25},{17,1},{25,9},{2,18},{10... | collective-permute-start | bytes 18440 | tf_op jit(solution)/shard_map/ppermute | solution.py:20
  76.4 3.7 %collective-permute-start.29 = (f32[12,128]{1,0:T(8,128)S(1)}, f32[12,128]{1,0:T(8,128)S(1)}, u32[]{:S(2)}, u32[]{:S(2)}) collective-permute-start(f32[12,128]{1,0:T(8,128)S(1)} %shard_map.74), channel_id=1, source_target_pairs={{0,8},{8,0},{16,24},{24,16},{1,9},{9,1},{17,25},{25,17},{2,10},{10... | collective-permute-start | bytes 18440 | tf_op jit(solution)/shard_map/ppermute | solution.py:20
  80.8 3.1 %collective-permute-start.30 = (f32[2,4,128]{2,1,0:T(4,128)S(1)}, f32[2,4,128]{2,1,0:T(4,128)S(1)}, u32[]{:S(2)}, u32[]{:S(2)}) collective-permute-start(f32[2,4,128]{2,1,0:T(4,128)S(1)} %pad_maximum_fusion.3), channel_id=1, source_target_pairs={{0,3},{1,2},{2,1},{3,0},{4,7},{5,6},{6,5},{7,4},{8,11},{9,10},{10,... | collective-permute-start | bytes 12296 | tf_op jit(solution)/shard_map/ppermute | solution.py:20
  80.9 3.7 %collective-permute-start.31 = (f32[2,4,128]{2,1,0:T(4,128)S(1)}, f32[2,4,128]{2,1,0:T(4,128)S(1)}, u32[]{:S(2)}, u32[]{:S(2)}) collective-permute-start(f32[2,4,128]{2,1,0:T(4,128)S(1)} %pad_maximum_fusion.3), channel_id=1, source_target_pairs={{0,2},{1,3},{2,0},{3,1},{4,6},{5,7},{6,4},{7,5},{8,10},{9,11},{10,... | collective-permute-start | bytes 12296 | tf_op jit(solution)/shard_map/ppermute | solution.py:20
  81.4 3.2 %collective-permute-start.32 = (f32[2,4,128]{2,1,0:T(4,128)S(1)}, f32[2,4,128]{2,1,0:T(4,128)S(1)}, u32[]{:S(2)}, u32[]{:S(2)}) collective-permute-start(f32[2,4,128]{2,1,0:T(4,128)S(1)} %pad_maximum_fusion.3), channel_id=1, source_target_pairs={{0,1},{1,0},{2,3},{3,2},{4,5},{5,4},{6,7},{7,6},{8,9},{9,8},{10,11... | collective-permute-start | bytes 12296 | tf_op jit(solution)/shard_map/ppermute | solution.py:20
  85.5 2.4 %collective-permute-start.33 = (f32[256,768]{1,0:T(8,128)S(1)}, f32[256,768]{1,0:T(8,128)S(1)}, u32[]{:S(2)}, u32[]{:S(2)}) collective-permute-start(f32[256,768]{1,0:T(8,128)S(1)} %shard_map.77), channel_id=1, source_target_pairs={{0,1},{1,0},{2,3},{3,2},{4,5},{5,4},{6,7},{7,6},{8,9},{9,8},{10,11... | collective-permute-start | bytes 2359304 | tf_op jit(solution)/shard_map/ppermute | solution.py:20
  87.9 7.0 %collective-permute-start.34 = (f16[128,768]{1,0:T(8,128)(2,1)S(1)}, f16[128,768]{1,0:T(8,128)(2,1)S(1)}, u32[]{:S(2)}, u32[]{:S(2)}) collective-permute-start(f16[128,768]{1,0:T(8,128)(2,1)S(1)} %fusion.1), channel_id=1, source_target_pairs={{0,2},{2,0},{1,3},{3,1},{4,6},{6,4},{5,7},{7,5},{8,10},{10,8},{9,1... | collective-permute-start | bytes 589832 | tf_op jit(solution)/shard_map/ppermute | solution.py:20

commit v7 on v6

--- a/solution.py
+++ b/solution.py
@@ -24,10 +24,10 @@
     return [x] + [swap(x, axes, k) for k in range(1, lax.axis_size(axes))]
 
 
-def place(blocks, index):
+def place(blocks, index, forward=False):
     whole = jnp.zeros((len(blocks),) + blocks[0].shape, blocks[0].dtype)
-    for k, block in reversed(list(enumerate(blocks))):
-        whole = lax.dynamic_update_index_in_dim(whole, block, index ^ k, 0)
+    for k in range(len(blocks))[:: 1 if forward else -1]:
+        whole = lax.dynamic_update_index_in_dim(whole, blocks[k], index ^ k, 0)
     return whole
 
 
@@ -144,11 +144,11 @@
 
 
 def dot_kernel(scaling, a, b, out):
-    for r in range(0, out.shape[0], 256):
+    for r in range(0, out.shape[0], 512):
         part = lax.dot_general(
-            a[r : r + 256, :], b[...], (((1,), (1,)), ((), ())), preferred_element_type=jnp.float32
+            a[r : r + 512, :], b[...], (((1,), (1,)), ((), ())), preferred_element_type=jnp.float32
         )
-        out[r : r + 256, :] = part * scaling
+        out[r : r + 512, :] = part * scaling
 
 
 def scaled_dot(a, b, scaling):
@@ -184,7 +184,7 @@
     far_queries = place(swaps(far, "zl"), li)
     far_queries, other_mass = lax.optimization_barrier((far_queries, other_mass))
     tile_queries = jnp.stack([near_queries, far_queries])
-    tile_queries = jnp.moveaxis(place(pairs(tile_queries, "core"), core), 0, 1).reshape(-1, features)
+    tile_queries = jnp.moveaxis(place(pairs(tile_queries, "core"), core, True), 0, 1).reshape(-1, features)
     log_tool = jnp.concatenate([jnp.log2(tool_mass), jnp.log2(other_mass)]).reshape(-1, LANES)
     log_query = jnp.log2(query_mass).reshape(2, nl, 2, bq).transpose(0, 2, 1, 3)
     log_query = by_place([log_query[0], log_query[1]], hi).reshape(-1, LANES)

time: 95.9 us -> 95.7 us (level)
  transfers between devices with their start and end apart: 35 -> 35, of which waited for: 24 -> 25; matrix products, arithmetic and copies ran while one was open for 4% -> 4% of each run, Pallas kernels for 1% -> 1%
where the time goes in v7:
time: 95.7 us; the launch traced here: 95.5 us
  waiting for transfers between devices  37.9 us (40%)
  starting transfers between devices  37.4 us (39%)
  Pallas kernels  13.7 us (14%)
  other arithmetic  3.11 us (3%)
  local copies, waits for them, and re-layouts  2.36 us (2%)
  between operations  0.97 us (1%)
    ppermute x35, waiting for transfers between devices, swap(): return lax.ppermute(x, axes, [(i, i ^ k) for i in range(n)])  37.9 us
    ppermute x35, starting transfers between devices, swap(): return lax.ppermute(x, axes, [(i, i ^ k) for i in range(n)])  37.4 us
    pallas_call x11, Pallas kernels, call(): pl.pallas_call(kernel, out_shape=out_shape, in_specs=[vmem] * (len(args)...  13.7 us
  transfers between devices with their start and end apart: 35, of which 25 were waited for; matrix products, arithmetic and copies ran while one was open for 4% of the time, Pallas kernels for 1%

profile of v7, /device:TPU:0, one launch (start us, length us, event | category | flops | bytes accessed | tf_op | source)
XLA Modules:
  0.0 95.5 jit_solution(7626018866319531428)
XLA Ops:
  0.7 3.0 %collective-permute-start.1 = (bf16[192,768]{1,0:T(8,128)(2,1)}, bf16[192,768]{1,0:T(8,128)(2,1)S(1)}, u32[]{:S(2)}, u32[]{:S(2)}) collective-permute-start(bf16[192,768]{1,0:T(8,128)(2,1)} %param.5), channel_id=1, source_target_pairs={{0,16},{8,24},{16,0},{24,8},{1,17},{9,25},{17,1},{25,9},{2,18},{10... | collective-permute-start | bytes 884744 | tf_op jit(solution)/shard_map/ppermute | solution.py:20
  3.7 2.6 %collective-permute-start.8 = (bf16[192,768]{1,0:T(8,128)(2,1)}, bf16[192,768]{1,0:T(8,128)(2,1)S(1)}, u32[]{:S(2)}, u32[]{:S(2)}) collective-permute-start(bf16[192,768]{1,0:T(8,128)(2,1)} %param.5), channel_id=1, source_target_pairs={{0,4},{4,0},{1,5},{5,1},{2,6},{6,2},{3,7},{7,3},{8,12},{12,8},{9,1... | collective-permute-start | bytes 884744 | tf_op jit(solution)/shard_map/ppermute | solution.py:20
  6.3 1.4 %collective-permute-start.6 = (bf16[192,768]{1,0:T(8,128)(2,1)}, bf16[192,768]{1,0:T(8,128)(2,1)S(1)}, u32[]{:S(2)}, u32[]{:S(2)}) collective-permute-start(bf16[192,768]{1,0:T(8,128)(2,1)} %param.5), channel_id=1, source_target_pairs={{0,24},{8,16},{16,8},{24,0},{1,25},{9,17},{17,9},{25,1},{2,26},{10... | collective-permute-start | bytes 884744 | tf_op jit(solution)/shard_map/ppermute | solution.py:20
  8.2 1.6 %collective-permute-start = (bf16[128,768]{1,0:T(8,128)(2,1)}, bf16[128,768]{1,0:T(8,128)(2,1)S(1)}, u32[]{:S(2)}, u32[]{:S(2)}) collective-permute-start(bf16[128,768]{1,0:T(8,128)(2,1)} %param.4), channel_id=1, source_target_pairs={{0,2},{2,0},{1,3},{3,1},{4,6},{6,4},{5,7},{7,5},{8,10},{10,8},{9,1... | collective-permute-start | bytes 589832 | tf_op jit(solution)/shard_map/ppermute | solution.py:20
  9.8 0.7 log_multiply_fusion
  10.5 0.7 multiply_bitcast_fusion.2
  11.2 5.6 %collective-permute-done = bf16[128,768]{1,0:T(8,128)(2,1)S(1)} collective-permute-done((bf16[128,768]{1,0:T(8,128)(2,1)}, bf16[128,768]{1,0:T(8,128)(2,1)S(1)}, u32[]{:S(2)}, u32[]{:S(2)}) %collective-permute-start) | collective-permute-done | bytes 196640 | tf_op jit(solution)/shard_map/ppermute | solution.py:20
  16.9 0.9 bitcast_dynamic-update-slice_fusion.12
  17.9 2.3 %collective-permute-start.2 = (bf16[128,768]{1,0:T(8,128)(2,1)S(1)}, bf16[128,768]{1,0:T(8,128)(2,1)S(1)}, u32[]{:S(2)}, u32[]{:S(2)}) collective-permute-start(bf16[128,768]{1,0:T(8,128)(2,1)S(1)} %copy-done.1), channel_id=1, source_target_pairs={{0,4},{4,0},{1,5},{5,1},{2,6},{6,2},{3,7},{7,3},{8,12},{12,8},{9,1... | collective-permute-start | bytes 589832 | tf_op jit(solution)/shard_map/ppermute | solution.py:20
  20.9 4.9 %collective-permute-start.9 = (bf16[192,768]{1,0:T(8,128)(2,1)S(1)}, bf16[192,768]{1,0:T(8,128)(2,1)S(1)}, u32[]{:S(2)}, u32[]{:S(2)}) collective-permute-start(bf16[192,768]{1,0:T(8,128)(2,1)S(1)} %collective-permute-done.8), channel_id=1, source_target_pairs={{0,24},{8,16},{16,8},{24,0},{1,25},{9,17},{17,9},{25,1},{2,26},{10... | collective-permute-start | bytes 884744 | tf_op jit(solution)/shard_map/ppermute | solution.py:20
  26.0 0.7 collective-permute-start.11
  26.9 1.7 %collective-permute-done.2 = bf16[128,768]{1,0:T(8,128)(2,1)S(1)} collective-permute-done((bf16[128,768]{1,0:T(8,128)(2,1)S(1)}, bf16[128,768]{1,0:T(8,128)(2,1)S(1)}, u32[]{:S(2)}, u32[]{:S(2)}) %collective-permute-start.2) | collective-permute-done | bytes 196640 | tf_op jit(solution)/shard_map/ppermute | solution.py:20
  29.2 2.9 %collective-permute-done.9 = bf16[192,768]{1,0:T(8,128)(2,1)S(1)} collective-permute-done((bf16[192,768]{1,0:T(8,128)(2,1)S(1)}, bf16[192,768]{1,0:T(8,128)(2,1)S(1)}, u32[]{:S(2)}, u32[]{:S(2)}) %collective-permute-start.9) | collective-permute-done | bytes 294944 | tf_op jit(solution)/shard_map/ppermute | solution.py:20
  32.2 2.1 %collective-permute-done.3 = bf16[128,768]{1,0:T(8,128)(2,1)S(1)} collective-permute-done((bf16[128,768]{1,0:T(8,128)(2,1)S(1)}, bf16[128,768]{1,0:T(8,128)(2,1)S(1)}, u32[]{:S(2)}, u32[]{:S(2)}) %collective-permute-start.3) | collective-permute-done | bytes 196640 | tf_op jit(solution)/shard_map/ppermute | solution.py:20
  35.4 1.5 %collective-permute-done.5 = bf16[2,2,128,768]{3,2,1,0:T(8,128)(2,1)S(1)} collective-permute-done((bf16[2,2,128,768]{3,2,1,0:T(8,128)(2,1)S(1)}, bf16[2,2,128,768]{3,2,1,0:T(8,128)(2,1)S(1)}, u32[]{:S(2)}, u32[]{:S(2)}) %collective-permute-start.5) | collective-permute-done | bytes 786464 | tf_op jit(solution)/shard_map/ppermute | solution.py:20
  36.9 1.4 %shard_map.68.refs_1_.tile1 = f32[1024,768]{1,0:T(8,128)S(1)} custom-call(bf16[1024,768]{1,0:T(8,128)(2,1)S(1)} %bitcast.96, bf16[768,768]{1,0:T(8,128)(2,1)S(1)} %bitcast.90), custom_call_target="tpu_custom_call" | custom-call | flops 1207959552 | bytes 5505024 | tf_op jit(solution)/shard_map/pallas_call | solution.py:122
  38.3 1.4 %shard_map.67.refs_0_.tile0 = f32[1024,768]{1,0:T(8,128)S(1)} custom-call(bf16[1024,768]{1,0:T(8,128)(2,1)S(1)} %bitcast.97, bf16[768,768]{1,0:T(8,128)(2,1)S(1)} %bitcast.93), custom_call_target="tpu_custom_call" | custom-call | flops 1207959552 | bytes 5505024 | tf_op jit(solution)/shard_map/pallas_call | solution.py:122
  39.8 1.3 %shard_map.69 = f32[8,128]{1,0:T(8,128)S(1)} custom-call(f32[1024,768]{1,0:T(8,128)S(1)} %shard_map.67.refs_0_.tile0, f32[1024,768]{1,0:T(8,128)S(1)} %shard_map.68.refs_1_.tile1, f32[12,128]{1,0:T(8,128)S(1)} %broadcast_in_dim.68.refs_2_), custom_call_target="tpu_custom_call" | custom-call | flops 9446400 | bytes 6297600 | tf_op jit(solution)/shard_map/pallas_call | solution.py:122
  41.1 1.4 %collective-permute-start.12 = (f32[8,128]{1,0:T(8,128)S(1)}, f32[8,128]{1,0:T(8,128)S(1)}, u32[]{:S(2)}, u32[]{:S(2)}) collective-permute-start(f32[8,128]{1,0:T(8,128)S(1)} %shard_map.69), channel_id=1, source_target_pairs={{0,3},{1,2},{2,1},{3,0},{4,7},{5,6},{6,5},{7,4},{8,11},{9,10},{10,... | collective-permute-start | bytes 12296 | tf_op jit(solution)/shard_map/ppermute | solution.py:20
  43.0 1.2 %collective-permute-done.12 = f32[8,128]{1,0:T(8,128)S(1)} collective-permute-done((f32[8,128]{1,0:T(8,128)S(1)}, f32[8,128]{1,0:T(8,128)S(1)}, u32[]{:S(2)}, u32[]{:S(2)}) %collective-permute-start.12) | collective-permute-done | bytes 4128 | tf_op jit(solution)/shard_map/ppermute | solution.py:20
  44.2 1.9 %collective-permute-done.13 = f32[8,128]{1,0:T(8,128)S(1)} collective-permute-done((f32[8,128]{1,0:T(8,128)S(1)}, f32[8,128]{1,0:T(8,128)S(1)}, u32[]{:S(2)}, u32[]{:S(2)}) %collective-permute-start.13) | collective-permute-done | bytes 4128 | tf_op jit(solution)/shard_map/ppermute | solution.py:20
  46.1 1.4 %shard_map.70 = f32[12,128]{1,0:T(8,128)S(1)} custom-call(f32[1024,768]{1,0:T(8,128)S(1)} %shard_map.67.refs_0_.tile0, f32[1024,768]{1,0:T(8,128)S(1)} %shard_map.68.refs_1_.tile1, f32[8,128]{1,0:T(8,128)S(1)} %add_subtract_fusion.5.refs_2_), custom_call_target="tpu_custom_call" | custom-call | flops 9443328 | bytes 6295552 | tf_op jit(solution)/shard_map/pallas_call | solution.py:122
  47.6 2.5 %collective-permute-start.15 = (f32[12,128]{1,0:T(8,128)S(1)}, f32[12,128]{1,0:T(8,128)S(1)}, u32[]{:S(2)}, u32[]{:S(2)}) collective-permute-start(f32[12,128]{1,0:T(8,128)S(1)} %shard_map.70), channel_id=1, source_target_pairs={{0,24},{8,16},{16,8},{24,0},{1,25},{9,17},{17,9},{25,1},{2,26},{10... | collective-permute-start | bytes 18440 | tf_op jit(solution)/shard_map/ppermute | solution.py:20
  51.1 1.1 %collective-permute-done.15 = f32[12,128]{1,0:T(8,128)S(1)} collective-permute-done((f32[12,128]{1,0:T(8,128)S(1)}, f32[12,128]{1,0:T(8,128)S(1)}, u32[]{:S(2)}, u32[]{:S(2)}) %collective-permute-start.15) | collective-permute-done | bytes 6176 | tf_op jit(solution)/shard_map/ppermute | solution.py:20
  52.2 1.5 %collective-permute-done.16 = f32[12,128]{1,0:T(8,128)S(1)} collective-permute-done((f32[12,128]{1,0:T(8,128)S(1)}, f32[12,128]{1,0:T(8,128)S(1)}, u32[]{:S(2)}, u32[]{:S(2)}) %collective-permute-start.16) | collective-permute-done | bytes 6176 | tf_op jit(solution)/shard_map/ppermute | solution.py:20
  54.3 1.3 %shard_map.71 = f32[8,128]{1,0:T(8,128)S(1)} custom-call(f32[1024,768]{1,0:T(8,128)S(1)} %shard_map.67.refs_0_.tile0, f32[1024,768]{1,0:T(8,128)S(1)} %shard_map.68.refs_1_.tile1, f32[12,128]{1,0:T(8,128)S(1)} %add_subtract_fusion.2.refs_2_), custom_call_target="tpu_custom_call" | custom-call | flops 9446400 | bytes 6297600 | tf_op jit(solution)/shard_map/pallas_call | solution.py:122
  56.1 1.4 %collective-permute-start.20 = (f32[8,128]{1,0:T(8,128)S(1)}, f32[8,128]{1,0:T(8,128)S(1)}, u32[]{:S(2)}, u32[]{:S(2)}) collective-permute-start(f32[8,128]{1,0:T(8,128)S(1)} %shard_map.71), channel_id=1, source_target_pairs={{0,1},{1,0},{2,3},{3,2},{4,5},{5,4},{6,7},{7,6},{8,9},{9,8},{10,11... | collective-permute-start | bytes 12296 | tf_op jit(solution)/shard_map/ppermute | solution.py:20
  57.5 1.2 %collective-permute-done.18 = f32[8,128]{1,0:T(8,128)S(1)} collective-permute-done((f32[8,128]{1,0:T(8,128)S(1)}, f32[8,128]{1,0:T(8,128)S(1)}, u32[]{:S(2)}, u32[]{:S(2)}) %collective-permute-start.18) | collective-permute-done | bytes 4128 | tf_op jit(solution)/shard_map/ppermute | solution.py:20
  59.4 1.4 %shard_map.72 = f32[12,128]{1,0:T(8,128)S(1)} custom-call(f32[1024,768]{1,0:T(8,128)S(1)} %shard_map.67.refs_0_.tile0, f32[1024,768]{1,0:T(8,128)S(1)} %shard_map.68.refs_1_.tile1, f32[8,128]{1,0:T(8,128)S(1)} %add_subtract_fusion.4.refs_2_), custom_call_target="tpu_custom_call" | custom-call | flops 9443328 | bytes 6295552 | tf_op jit(solution)/shard_map/pallas_call | solution.py:122
  60.8 1.6 %collective-permute-start.21 = (f32[12,128]{1,0:T(8,128)S(1)}, f32[12,128]{1,0:T(8,128)S(1)}, u32[]{:S(2)}, u32[]{:S(2)}) collective-permute-start(f32[12,128]{1,0:T(8,128)S(1)} %shard_map.72), channel_id=1, source_target_pairs={{0,24},{8,16},{16,8},{24,0},{1,25},{9,17},{17,9},{25,1},{2,26},{10... | collective-permute-start | bytes 18440 | tf_op jit(solution)/shard_map/ppermute | solution.py:20
  62.8 1.5 %collective-permute-start.23 = (f32[12,128]{1,0:T(8,128)S(1)}, f32[12,128]{1,0:T(8,128)S(1)}, u32[]{:S(2)}, u32[]{:S(2)}) collective-permute-start(f32[12,128]{1,0:T(8,128)S(1)} %shard_map.72), channel_id=1, source_target_pairs={{0,8},{8,0},{16,24},{24,16},{1,9},{9,1},{17,25},{25,17},{2,10},{10... | collective-permute-start | bytes 18440 | tf_op jit(solution)/shard_map/ppermute | solution.py:20
  64.3 1.1 %collective-permute-done.21 = f32[12,128]{1,0:T(8,128)S(1)} collective-permute-done((f32[12,128]{1,0:T(8,128)S(1)}, f32[12,128]{1,0:T(8,128)S(1)}, u32[]{:S(2)}, u32[]{:S(2)}) %collective-permute-start.21) | collective-permute-done | bytes 6176 | tf_op jit(solution)/shard_map/ppermute | solution.py:20
  66.5 1.3 %shard_map.73 = f32[8,128]{1,0:T(8,128)S(1)} custom-call(f32[1024,768]{1,0:T(8,128)S(1)} %shard_map.67.refs_0_.tile0, f32[1024,768]{1,0:T(8,128)S(1)} %shard_map.68.refs_1_.tile1, f32[12,128]{1,0:T(8,128)S(1)} %add_subtract_fusion.1.refs_2_), custom_call_target="tpu_custom_call" | custom-call | flops 9446400 | bytes 6297600 | tf_op jit(solution)/shard_map/pallas_call | solution.py:122
  68.4 1.4 %collective-permute-start.26 = (f32[8,128]{1,0:T(8,128)S(1)}, f32[8,128]{1,0:T(8,128)S(1)}, u32[]{:S(2)}, u32[]{:S(2)}) collective-permute-start(f32[8,128]{1,0:T(8,128)S(1)} %shard_map.73), channel_id=1, source_target_pairs={{0,1},{1,0},{2,3},{3,2},{4,5},{5,4},{6,7},{7,6},{8,9},{9,8},{10,11... | collective-permute-start | bytes 12296 | tf_op jit(solution)/shard_map/ppermute | solution.py:20
  69.8 1.2 %collective-permute-done.24 = f32[8,128]{1,0:T(8,128)S(1)} collective-permute-done((f32[8,128]{1,0:T(8,128)S(1)}, f32[8,128]{1,0:T(8,128)S(1)}, u32[]{:S(2)}, u32[]{:S(2)}) %collective-permute-start.24) | collective-permute-done | bytes 4128 | tf_op jit(solution)/shard_map/ppermute | solution.py:20
  70.9 0.7 collective-permute-done.25
  71.6 1.6 %shard_map.74 = f32[12,128]{1,0:T(8,128)S(1)} custom-call(f32[1024,768]{1,0:T(8,128)S(1)} %shard_map.67.refs_0_.tile0, f32[1024,768]{1,0:T(8,128)S(1)} %shard_map.68.refs_1_.tile1, f32[8,128]{1,0:T(8,128)S(1)} %add_subtract_fusion.3.refs_2_), custom_call_target="tpu_custom_call" | custom-call | flops 9443328 | bytes 6295552 | tf_op jit(solution)/shard_map/pallas_call | solution.py:122
  73.2 2.5 %collective-permute-start.27 = (f32[12,128]{1,0:T(8,128)S(1)}, f32[12,128]{1,0:T(8,128)S(1)}, u32[]{:S(2)}, u32[]{:S(2)}) collective-permute-start(f32[12,128]{1,0:T(8,128)S(1)} %shard_map.74), channel_id=1, source_target_pairs={{0,24},{8,16},{16,8},{24,0},{1,25},{9,17},{17,9},{25,1},{2,26},{10... | collective-permute-start | bytes 18440 | tf_op jit(solution)/shard_map/ppermute | solution.py:20
  76.8 1.1 %collective-permute-done.27 = f32[12,128]{1,0:T(8,128)S(1)} collective-permute-done((f32[12,128]{1,0:T(8,128)S(1)}, f32[12,128]{1,0:T(8,128)S(1)}, u32[]{:S(2)}, u32[]{:S(2)}) %collective-permute-start.27) | collective-permute-done | bytes 6176 | tf_op jit(solution)/shard_map/ppermute | solution.py:20
  77.8 1.6 %collective-permute-done.28 = f32[12,128]{1,0:T(8,128)S(1)} collective-permute-done((f32[12,128]{1,0:T(8,128)S(1)}, f32[12,128]{1,0:T(8,128)S(1)}, u32[]{:S(2)}, u32[]{:S(2)}) %collective-permute-start.28) | collective-permute-done | bytes 6176 | tf_op jit(solution)/shard_map/ppermute | solution.py:20
  79.9 0.7 shard_map.75
  81.2 1.4 %collective-permute-start.32 = (f32[2,4,128]{2,1,0:T(4,128)S(1)}, f32[2,4,128]{2,1,0:T(4,128)S(1)}, u32[]{:S(2)}, u32[]{:S(2)}) collective-permute-start(f32[2,4,128]{2,1,0:T(4,128)S(1)} %pad_maximum_fusion.3), channel_id=1, source_target_pairs={{0,1},{1,0},{2,3},{3,2},{4,5},{5,4},{6,7},{7,6},{8,9},{9,8},{10,11... | collective-permute-start | bytes 12296 | tf_op jit(solution)/shard_map/ppermute | solution.py:20
  82.6 1.2 %collective-permute-done.30 = f32[2,4,128]{2,1,0:T(4,128)S(1)} collective-permute-done((f32[2,4,128]{2,1,0:T(4,128)S(1)}, f32[2,4,128]{2,1,0:T(4,128)S(1)}, u32[]{:S(2)}, u32[]{:S(2)}) %collective-permute-start.30) | collective-permute-done | bytes 4128 | tf_op jit(solution)/shard_map/ppermute | solution.py:20
  84.4 0.9 shard_map.77
  85.4 0.9 shard_map.76
  86.9 0.8 collective-permute-done.33
  88.9 5.8 %collective-permute-done.34 = f16[128,768]{1,0:T(8,128)(2,1)S(1)} collective-permute-done((f16[128,768]{1,0:T(8,128)(2,1)S(1)}, f16[128,768]{1,0:T(8,128)(2,1)S(1)}, u32[]{:S(2)}, u32[]{:S(2)}) %collective-permute-start.34) | collective-permute-done | bytes 196640 | tf_op jit(solution)/shard_map/ppermute | solution.py:20
  94.7 0.8 fusion
  (80 shorter events, 13.4 us)
Async XLA Ops:
  0.6 17.2 %copy-start.1 = (bf16[128,768]{1,0:T(8,128)(2,1)S(1)}, bf16[128,768]{1,0:T(8,128)(2,1)}, u32[]{:S(2)}) copy-start(bf16[128,768]{1,0:T(8,128)(2,1)} %param.4) | copy-start | bytes 589828
  0.6 19.6 %copy-start.2 = (f32[768]{0:T(1024)S(1)}, f32[768]{0:T(1024)}, u32[]{:S(2)}) copy-start(f32[768]{0:T(1024)} %param.7) | copy-start | bytes 9220
  0.7 17.2 %collective-permute-start.1 = (bf16[192,768]{1,0:T(8,128)(2,1)}, bf16[192,768]{1,0:T(8,128)(2,1)S(1)}, u32[]{:S(2)}, u32[]{:S(2)}) collective-permute-start(bf16[192,768]{1,0:T(8,128)(2,1)} %param.5), channel_id=1, source_target_pairs={{0,16},{8,24},{16,0},{24,8},{1,17},{9,25},{17,1},{25,9},{2,18},{10... | collective-permute-start | bytes 884744 | tf_op jit(solution)/shard_map/ppermute | solution.py:20
  3.7 17.2 %collective-permute-start.8 = (bf16[192,768]{1,0:T(8,128)(2,1)}, bf16[192,768]{1,0:T(8,128)(2,1)S(1)}, u32[]{:S(2)}, u32[]{:S(2)}) collective-permute-start(bf16[192,768]{1,0:T(8,128)(2,1)} %param.5), channel_id=1, source_target_pairs={{0,4},{4,0},{1,5},{5,1},{2,6},{6,2},{3,7},{7,3},{8,12},{12,8},{9,1... | collective-permute-start | bytes 884744 | tf_op jit(solution)/shard_map/ppermute | solution.py:20
  6.3 19.5 %collective-permute-start.6 = (bf16[192,768]{1,0:T(8,128)(2,1)}, bf16[192,768]{1,0:T(8,128)(2,1)S(1)}, u32[]{:S(2)}, u32[]{:S(2)}) collective-permute-start(bf16[192,768]{1,0:T(8,128)(2,1)} %param.5), channel_id=1, source_target_pairs={{0,24},{8,16},{16,8},{24,0},{1,25},{9,17},{17,9},{25,1},{2,26},{10... | collective-permute-start | bytes 884744 | tf_op jit(solution)/shard_map/ppermute | solution.py:20
  7.7 18.3 %collective-permute-start.7 = (bf16[192,768]{1,0:T(8,128)(2,1)}, bf16[192,768]{1,0:T(8,128)(2,1)S(1)}, u32[]{:S(2)}, u32[]{:S(2)}) collective-permute-start(bf16[192,768]{1,0:T(8,128)(2,1)} %param.5), channel_id=1, source_target_pairs={{0,8},{8,0},{16,24},{24,16},{1,9},{9,1},{17,25},{25,17},{2,10},{10... | collective-permute-start | bytes 884744 | tf_op jit(solution)/shard_map/ppermute | solution.py:20
  8.2 8.6 %collective-permute-start = (bf16[128,768]{1,0:T(8,128)(2,1)}, bf16[128,768]{1,0:T(8,128)(2,1)S(1)}, u32[]{:S(2)}, u32[]{:S(2)}) collective-permute-start(bf16[128,768]{1,0:T(8,128)(2,1)} %param.4), channel_id=1, source_target_pairs={{0,2},{2,0},{1,3},{3,1},{4,6},{6,4},{5,7},{7,5},{8,10},{10,8},{9,1... | collective-permute-start | bytes 589832 | tf_op jit(solution)/shard_map/ppermute | solution.py:20
  17.9 10.8 %collective-permute-start.2 = (bf16[128,768]{1,0:T(8,128)(2,1)S(1)}, bf16[128,768]{1,0:T(8,128)(2,1)S(1)}, u32[]{:S(2)}, u32[]{:S(2)}) collective-permute-start(bf16[128,768]{1,0:T(8,128)(2,1)S(1)} %copy-done.1), channel_id=1, source_target_pairs={{0,4},{4,0},{1,5},{5,1},{2,6},{6,2},{3,7},{7,3},{8,12},{12,8},{9,1... | collective-permute-start | bytes 589832 | tf_op jit(solution)/shard_map/ppermute | solution.py:20
  20.2 14.2 %collective-permute-start.4 = (f32[768]{0:T(1024)S(1)}, f32[768]{0:T(1024)S(1)}, u32[]{:S(2)}, u32[]{:S(2)}) collective-permute-start(f32[768]{0:T(1024)S(1)} %copy-done.2), channel_id=1, source_target_pairs={{0,4},{4,0},{1,5},{5,1},{2,6},{6,2},{3,7},{7,3},{8,12},{12,8},{9,1... | collective-permute-start | bytes 9224 | tf_op jit(solution)/shard_map/ppermute | solution.py:20
  20.9 11.2 %collective-permute-start.9 = (bf16[192,768]{1,0:T(8,128)(2,1)S(1)}, bf16[192,768]{1,0:T(8,128)(2,1)S(1)}, u32[]{:S(2)}, u32[]{:S(2)}) collective-permute-start(bf16[192,768]{1,0:T(8,128)(2,1)S(1)} %collective-permute-done.8), channel_id=1, source_target_pairs={{0,24},{8,16},{16,8},{24,0},{1,25},{9,17},{17,9},{25,1},{2,26},{10... | collective-permute-start | bytes 884744 | tf_op jit(solution)/shard_map/ppermute | solution.py:20
  25.8 9.3 %collective-permute-start.10 = (bf16[192,768]{1,0:T(8,128)(2,1)S(1)}, bf16[192,768]{1,0:T(8,128)(2,1)S(1)}, u32[]{:S(2)}, u32[]{:S(2)}) collective-permute-start(bf16[192,768]{1,0:T(8,128)(2,1)S(1)} %collective-permute-done.8), channel_id=1, source_target_pairs={{0,16},{8,24},{16,0},{24,8},{1,17},{9,25},{17,1},{25,9},{2,18},{10... | collective-permute-start | bytes 884744 | tf_op jit(solution)/shard_map/ppermute | solution.py:20
  25.9 1.0 %copy-start = (bf16[192,768]{1,0:T(8,128)(2,1)S(1)}, bf16[192,768]{1,0:T(8,128)(2,1)}, u32[]{:S(2)}) copy-start(bf16[192,768]{1,0:T(8,128)(2,1)} %param.5) | copy-start | bytes 884740
  26.0 9.1 %collective-permute-start.11 = (bf16[192,768]{1,0:T(8,128)(2,1)S(1)}, bf16[192,768]{1,0:T(8,128)(2,1)S(1)}, u32[]{:S(2)}, u32[]{:S(2)}) collective-permute-start(bf16[192,768]{1,0:T(8,128)(2,1)S(1)} %collective-permute-done.8), channel_id=1, source_target_pairs={{0,8},{8,0},{16,24},{24,16},{1,9},{9,1},{17,25},{25,17},{2,10},{10... | collective-permute-start | bytes 884744 | tf_op jit(solution)/shard_map/ppermute | solution.py:20
  28.6 5.7 %collective-permute-start.3 = (bf16[128,768]{1,0:T(8,128)(2,1)S(1)}, bf16[128,768]{1,0:T(8,128)(2,1)S(1)}, u32[]{:S(2)}, u32[]{:S(2)}) collective-permute-start(bf16[128,768]{1,0:T(8,128)(2,1)S(1)} %collective-permute-done.2), channel_id=1, source_target_pairs={{0,2},{2,0},{1,3},{3,1},{4,6},{6,4},{5,7},{7,5},{8,10},{10,8},{9,1... | collective-permute-start | bytes 589832 | tf_op jit(solution)/shard_map/ppermute | solution.py:20
  34.5 2.4 %collective-permute-start.5 = (bf16[2,2,128,768]{3,2,1,0:T(8,128)(2,1)S(1)}, bf16[2,2,128,768]{3,2,1,0:T(8,128)(2,1)S(1)}, u32[]{:S(2)}, u32[]{:S(2)}) collective-permute-start(bf16[2,2,128,768]{3,2,1,0:T(8,128)(2,1)S(1)} %pad_maximum_fusion), channel_id=1, source_target_pairs={{0,1},{1,0},{2,3},{3,2},{4,5},{5,4},{6,7},{7,6},{8,9},{9,8},{10,11... | collective-permute-start | bytes 2359304 | tf_op jit(solution)/shard_map/ppermute | solution.py:20
  41.1 3.1 %collective-permute-start.12 = (f32[8,128]{1,0:T(8,128)S(1)}, f32[8,128]{1,0:T(8,128)S(1)}, u32[]{:S(2)}, u32[]{:S(2)}) collective-permute-start(f32[8,128]{1,0:T(8,128)S(1)} %shard_map.69), channel_id=1, source_target_pairs={{0,3},{1,2},{2,1},{3,0},{4,7},{5,6},{6,5},{7,4},{8,11},{9,10},{10,... | collective-permute-start | bytes 12296 | tf_op jit(solution)/shard_map/ppermute | solution.py:20
  42.5 3.6 %collective-permute-start.13 = (f32[8,128]{1,0:T(8,128)S(1)}, f32[8,128]{1,0:T(8,128)S(1)}, u32[]{:S(2)}, u32[]{:S(2)}) collective-permute-start(f32[8,128]{1,0:T(8,128)S(1)} %shard_map.69), channel_id=1, source_target_pairs={{0,2},{1,3},{2,0},{3,1},{4,6},{5,7},{6,4},{7,5},{8,10},{9,11},{10,... | collective-permute-start | bytes 12296 | tf_op jit(solution)/shard_map/ppermute | solution.py:20
  42.9 3.2 %collective-permute-start.14 = (f32[8,128]{1,0:T(8,128)S(1)}, f32[8,128]{1,0:T(8,128)S(1)}, u32[]{:S(2)}, u32[]{:S(2)}) collective-permute-start(f32[8,128]{1,0:T(8,128)S(1)} %shard_map.69), channel_id=1, source_target_pairs={{0,1},{1,0},{2,3},{3,2},{4,5},{5,4},{6,7},{7,6},{8,9},{9,8},{10,11... | collective-permute-start | bytes 12296 | tf_op jit(solution)/shard_map/ppermute | solution.py:20
  47.6 4.6 %collective-permute-start.15 = (f32[12,128]{1,0:T(8,128)S(1)}, f32[12,128]{1,0:T(8,128)S(1)}, u32[]{:S(2)}, u32[]{:S(2)}) collective-permute-start(f32[12,128]{1,0:T(8,128)S(1)} %shard_map.70), channel_id=1, source_target_pairs={{0,24},{8,16},{16,8},{24,0},{1,25},{9,17},{17,9},{25,1},{2,26},{10... | collective-permute-start | bytes 18440 | tf_op jit(solution)/shard_map/ppermute | solution.py:20
  50.1 3.7 %collective-permute-start.16 = (f32[12,128]{1,0:T(8,128)S(1)}, f32[12,128]{1,0:T(8,128)S(1)}, u32[]{:S(2)}, u32[]{:S(2)}) collective-permute-start(f32[12,128]{1,0:T(8,128)S(1)} %shard_map.70), channel_id=1, source_target_pairs={{0,16},{8,24},{16,0},{24,8},{1,17},{9,25},{17,1},{25,9},{2,18},{10... | collective-permute-start | bytes 18440 | tf_op jit(solution)/shard_map/ppermute | solution.py:20
  50.6 3.7 %collective-permute-start.17 = (f32[12,128]{1,0:T(8,128)S(1)}, f32[12,128]{1,0:T(8,128)S(1)}, u32[]{:S(2)}, u32[]{:S(2)}) collective-permute-start(f32[12,128]{1,0:T(8,128)S(1)} %shard_map.70), channel_id=1, source_target_pairs={{0,8},{8,0},{16,24},{24,16},{1,9},{9,1},{17,25},{25,17},{2,10},{10... | collective-permute-start | bytes 18440 | tf_op jit(solution)/shard_map/ppermute | solution.py:20
  55.6 3.1 %collective-permute-start.18 = (f32[8,128]{1,0:T(8,128)S(1)}, f32[8,128]{1,0:T(8,128)S(1)}, u32[]{:S(2)}, u32[]{:S(2)}) collective-permute-start(f32[8,128]{1,0:T(8,128)S(1)} %shard_map.71), channel_id=1, source_target_pairs={{0,3},{1,2},{2,1},{3,0},{4,7},{5,6},{6,5},{7,4},{8,11},{9,10},{10,... | collective-permute-start | bytes 12296 | tf_op jit(solution)/shard_map/ppermute | solution.py:20
  55.7 3.7 %collective-permute-start.19 = (f32[8,128]{1,0:T(8,128)S(1)}, f32[8,128]{1,0:T(8,128)S(1)}, u32[]{:S(2)}, u32[]{:S(2)}) collective-permute-start(f32[8,128]{1,0:T(8,128)S(1)} %shard_map.71), channel_id=1, source_target_pairs={{0,2},{1,3},{2,0},{3,1},{4,6},{5,7},{6,4},{7,5},{8,10},{9,11},{10,... | collective-permute-start | bytes 12296 | tf_op jit(solution)/shard_map/ppermute | solution.py:20
  56.1 3.2 %collective-permute-start.20 = (f32[8,128]{1,0:T(8,128)S(1)}, f32[8,128]{1,0:T(8,128)S(1)}, u32[]{:S(2)}, u32[]{:S(2)}) collective-permute-start(f32[8,128]{1,0:T(8,128)S(1)} %shard_map.71), channel_id=1, source_target_pairs={{0,1},{1,0},{2,3},{3,2},{4,5},{5,4},{6,7},{7,6},{8,9},{9,8},{10,11... | collective-permute-start | bytes 12296 | tf_op jit(solution)/shard_map/ppermute | solution.py:20
  60.8 4.7 %collective-permute-start.21 = (f32[12,128]{1,0:T(8,128)S(1)}, f32[12,128]{1,0:T(8,128)S(1)}, u32[]{:S(2)}, u32[]{:S(2)}) collective-permute-start(f32[12,128]{1,0:T(8,128)S(1)} %shard_map.72), channel_id=1, source_target_pairs={{0,24},{8,16},{16,8},{24,0},{1,25},{9,17},{17,9},{25,1},{2,26},{10... | collective-permute-start | bytes 18440 | tf_op jit(solution)/shard_map/ppermute | solution.py:20
  62.4 3.7 %collective-permute-start.22 = (f32[12,128]{1,0:T(8,128)S(1)}, f32[12,128]{1,0:T(8,128)S(1)}, u32[]{:S(2)}, u32[]{:S(2)}) collective-permute-start(f32[12,128]{1,0:T(8,128)S(1)} %shard_map.72), channel_id=1, source_target_pairs={{0,16},{8,24},{16,0},{24,8},{1,17},{9,25},{17,1},{25,9},{2,18},{10... | collective-permute-start | bytes 18440 | tf_op jit(solution)/shard_map/ppermute | solution.py:20
  62.8 3.7 %collective-permute-start.23 = (f32[12,128]{1,0:T(8,128)S(1)}, f32[12,128]{1,0:T(8,128)S(1)}, u32[]{:S(2)}, u32[]{:S(2)}) collective-permute-start(f32[12,128]{1,0:T(8,128)S(1)} %shard_map.72), channel_id=1, source_target_pairs={{0,8},{8,0},{16,24},{24,16},{1,9},{9,1},{17,25},{25,17},{2,10},{10... | collective-permute-start | bytes 18440 | tf_op jit(solution)/shard_map/ppermute | solution.py:20
  67.8 3.1 %collective-permute-start.24 = (f32[8,128]{1,0:T(8,128)S(1)}, f32[8,128]{1,0:T(8,128)S(1)}, u32[]{:S(2)}, u32[]{:S(2)}) collective-permute-start(f32[8,128]{1,0:T(8,128)S(1)} %shard_map.73), channel_id=1, source_target_pairs={{0,3},{1,2},{2,1},{3,0},{4,7},{5,6},{6,5},{7,4},{8,11},{9,10},{10,... | collective-permute-start | bytes 12296 | tf_op jit(solution)/shard_map/ppermute | solution.py:20
  67.9 3.7 %collective-permute-start.25 = (f32[8,128]{1,0:T(8,128)S(1)}, f32[8,128]{1,0:T(8,128)S(1)}, u32[]{:S(2)}, u32[]{:S(2)}) collective-permute-start(f32[8,128]{1,0:T(8,128)S(1)} %shard_map.73), channel_id=1, source_target_pairs={{0,2},{1,3},{2,0},{3,1},{4,6},{5,7},{6,4},{7,5},{8,10},{9,11},{10,... | collective-permute-start | bytes 12296 | tf_op jit(solution)/shard_map/ppermute | solution.py:20
  68.4 3.2 %collective-permute-start.26 = (f32[8,128]{1,0:T(8,128)S(1)}, f32[8,128]{1,0:T(8,128)S(1)}, u32[]{:S(2)}, u32[]{:S(2)}) collective-permute-start(f32[8,128]{1,0:T(8,128)S(1)} %shard_map.73), channel_id=1, source_target_pairs={{0,1},{1,0},{2,3},{3,2},{4,5},{5,4},{6,7},{7,6},{8,9},{9,8},{10,11... | collective-permute-start | bytes 12296 | tf_op jit(solution)/shard_map/ppermute | solution.py:20
  73.2 4.6 %collective-permute-start.27 = (f32[12,128]{1,0:T(8,128)S(1)}, f32[12,128]{1,0:T(8,128)S(1)}, u32[]{:S(2)}, u32[]{:S(2)}) collective-permute-start(f32[12,128]{1,0:T(8,128)S(1)} %shard_map.74), channel_id=1, source_target_pairs={{0,24},{8,16},{16,8},{24,0},{1,25},{9,17},{17,9},{25,1},{2,26},{10... | collective-permute-start | bytes 18440 | tf_op jit(solution)/shard_map/ppermute | solution.py:20
  75.7 3.7 %collective-permute-start.28 = (f32[12,128]{1,0:T(8,128)S(1)}, f32[12,128]{1,0:T(8,128)S(1)}, u32[]{:S(2)}, u32[]{:S(2)}) collective-permute-start(f32[12,128]{1,0:T(8,128)S(1)} %shard_map.74), channel_id=1, source_target_pairs={{0,16},{8,24},{16,0},{24,8},{1,17},{9,25},{17,1},{25,9},{2,18},{10... | collective-permute-start | bytes 18440 | tf_op jit(solution)/shard_map/ppermute | solution.py:20
  76.2 3.7 %collective-permute-start.29 = (f32[12,128]{1,0:T(8,128)S(1)}, f32[12,128]{1,0:T(8,128)S(1)}, u32[]{:S(2)}, u32[]{:S(2)}) collective-permute-start(f32[12,128]{1,0:T(8,128)S(1)} %shard_map.74), channel_id=1, source_target_pairs={{0,8},{8,0},{16,24},{24,16},{1,9},{9,1},{17,25},{25,17},{2,10},{10... | collective-permute-start | bytes 18440 | tf_op jit(solution)/shard_map/ppermute | solution.py:20
  80.6 3.1 %collective-permute-start.30 = (f32[2,4,128]{2,1,0:T(4,128)S(1)}, f32[2,4,128]{2,1,0:T(4,128)S(1)}, u32[]{:S(2)}, u32[]{:S(2)}) collective-permute-start(f32[2,4,128]{2,1,0:T(4,128)S(1)} %pad_maximum_fusion.3), channel_id=1, source_target_pairs={{0,3},{1,2},{2,1},{3,0},{4,7},{5,6},{6,5},{7,4},{8,11},{9,10},{10,... | collective-permute-start | bytes 12296 | tf_op jit(solution)/shard_map/ppermute | solution.py:20
  80.7 3.7 %collective-permute-start.31 = (f32[2,4,128]{2,1,0:T(4,128)S(1)}, f32[2,4,128]{2,1,0:T(4,128)S(1)}, u32[]{:S(2)}, u32[]{:S(2)}) collective-permute-start(f32[2,4,128]{2,1,0:T(4,128)S(1)} %pad_maximum_fusion.3), channel_id=1, source_target_pairs={{0,2},{1,3},{2,0},{3,1},{4,6},{5,7},{6,4},{7,5},{8,10},{9,11},{10,... | collective-permute-start | bytes 12296 | tf_op jit(solution)/shard_map/ppermute | solution.py:20
  81.2 3.2 %collective-permute-start.32 = (f32[2,4,128]{2,1,0:T(4,128)S(1)}, f32[2,4,128]{2,1,0:T(4,128)S(1)}, u32[]{:S(2)}, u32[]{:S(2)}) collective-permute-start(f32[2,4,128]{2,1,0:T(4,128)S(1)} %pad_maximum_fusion.3), channel_id=1, source_target_pairs={{0,1},{1,0},{2,3},{3,2},{4,5},{5,4},{6,7},{7,6},{8,9},{9,8},{10,11... | collective-permute-start | bytes 12296 | tf_op jit(solution)/shard_map/ppermute | solution.py:20
  85.3 2.4 %collective-permute-start.33 = (f32[256,768]{1,0:T(8,128)S(1)}, f32[256,768]{1,0:T(8,128)S(1)}, u32[]{:S(2)}, u32[]{:S(2)}) collective-permute-start(f32[256,768]{1,0:T(8,128)S(1)} %shard_map.77), channel_id=1, source_target_pairs={{0,1},{1,0},{2,3},{3,2},{4,5},{5,4},{6,7},{7,6},{8,9},{9,8},{10,11... | collective-permute-start | bytes 2359304 | tf_op jit(solution)/shard_map/ppermute | solution.py:20
  87.7 7.0 %collective-permute-start.34 = (f16[128,768]{1,0:T(8,128)(2,1)S(1)}, f16[128,768]{1,0:T(8,128)(2,1)S(1)}, u32[]{:S(2)}, u32[]{:S(2)}) collective-permute-start(f16[128,768]{1,0:T(8,128)(2,1)S(1)} %fusion.1), channel_id=1, source_target_pairs={{0,2},{2,0},{1,3},{3,1},{4,6},{6,4},{5,7},{7,5},{8,10},{10,8},{9,1... | collective-permute-start | bytes 589832 | tf_op jit(solution)/shard_map/ppermute | solution.py:20

commit v8 on v7

--- a/solution.py
+++ b/solution.py
@@ -49,24 +49,29 @@
     return x.reshape(x.shape[0] // 8, 8, LANES)
 
 
+def row_lse(tiles, side, at):
+    rows = pl.ds(at * LANES, LANES)
+
+    def blocks():
+        c = 0
+        for t in tiles:
+            for k in range(0, t.shape[1], LANES):
+                x = t[rows, k : k + LANES]
+                yield x if side is None else x + side[c : c + 1, :]
+                c += 1
+
+    m = functools.reduce(jnp.maximum, blocks())
+    s = sum(jnp.exp2(x - m) for x in blocks())
+    m, s = m.T, s.T
+    high = jnp.max(m, axis=0, keepdims=True)
+    s = jnp.sum(s * jnp.exp2(m - high), axis=0, keepdims=True)
+    return high + jnp.log2(s), high
+
+
 def row_kernel(n, *refs):
     tiles, (side, out, *peak) = refs[:n], refs[n:]
     for at in range(out.shape[0]):
-        rows = pl.ds(at * LANES, LANES)
-
-        def blocks():
-            c = 0
-            for t in tiles:
-                for k in range(0, t.shape[1], LANES):
-                    yield t[rows, k : k + LANES] + side[c : c + 1, :]
-                    c += 1
-
-        m = functools.reduce(jnp.maximum, blocks())
-        s = sum(jnp.exp2(x - m) for x in blocks())
-        m, s = m.T, s.T
-        high = jnp.max(m, axis=0, keepdims=True)
-        s = jnp.sum(s * jnp.exp2(m - high), axis=0, keepdims=True)
-        out[at : at + 1, :] = high + jnp.log2(s)
+        out[at : at + 1, :], high = row_lse(tiles, side, at)
         if peak:
             peak[0][at : at + 1, :] = high
 
@@ -143,17 +148,28 @@
     return call(functools.partial(col_kernel, len(tiles)), vector(sum(t.shape[1] for t in tiles)), tiles + [side], scratch)
 
 
-def dot_kernel(scaling, a, b, out):
-    for r in range(0, out.shape[0], 512):
-        part = lax.dot_general(
-            a[r : r + 512, :], b[...], (((1,), (1,)), ((), ())), preferred_element_type=jnp.float32
-        )
-        out[r : r + 512, :] = part * scaling
-
-
-def scaled_dot(a, b, scaling):
-    out_shape = jax.ShapeDtypeStruct((a.shape[0], b.shape[0]), jnp.float32)
-    return call(functools.partial(dot_kernel, scaling), out_shape, [a, b], flops=2 * a.size * b.shape[0])
+def first_kernel(scaling, a, b0, b1, t0, t1, out):
+    step = 2 * LANES
+
+    def multiply(r):
+        for b, t in ((b0, t0), (b1, t1)):
+            part = lax.dot_general(
+                a[r : r + step, :], b[...], (((1,), (1,)), ((), ())), preferred_element_type=jnp.float32
+            )
+            t[r : r + step, :] = part * scaling
+
+    multiply(0)
+    for r in range(0, a.shape[0], step):
+        if r + step < a.shape[0]:
+            multiply(r + step)
+        for at in range(r // LANES, (r + step) // LANES):
+            out[at : at + 1, :] = row_lse((t0, t1), None, at)[0]
+
+
+def first_pass(a, tools, scaling):
+    tiles = [jax.ShapeDtypeStruct((a.shape[0], b.shape[0]), jnp.float32) for b in tools]
+    flops = 2 * a.size * sum(b.shape[0] for b in tools)
+    return call(functools.partial(first_kernel, scaling), tiles + [vector(a.shape[0])], [a] + tools, flops=flops)
 
 
 def pairs(x, axes):
@@ -189,10 +205,10 @@
     log_query = jnp.log2(query_mass).reshape(2, nl, 2, bq).transpose(0, 2, 1, 3)
     log_query = by_place([log_query[0], log_query[1]], hi).reshape(-1, LANES)
 
-    tiles = [scaled_dot(tile_queries, t, scaling) for t in tile_tools]
-    tool_side = jnp.zeros_like(log_tool)
+    *tiles, part = first_pass(tile_queries, tile_tools, scaling)
     for sweep in range(ITERS):
-        (part,) = row_pass(tiles, tool_side, log_query.size)
+        if sweep:
+            (part,) = row_pass(tiles, tool_side, log_query.size)
         got = swaps(part, ("zl", "core"))
         query_side = log_query - lse_of(got[:1] + got[:0:-1])
         got = swaps(col_pass(tiles, query_side), "row")

time: 95.7 us -> 95.9 us (level)
  waiting for transfers between devices: 37.9 us -> 40.8 us
  starting transfers between devices: 37.4 us -> 35.6 us
    ppermute x35, waiting for transfers between devices: 37.9 us -> 40.8 us  [swap(): return lax.ppermute(x, axes, [(i, i ^ k) for i in range(n)])]
    ppermute x35, starting transfers between devices: 37.4 us -> 35.6 us  [swap(): return lax.ppermute(x, axes, [(i, i ^ k) for i in range(n)])]
    pallas_call x11 -> x9, Pallas kernels: 13.7 us -> 12.9 us  [call(): pl.pallas_call(kernel, out_shape=out_shape, in_specs=[vmem] * (len(args)...]
  transfers between devices with their start and end apart: 35 -> 35, of which waited for: 25 -> 26; matrix products, arithmetic and copies ran while one was open for 4% -> 4% of each run, Pallas kernels for 1% -> 1%
where the time goes in v8:
time: 95.9 us; the launch traced here: 95.7 us
  waiting for transfers between devices  40.8 us (43%)
  starting transfers between devices  35.6 us (37%)
  Pallas kernels  12.9 us (13%)
  other arithmetic  3.09 us (3%)
  local copies, waits for them, and re-layouts  2.45 us (3%)
    ppermute x35, waiting for transfers between devices, swap(): return lax.ppermute(x, axes, [(i, i ^ k) for i in range(n)])  40.8 us
    ppermute x35, starting transfers between devices, swap(): return lax.ppermute(x, axes, [(i, i ^ k) for i in range(n)])  35.6 us
    pallas_call x9, Pallas kernels, call(): pl.pallas_call(kernel, out_shape=out_shape, in_specs=[vmem] * (len(args)...  12.9 us
  transfers between devices with their start and end apart: 35, of which 26 were waited for; matrix products, arithmetic and copies ran while one was open for 4% of the time, Pallas kernels for 1%

profile of v8, /device:TPU:0, one launch (start us, length us, event | category | flops | bytes accessed | tf_op | source)
XLA Modules:
  0.0 95.7 jit_solution(4619560415256798195)
XLA Ops:
  0.7 3.0 %collective-permute-start.1 = (bf16[192,768]{1,0:T(8,128)(2,1)}, bf16[192,768]{1,0:T(8,128)(2,1)S(1)}, u32[]{:S(2)}, u32[]{:S(2)}) collective-permute-start(bf16[192,768]{1,0:T(8,128)(2,1)} %param.5), channel_id=1, source_target_pairs={{0,16},{8,24},{16,0},{24,8},{1,17},{9,25},{17,1},{25,9},{2,18},{10... | collective-permute-start | bytes 884744 | tf_op jit(solution)/shard_map/ppermute | solution.py:20
  3.7 1.4 %collective-permute-start.6 = (bf16[192,768]{1,0:T(8,128)(2,1)}, bf16[192,768]{1,0:T(8,128)(2,1)S(1)}, u32[]{:S(2)}, u32[]{:S(2)}) collective-permute-start(bf16[192,768]{1,0:T(8,128)(2,1)} %param.5), channel_id=1, source_target_pairs={{0,24},{8,16},{16,8},{24,0},{1,25},{9,17},{17,9},{25,1},{2,26},{10... | collective-permute-start | bytes 884744 | tf_op jit(solution)/shard_map/ppermute | solution.py:20
  5.2 3.0 %collective-permute-start.8 = (bf16[192,768]{1,0:T(8,128)(2,1)}, bf16[192,768]{1,0:T(8,128)(2,1)S(1)}, u32[]{:S(2)}, u32[]{:S(2)}) collective-permute-start(bf16[192,768]{1,0:T(8,128)(2,1)} %param.5), channel_id=1, source_target_pairs={{0,4},{4,0},{1,5},{5,1},{2,6},{6,2},{3,7},{7,3},{8,12},{12,8},{9,1... | collective-permute-start | bytes 884744 | tf_op jit(solution)/shard_map/ppermute | solution.py:20
  8.2 1.6 %collective-permute-start = (bf16[128,768]{1,0:T(8,128)(2,1)}, bf16[128,768]{1,0:T(8,128)(2,1)S(1)}, u32[]{:S(2)}, u32[]{:S(2)}) collective-permute-start(bf16[128,768]{1,0:T(8,128)(2,1)} %param.4), channel_id=1, source_target_pairs={{0,2},{2,0},{1,3},{3,1},{4,6},{6,4},{5,7},{7,5},{8,10},{10,8},{9,1... | collective-permute-start | bytes 589832 | tf_op jit(solution)/shard_map/ppermute | solution.py:20
  9.8 0.7 log_multiply_fusion
  10.5 0.7 multiply_bitcast_fusion.2
  11.2 7.0 %collective-permute-done = bf16[128,768]{1,0:T(8,128)(2,1)S(1)} collective-permute-done((bf16[128,768]{1,0:T(8,128)(2,1)}, bf16[128,768]{1,0:T(8,128)(2,1)S(1)}, u32[]{:S(2)}, u32[]{:S(2)}) %collective-permute-start) | collective-permute-done | bytes 196640 | tf_op jit(solution)/shard_map/ppermute | solution.py:20
  18.3 0.9 bitcast_dynamic-update-slice_fusion.12
  19.3 2.3 %collective-permute-start.2 = (bf16[128,768]{1,0:T(8,128)(2,1)S(1)}, bf16[128,768]{1,0:T(8,128)(2,1)S(1)}, u32[]{:S(2)}, u32[]{:S(2)}) collective-permute-start(bf16[128,768]{1,0:T(8,128)(2,1)S(1)} %copy-done.1), channel_id=1, source_target_pairs={{0,4},{4,0},{1,5},{5,1},{2,6},{6,2},{3,7},{7,3},{8,12},{12,8},{9,1... | collective-permute-start | bytes 589832 | tf_op jit(solution)/shard_map/ppermute | solution.py:20
  22.3 2.4 %collective-permute-start.9 = (bf16[192,768]{1,0:T(8,128)(2,1)S(1)}, bf16[192,768]{1,0:T(8,128)(2,1)S(1)}, u32[]{:S(2)}, u32[]{:S(2)}) collective-permute-start(bf16[192,768]{1,0:T(8,128)(2,1)S(1)} %collective-permute-done.8), channel_id=1, source_target_pairs={{0,24},{8,16},{16,8},{24,0},{1,25},{9,17},{17,9},{25,1},{2,26},{10... | collective-permute-start | bytes 884744 | tf_op jit(solution)/shard_map/ppermute | solution.py:20
  26.3 3.2 %collective-permute-done.2 = bf16[128,768]{1,0:T(8,128)(2,1)S(1)} collective-permute-done((bf16[128,768]{1,0:T(8,128)(2,1)S(1)}, bf16[128,768]{1,0:T(8,128)(2,1)S(1)}, u32[]{:S(2)}, u32[]{:S(2)}) %collective-permute-start.2) | collective-permute-done | bytes 196640 | tf_op jit(solution)/shard_map/ppermute | solution.py:20
  29.5 0.7 collective-permute-start.3
  30.3 2.6 %collective-permute-done.9 = bf16[192,768]{1,0:T(8,128)(2,1)S(1)} collective-permute-done((bf16[192,768]{1,0:T(8,128)(2,1)S(1)}, bf16[192,768]{1,0:T(8,128)(2,1)S(1)}, u32[]{:S(2)}, u32[]{:S(2)}) %collective-permute-start.9) | collective-permute-done | bytes 294944 | tf_op jit(solution)/shard_map/ppermute | solution.py:20
  33.0 2.2 %collective-permute-done.3 = bf16[128,768]{1,0:T(8,128)(2,1)S(1)} collective-permute-done((bf16[128,768]{1,0:T(8,128)(2,1)S(1)}, bf16[128,768]{1,0:T(8,128)(2,1)S(1)}, u32[]{:S(2)}, u32[]{:S(2)}) %collective-permute-start.3) | collective-permute-done | bytes 196640 | tf_op jit(solution)/shard_map/ppermute | solution.py:20
  36.4 1.4 %collective-permute-done.5 = bf16[2,2,128,768]{3,2,1,0:T(8,128)(2,1)S(1)} collective-permute-done((bf16[2,2,128,768]{3,2,1,0:T(8,128)(2,1)S(1)}, bf16[2,2,128,768]{3,2,1,0:T(8,128)(2,1)S(1)}, u32[]{:S(2)}, u32[]{:S(2)}) %collective-permute-start.5) | collective-permute-done | bytes 786464 | tf_op jit(solution)/shard_map/ppermute | solution.py:20
  37.9 3.3 %shard_map.67 = (f32[1024,768]{1,0:T(8,128)S(1)}, f32[1024,768]{1,0:T(8,128)S(1)}, f32[8,128]{1,0:T(8,128)S(1)}) custom-call(bf16[1024,768]{1,0:T(8,128)(2,1)S(1)} %bitcast.98, bf16[768,768]{1,0:T(8,128)(2,1)S(1)} %bitcast.93, bf16[768,768]{1,0:T(8,128)(2,1)S(1)} %bitcast.90), custom_call_target="tpu_custom_call" | custom-call | flops 2415919104 | bytes 7864320 | tf_op jit(solution)/shard_map/pallas_call | solution.py:127
  41.2 1.5 %collective-permute-start.12 = (f32[8,128]{1,0:T(8,128)S(1)}, f32[8,128]{1,0:T(8,128)S(1)}, u32[]{:S(2)}, u32[]{:S(2)}) collective-permute-start(f32[8,128]{1,0:T(8,128)S(1)} %get-tuple-element.25), channel_id=1, source_target_pairs={{0,3},{1,2},{2,1},{3,0},{4,7},{5,6},{6,5},{7,4},{8,11},{9,10},{10,... | collective-permute-start | bytes 12296 | tf_op jit(solution)/shard_map/ppermute | solution.py:20
  43.1 1.1 %collective-permute-done.12 = f32[8,128]{1,0:T(8,128)S(1)} collective-permute-done((f32[8,128]{1,0:T(8,128)S(1)}, f32[8,128]{1,0:T(8,128)S(1)}, u32[]{:S(2)}, u32[]{:S(2)}) %collective-permute-start.12) | collective-permute-done | bytes 4128 | tf_op jit(solution)/shard_map/ppermute | solution.py:20
  44.3 2.1 %collective-permute-done.13 = f32[8,128]{1,0:T(8,128)S(1)} collective-permute-done((f32[8,128]{1,0:T(8,128)S(1)}, f32[8,128]{1,0:T(8,128)S(1)}, u32[]{:S(2)}, u32[]{:S(2)}) %collective-permute-start.13) | collective-permute-done | bytes 4128 | tf_op jit(solution)/shard_map/ppermute | solution.py:20
  46.4 1.4 %shard_map.68 = f32[12,128]{1,0:T(8,128)S(1)} custom-call(f32[1024,768]{1,0:T(8,128)S(1)} %get-tuple-element.22.refs_0_.tile0, f32[1024,768]{1,0:T(8,128)S(1)} %get-tuple-element.23.refs_1_.tile1, f32[8,128]{1,0:T(8,128)S(1)} %add_subtract_fusion.5.refs_2_), custom_call_target="tpu_custom_call" | custom-call | flops 9443328 | bytes 6295552 | tf_op jit(solution)/shard_map/pallas_call | solution.py:127
  47.8 2.5 %collective-permute-start.15 = (f32[12,128]{1,0:T(8,128)S(1)}, f32[12,128]{1,0:T(8,128)S(1)}, u32[]{:S(2)}, u32[]{:S(2)}) collective-permute-start(f32[12,128]{1,0:T(8,128)S(1)} %shard_map.68), channel_id=1, source_target_pairs={{0,24},{8,16},{16,8},{24,0},{1,25},{9,17},{17,9},{25,1},{2,26},{10... | collective-permute-start | bytes 18440 | tf_op jit(solution)/shard_map/ppermute | solution.py:20
  51.3 1.1 %collective-permute-done.15 = f32[12,128]{1,0:T(8,128)S(1)} collective-permute-done((f32[12,128]{1,0:T(8,128)S(1)}, f32[12,128]{1,0:T(8,128)S(1)}, u32[]{:S(2)}, u32[]{:S(2)}) %collective-permute-start.15) | collective-permute-done | bytes 6176 | tf_op jit(solution)/shard_map/ppermute | solution.py:20
  52.4 1.5 %collective-permute-done.16 = f32[12,128]{1,0:T(8,128)S(1)} collective-permute-done((f32[12,128]{1,0:T(8,128)S(1)}, f32[12,128]{1,0:T(8,128)S(1)}, u32[]{:S(2)}, u32[]{:S(2)}) %collective-permute-start.16) | collective-permute-done | bytes 6176 | tf_op jit(solution)/shard_map/ppermute | solution.py:20
  54.5 1.3 %shard_map.69 = f32[8,128]{1,0:T(8,128)S(1)} custom-call(f32[1024,768]{1,0:T(8,128)S(1)} %get-tuple-element.22.refs_0_.tile0, f32[1024,768]{1,0:T(8,128)S(1)} %get-tuple-element.23.refs_1_.tile1, f32[12,128]{1,0:T(8,128)S(1)} %add_subtract_fusion.2.refs_2_), custom_call_target="tpu_custom_call" | custom-call | flops 9446400 | bytes 6297600 | tf_op jit(solution)/shard_map/pallas_call | solution.py:127
  56.3 1.5 %collective-permute-start.20 = (f32[8,128]{1,0:T(8,128)S(1)}, f32[8,128]{1,0:T(8,128)S(1)}, u32[]{:S(2)}, u32[]{:S(2)}) collective-permute-start(f32[8,128]{1,0:T(8,128)S(1)} %shard_map.69), channel_id=1, source_target_pairs={{0,1},{1,0},{2,3},{3,2},{4,5},{5,4},{6,7},{7,6},{8,9},{9,8},{10,11... | collective-permute-start | bytes 12296 | tf_op jit(solution)/shard_map/ppermute | solution.py:20
  57.7 1.2 %collective-permute-done.18 = f32[8,128]{1,0:T(8,128)S(1)} collective-permute-done((f32[8,128]{1,0:T(8,128)S(1)}, f32[8,128]{1,0:T(8,128)S(1)}, u32[]{:S(2)}, u32[]{:S(2)}) %collective-permute-start.18) | collective-permute-done | bytes 4128 | tf_op jit(solution)/shard_map/ppermute | solution.py:20
  58.9 0.7 collective-permute-done.19
  59.6 1.4 %shard_map.70 = f32[12,128]{1,0:T(8,128)S(1)} custom-call(f32[1024,768]{1,0:T(8,128)S(1)} %get-tuple-element.22.refs_0_.tile0, f32[1024,768]{1,0:T(8,128)S(1)} %get-tuple-element.23.refs_1_.tile1, f32[8,128]{1,0:T(8,128)S(1)} %add_subtract_fusion.4.refs_2_), custom_call_target="tpu_custom_call" | custom-call | flops 9443328 | bytes 6295552 | tf_op jit(solution)/shard_map/pallas_call | solution.py:127
  61.0 1.6 %collective-permute-start.21 = (f32[12,128]{1,0:T(8,128)S(1)}, f32[12,128]{1,0:T(8,128)S(1)}, u32[]{:S(2)}, u32[]{:S(2)}) collective-permute-start(f32[12,128]{1,0:T(8,128)S(1)} %shard_map.70), channel_id=1, source_target_pairs={{0,24},{8,16},{16,8},{24,0},{1,25},{9,17},{17,9},{25,1},{2,26},{10... | collective-permute-start | bytes 18440 | tf_op jit(solution)/shard_map/ppermute | solution.py:20
  63.1 1.5 %collective-permute-start.23 = (f32[12,128]{1,0:T(8,128)S(1)}, f32[12,128]{1,0:T(8,128)S(1)}, u32[]{:S(2)}, u32[]{:S(2)}) collective-permute-start(f32[12,128]{1,0:T(8,128)S(1)} %shard_map.70), channel_id=1, source_target_pairs={{0,8},{8,0},{16,24},{24,16},{1,9},{9,1},{17,25},{25,17},{2,10},{10... | collective-permute-start | bytes 18440 | tf_op jit(solution)/shard_map/ppermute | solution.py:20
  64.6 1.1 %collective-permute-done.21 = f32[12,128]{1,0:T(8,128)S(1)} collective-permute-done((f32[12,128]{1,0:T(8,128)S(1)}, f32[12,128]{1,0:T(8,128)S(1)}, u32[]{:S(2)}, u32[]{:S(2)}) %collective-permute-start.21) | collective-permute-done | bytes 6176 | tf_op jit(solution)/shard_map/ppermute | solution.py:20
  66.8 1.3 %shard_map.71 = f32[8,128]{1,0:T(8,128)S(1)} custom-call(f32[1024,768]{1,0:T(8,128)S(1)} %get-tuple-element.22.refs_0_.tile0, f32[1024,768]{1,0:T(8,128)S(1)} %get-tuple-element.23.refs_1_.tile1, f32[12,128]{1,0:T(8,128)S(1)} %add_subtract_fusion.1.refs_2_), custom_call_target="tpu_custom_call" | custom-call | flops 9446400 | bytes 6297600 | tf_op jit(solution)/shard_map/pallas_call | solution.py:127
  68.5 1.5 %collective-permute-start.26 = (f32[8,128]{1,0:T(8,128)S(1)}, f32[8,128]{1,0:T(8,128)S(1)}, u32[]{:S(2)}, u32[]{:S(2)}) collective-permute-start(f32[8,128]{1,0:T(8,128)S(1)} %shard_map.71), channel_id=1, source_target_pairs={{0,1},{1,0},{2,3},{3,2},{4,5},{5,4},{6,7},{7,6},{8,9},{9,8},{10,11... | collective-permute-start | bytes 12296 | tf_op jit(solution)/shard_map/ppermute | solution.py:20
  70.0 1.2 %collective-permute-done.24 = f32[8,128]{1,0:T(8,128)S(1)} collective-permute-done((f32[8,128]{1,0:T(8,128)S(1)}, f32[8,128]{1,0:T(8,128)S(1)}, u32[]{:S(2)}, u32[]{:S(2)}) %collective-permute-start.24) | collective-permute-done | bytes 4128 | tf_op jit(solution)/shard_map/ppermute | solution.py:20
  71.2 0.7 collective-permute-done.25
  71.9 1.6 %shard_map.72 = f32[12,128]{1,0:T(8,128)S(1)} custom-call(f32[1024,768]{1,0:T(8,128)S(1)} %get-tuple-element.22.refs_0_.tile0, f32[1024,768]{1,0:T(8,128)S(1)} %get-tuple-element.23.refs_1_.tile1, f32[8,128]{1,0:T(8,128)S(1)} %add_subtract_fusion.3.refs_2_), custom_call_target="tpu_custom_call" | custom-call | flops 9443328 | bytes 6295552 | tf_op jit(solution)/shard_map/pallas_call | solution.py:127
  73.5 2.5 %collective-permute-start.27 = (f32[12,128]{1,0:T(8,128)S(1)}, f32[12,128]{1,0:T(8,128)S(1)}, u32[]{:S(2)}, u32[]{:S(2)}) collective-permute-start(f32[12,128]{1,0:T(8,128)S(1)} %shard_map.72), channel_id=1, source_target_pairs={{0,24},{8,16},{16,8},{24,0},{1,25},{9,17},{17,9},{25,1},{2,26},{10... | collective-permute-start | bytes 18440 | tf_op jit(solution)/shard_map/ppermute | solution.py:20
  77.0 1.1 %collective-permute-done.27 = f32[12,128]{1,0:T(8,128)S(1)} collective-permute-done((f32[12,128]{1,0:T(8,128)S(1)}, f32[12,128]{1,0:T(8,128)S(1)}, u32[]{:S(2)}, u32[]{:S(2)}) %collective-permute-start.27) | collective-permute-done | bytes 6176 | tf_op jit(solution)/shard_map/ppermute | solution.py:20
  78.1 1.5 %collective-permute-done.28 = f32[12,128]{1,0:T(8,128)S(1)} collective-permute-done((f32[12,128]{1,0:T(8,128)S(1)}, f32[12,128]{1,0:T(8,128)S(1)}, u32[]{:S(2)}, u32[]{:S(2)}) %collective-permute-start.28) | collective-permute-done | bytes 6176 | tf_op jit(solution)/shard_map/ppermute | solution.py:20
  80.1 0.7 shard_map.73
  81.3 1.5 %collective-permute-start.32 = (f32[2,4,128]{2,1,0:T(4,128)S(1)}, f32[2,4,128]{2,1,0:T(4,128)S(1)}, u32[]{:S(2)}, u32[]{:S(2)}) collective-permute-start(f32[2,4,128]{2,1,0:T(4,128)S(1)} %pad_maximum_fusion.3), channel_id=1, source_target_pairs={{0,1},{1,0},{2,3},{3,2},{4,5},{5,4},{6,7},{7,6},{8,9},{9,8},{10,11... | collective-permute-start | bytes 12296 | tf_op jit(solution)/shard_map/ppermute | solution.py:20
  82.8 1.2 %collective-permute-done.30 = f32[2,4,128]{2,1,0:T(4,128)S(1)} collective-permute-done((f32[2,4,128]{2,1,0:T(4,128)S(1)}, f32[2,4,128]{2,1,0:T(4,128)S(1)}, u32[]{:S(2)}, u32[]{:S(2)}) %collective-permute-start.30) | collective-permute-done | bytes 4128 | tf_op jit(solution)/shard_map/ppermute | solution.py:20
  84.0 0.7 collective-permute-done.31
  84.6 0.9 shard_map.75
  85.6 0.9 shard_map.74
  87.1 0.8 collective-permute-done.33
  89.2 5.8 %collective-permute-done.34 = f16[128,768]{1,0:T(8,128)(2,1)S(1)} collective-permute-done((f16[128,768]{1,0:T(8,128)(2,1)S(1)}, f16[128,768]{1,0:T(8,128)(2,1)S(1)}, u32[]{:S(2)}, u32[]{:S(2)}) %collective-permute-start.34) | collective-permute-done | bytes 196640 | tf_op jit(solution)/shard_map/ppermute | solution.py:20
  94.9 0.7 fusion
  (77 shorter events, 12.1 us)
Async XLA Ops:
  0.6 18.6 %copy-start.1 = (bf16[128,768]{1,0:T(8,128)(2,1)S(1)}, bf16[128,768]{1,0:T(8,128)(2,1)}, u32[]{:S(2)}) copy-start(bf16[128,768]{1,0:T(8,128)(2,1)} %param.4) | copy-start | bytes 589828
  0.6 21.0 %copy-start.2 = (f32[768]{0:T(1024)S(1)}, f32[768]{0:T(1024)}, u32[]{:S(2)}) copy-start(f32[768]{0:T(1024)} %param.7) | copy-start | bytes 9220
  0.7 18.6 %collective-permute-start.1 = (bf16[192,768]{1,0:T(8,128)(2,1)}, bf16[192,768]{1,0:T(8,128)(2,1)S(1)}, u32[]{:S(2)}, u32[]{:S(2)}) collective-permute-start(bf16[192,768]{1,0:T(8,128)(2,1)} %param.5), channel_id=1, source_target_pairs={{0,16},{8,24},{16,0},{24,8},{1,17},{9,25},{17,1},{25,9},{2,18},{10... | collective-permute-start | bytes 884744 | tf_op jit(solution)/shard_map/ppermute | solution.py:20
  3.7 21.0 %collective-permute-start.6 = (bf16[192,768]{1,0:T(8,128)(2,1)}, bf16[192,768]{1,0:T(8,128)(2,1)S(1)}, u32[]{:S(2)}, u32[]{:S(2)}) collective-permute-start(bf16[192,768]{1,0:T(8,128)(2,1)} %param.5), channel_id=1, source_target_pairs={{0,24},{8,16},{16,8},{24,0},{1,25},{9,17},{17,9},{25,1},{2,26},{10... | collective-permute-start | bytes 884744 | tf_op jit(solution)/shard_map/ppermute | solution.py:20
  5.1 20.3 %collective-permute-start.7 = (bf16[192,768]{1,0:T(8,128)(2,1)}, bf16[192,768]{1,0:T(8,128)(2,1)S(1)}, u32[]{:S(2)}, u32[]{:S(2)}) collective-permute-start(bf16[192,768]{1,0:T(8,128)(2,1)} %param.5), channel_id=1, source_target_pairs={{0,8},{8,0},{16,24},{24,16},{1,9},{9,1},{17,25},{25,17},{2,10},{10... | collective-permute-start | bytes 884744 | tf_op jit(solution)/shard_map/ppermute | solution.py:20
  5.2 17.0 %collective-permute-start.8 = (bf16[192,768]{1,0:T(8,128)(2,1)}, bf16[192,768]{1,0:T(8,128)(2,1)S(1)}, u32[]{:S(2)}, u32[]{:S(2)}) collective-permute-start(bf16[192,768]{1,0:T(8,128)(2,1)} %param.5), channel_id=1, source_target_pairs={{0,4},{4,0},{1,5},{5,1},{2,6},{6,2},{3,7},{7,3},{8,12},{12,8},{9,1... | collective-permute-start | bytes 884744 | tf_op jit(solution)/shard_map/ppermute | solution.py:20
  8.2 10.0 %collective-permute-start = (bf16[128,768]{1,0:T(8,128)(2,1)}, bf16[128,768]{1,0:T(8,128)(2,1)S(1)}, u32[]{:S(2)}, u32[]{:S(2)}) collective-permute-start(bf16[128,768]{1,0:T(8,128)(2,1)} %param.4), channel_id=1, source_target_pairs={{0,2},{2,0},{1,3},{3,1},{4,6},{6,4},{5,7},{7,5},{8,10},{10,8},{9,1... | collective-permute-start | bytes 589832 | tf_op jit(solution)/shard_map/ppermute | solution.py:20
  19.3 10.3 %collective-permute-start.2 = (bf16[128,768]{1,0:T(8,128)(2,1)S(1)}, bf16[128,768]{1,0:T(8,128)(2,1)S(1)}, u32[]{:S(2)}, u32[]{:S(2)}) collective-permute-start(bf16[128,768]{1,0:T(8,128)(2,1)S(1)} %copy-done.1), channel_id=1, source_target_pairs={{0,4},{4,0},{1,5},{5,1},{2,6},{6,2},{3,7},{7,3},{8,12},{12,8},{9,1... | collective-permute-start | bytes 589832 | tf_op jit(solution)/shard_map/ppermute | solution.py:20
  21.6 13.7 %collective-permute-start.4 = (f32[768]{0:T(1024)S(1)}, f32[768]{0:T(1024)S(1)}, u32[]{:S(2)}, u32[]{:S(2)}) collective-permute-start(f32[768]{0:T(1024)S(1)} %copy-done.2), channel_id=1, source_target_pairs={{0,4},{4,0},{1,5},{5,1},{2,6},{6,2},{3,7},{7,3},{8,12},{12,8},{9,1... | collective-permute-start | bytes 9224 | tf_op jit(solution)/shard_map/ppermute | solution.py:20
  22.3 10.6 %collective-permute-start.9 = (bf16[192,768]{1,0:T(8,128)(2,1)S(1)}, bf16[192,768]{1,0:T(8,128)(2,1)S(1)}, u32[]{:S(2)}, u32[]{:S(2)}) collective-permute-start(bf16[192,768]{1,0:T(8,128)(2,1)S(1)} %collective-permute-done.8), channel_id=1, source_target_pairs={{0,24},{8,16},{16,8},{24,0},{1,25},{9,17},{17,9},{25,1},{2,26},{10... | collective-permute-start | bytes 884744 | tf_op jit(solution)/shard_map/ppermute | solution.py:20
  24.7 11.3 %collective-permute-start.10 = (bf16[192,768]{1,0:T(8,128)(2,1)S(1)}, bf16[192,768]{1,0:T(8,128)(2,1)S(1)}, u32[]{:S(2)}, u32[]{:S(2)}) collective-permute-start(bf16[192,768]{1,0:T(8,128)(2,1)S(1)} %collective-permute-done.8), channel_id=1, source_target_pairs={{0,16},{8,24},{16,0},{24,8},{1,17},{9,25},{17,1},{25,9},{2,18},{10... | collective-permute-start | bytes 884744 | tf_op jit(solution)/shard_map/ppermute | solution.py:20
  25.3 1.0 %copy-start = (bf16[192,768]{1,0:T(8,128)(2,1)S(1)}, bf16[192,768]{1,0:T(8,128)(2,1)}, u32[]{:S(2)}) copy-start(bf16[192,768]{1,0:T(8,128)(2,1)} %param.5) | copy-start | bytes 884740
  25.4 10.8 %collective-permute-start.11 = (bf16[192,768]{1,0:T(8,128)(2,1)S(1)}, bf16[192,768]{1,0:T(8,128)(2,1)S(1)}, u32[]{:S(2)}, u32[]{:S(2)}) collective-permute-start(bf16[192,768]{1,0:T(8,128)(2,1)S(1)} %collective-permute-done.8), channel_id=1, source_target_pairs={{0,8},{8,0},{16,24},{24,16},{1,9},{9,1},{17,25},{25,17},{2,10},{10... | collective-permute-start | bytes 884744 | tf_op jit(solution)/shard_map/ppermute | solution.py:20
  29.5 5.7 %collective-permute-start.3 = (bf16[128,768]{1,0:T(8,128)(2,1)S(1)}, bf16[128,768]{1,0:T(8,128)(2,1)S(1)}, u32[]{:S(2)}, u32[]{:S(2)}) collective-permute-start(bf16[128,768]{1,0:T(8,128)(2,1)S(1)} %collective-permute-done.2), channel_id=1, source_target_pairs={{0,2},{2,0},{1,3},{3,1},{4,6},{6,4},{5,7},{7,5},{8,10},{10,8},{9,1... | collective-permute-start | bytes 589832 | tf_op jit(solution)/shard_map/ppermute | solution.py:20
  35.4 2.4 %collective-permute-start.5 = (bf16[2,2,128,768]{3,2,1,0:T(8,128)(2,1)S(1)}, bf16[2,2,128,768]{3,2,1,0:T(8,128)(2,1)S(1)}, u32[]{:S(2)}, u32[]{:S(2)}) collective-permute-start(bf16[2,2,128,768]{3,2,1,0:T(8,128)(2,1)S(1)} %pad_maximum_fusion), channel_id=1, source_target_pairs={{0,1},{1,0},{2,3},{3,2},{4,5},{5,4},{6,7},{7,6},{8,9},{9,8},{10,11... | collective-permute-start | bytes 2359304 | tf_op jit(solution)/shard_map/ppermute | solution.py:20
  41.2 3.1 %collective-permute-start.12 = (f32[8,128]{1,0:T(8,128)S(1)}, f32[8,128]{1,0:T(8,128)S(1)}, u32[]{:S(2)}, u32[]{:S(2)}) collective-permute-start(f32[8,128]{1,0:T(8,128)S(1)} %get-tuple-element.25), channel_id=1, source_target_pairs={{0,3},{1,2},{2,1},{3,0},{4,7},{5,6},{6,5},{7,4},{8,11},{9,10},{10,... | collective-permute-start | bytes 12296 | tf_op jit(solution)/shard_map/ppermute | solution.py:20
  42.7 3.6 %collective-permute-start.13 = (f32[8,128]{1,0:T(8,128)S(1)}, f32[8,128]{1,0:T(8,128)S(1)}, u32[]{:S(2)}, u32[]{:S(2)}) collective-permute-start(f32[8,128]{1,0:T(8,128)S(1)} %get-tuple-element.25), channel_id=1, source_target_pairs={{0,2},{1,3},{2,0},{3,1},{4,6},{5,7},{6,4},{7,5},{8,10},{9,11},{10,... | collective-permute-start | bytes 12296 | tf_op jit(solution)/shard_map/ppermute | solution.py:20
  43.1 3.3 %collective-permute-start.14 = (f32[8,128]{1,0:T(8,128)S(1)}, f32[8,128]{1,0:T(8,128)S(1)}, u32[]{:S(2)}, u32[]{:S(2)}) collective-permute-start(f32[8,128]{1,0:T(8,128)S(1)} %get-tuple-element.25), channel_id=1, source_target_pairs={{0,1},{1,0},{2,3},{3,2},{4,5},{5,4},{6,7},{7,6},{8,9},{9,8},{10,11... | collective-permute-start | bytes 12296 | tf_op jit(solution)/shard_map/ppermute | solution.py:20
  47.8 4.6 %collective-permute-start.15 = (f32[12,128]{1,0:T(8,128)S(1)}, f32[12,128]{1,0:T(8,128)S(1)}, u32[]{:S(2)}, u32[]{:S(2)}) collective-permute-start(f32[12,128]{1,0:T(8,128)S(1)} %shard_map.68), channel_id=1, source_target_pairs={{0,24},{8,16},{16,8},{24,0},{1,25},{9,17},{17,9},{25,1},{2,26},{10... | collective-permute-start | bytes 18440 | tf_op jit(solution)/shard_map/ppermute | solution.py:20
  50.3 3.7 %collective-permute-start.16 = (f32[12,128]{1,0:T(8,128)S(1)}, f32[12,128]{1,0:T(8,128)S(1)}, u32[]{:S(2)}, u32[]{:S(2)}) collective-permute-start(f32[12,128]{1,0:T(8,128)S(1)} %shard_map.68), channel_id=1, source_target_pairs={{0,16},{8,24},{16,0},{24,8},{1,17},{9,25},{17,1},{25,9},{2,18},{10... | collective-permute-start | bytes 18440 | tf_op jit(solution)/shard_map/ppermute | solution.py:20
  50.8 3.7 %collective-permute-start.17 = (f32[12,128]{1,0:T(8,128)S(1)}, f32[12,128]{1,0:T(8,128)S(1)}, u32[]{:S(2)}, u32[]{:S(2)}) collective-permute-start(f32[12,128]{1,0:T(8,128)S(1)} %shard_map.68), channel_id=1, source_target_pairs={{0,8},{8,0},{16,24},{24,16},{1,9},{9,1},{17,25},{25,17},{2,10},{10... | collective-permute-start | bytes 18440 | tf_op jit(solution)/shard_map/ppermute | solution.py:20
  55.8 3.1 %collective-permute-start.18 = (f32[8,128]{1,0:T(8,128)S(1)}, f32[8,128]{1,0:T(8,128)S(1)}, u32[]{:S(2)}, u32[]{:S(2)}) collective-permute-start(f32[8,128]{1,0:T(8,128)S(1)} %shard_map.69), channel_id=1, source_target_pairs={{0,3},{1,2},{2,1},{3,0},{4,7},{5,6},{6,5},{7,4},{8,11},{9,10},{10,... | collective-permute-start | bytes 12296 | tf_op jit(solution)/shard_map/ppermute | solution.py:20
  55.9 3.7 %collective-permute-start.19 = (f32[8,128]{1,0:T(8,128)S(1)}, f32[8,128]{1,0:T(8,128)S(1)}, u32[]{:S(2)}, u32[]{:S(2)}) collective-permute-start(f32[8,128]{1,0:T(8,128)S(1)} %shard_map.69), channel_id=1, source_target_pairs={{0,2},{1,3},{2,0},{3,1},{4,6},{5,7},{6,4},{7,5},{8,10},{9,11},{10,... | collective-permute-start | bytes 12296 | tf_op jit(solution)/shard_map/ppermute | solution.py:20
  56.3 3.3 %collective-permute-start.20 = (f32[8,128]{1,0:T(8,128)S(1)}, f32[8,128]{1,0:T(8,128)S(1)}, u32[]{:S(2)}, u32[]{:S(2)}) collective-permute-start(f32[8,128]{1,0:T(8,128)S(1)} %shard_map.69), channel_id=1, source_target_pairs={{0,1},{1,0},{2,3},{3,2},{4,5},{5,4},{6,7},{7,6},{8,9},{9,8},{10,11... | collective-permute-start | bytes 12296 | tf_op jit(solution)/shard_map/ppermute | solution.py:20
  61.0 4.7 %collective-permute-start.21 = (f32[12,128]{1,0:T(8,128)S(1)}, f32[12,128]{1,0:T(8,128)S(1)}, u32[]{:S(2)}, u32[]{:S(2)}) collective-permute-start(f32[12,128]{1,0:T(8,128)S(1)} %shard_map.70), channel_id=1, source_target_pairs={{0,24},{8,16},{16,8},{24,0},{1,25},{9,17},{17,9},{25,1},{2,26},{10... | collective-permute-start | bytes 18440 | tf_op jit(solution)/shard_map/ppermute | solution.py:20
  62.6 3.7 %collective-permute-start.22 = (f32[12,128]{1,0:T(8,128)S(1)}, f32[12,128]{1,0:T(8,128)S(1)}, u32[]{:S(2)}, u32[]{:S(2)}) collective-permute-start(f32[12,128]{1,0:T(8,128)S(1)} %shard_map.70), channel_id=1, source_target_pairs={{0,16},{8,24},{16,0},{24,8},{1,17},{9,25},{17,1},{25,9},{2,18},{10... | collective-permute-start | bytes 18440 | tf_op jit(solution)/shard_map/ppermute | solution.py:20
  63.1 3.7 %collective-permute-start.23 = (f32[12,128]{1,0:T(8,128)S(1)}, f32[12,128]{1,0:T(8,128)S(1)}, u32[]{:S(2)}, u32[]{:S(2)}) collective-permute-start(f32[12,128]{1,0:T(8,128)S(1)} %shard_map.70), channel_id=1, source_target_pairs={{0,8},{8,0},{16,24},{24,16},{1,9},{9,1},{17,25},{25,17},{2,10},{10... | collective-permute-start | bytes 18440 | tf_op jit(solution)/shard_map/ppermute | solution.py:20
  68.1 3.1 %collective-permute-start.24 = (f32[8,128]{1,0:T(8,128)S(1)}, f32[8,128]{1,0:T(8,128)S(1)}, u32[]{:S(2)}, u32[]{:S(2)}) collective-permute-start(f32[8,128]{1,0:T(8,128)S(1)} %shard_map.71), channel_id=1, source_target_pairs={{0,3},{1,2},{2,1},{3,0},{4,7},{5,6},{6,5},{7,4},{8,11},{9,10},{10,... | collective-permute-start | bytes 12296 | tf_op jit(solution)/shard_map/ppermute | solution.py:20
  68.2 3.7 %collective-permute-start.25 = (f32[8,128]{1,0:T(8,128)S(1)}, f32[8,128]{1,0:T(8,128)S(1)}, u32[]{:S(2)}, u32[]{:S(2)}) collective-permute-start(f32[8,128]{1,0:T(8,128)S(1)} %shard_map.71), channel_id=1, source_target_pairs={{0,2},{1,3},{2,0},{3,1},{4,6},{5,7},{6,4},{7,5},{8,10},{9,11},{10,... | collective-permute-start | bytes 12296 | tf_op jit(solution)/shard_map/ppermute | solution.py:20
  68.5 3.3 %collective-permute-start.26 = (f32[8,128]{1,0:T(8,128)S(1)}, f32[8,128]{1,0:T(8,128)S(1)}, u32[]{:S(2)}, u32[]{:S(2)}) collective-permute-start(f32[8,128]{1,0:T(8,128)S(1)} %shard_map.71), channel_id=1, source_target_pairs={{0,1},{1,0},{2,3},{3,2},{4,5},{5,4},{6,7},{7,6},{8,9},{9,8},{10,11... | collective-permute-start | bytes 12296 | tf_op jit(solution)/shard_map/ppermute | solution.py:20
  73.5 4.6 %collective-permute-start.27 = (f32[12,128]{1,0:T(8,128)S(1)}, f32[12,128]{1,0:T(8,128)S(1)}, u32[]{:S(2)}, u32[]{:S(2)}) collective-permute-start(f32[12,128]{1,0:T(8,128)S(1)} %shard_map.72), channel_id=1, source_target_pairs={{0,24},{8,16},{16,8},{24,0},{1,25},{9,17},{17,9},{25,1},{2,26},{10... | collective-permute-start | bytes 18440 | tf_op jit(solution)/shard_map/ppermute | solution.py:20
  76.0 3.7 %collective-permute-start.28 = (f32[12,128]{1,0:T(8,128)S(1)}, f32[12,128]{1,0:T(8,128)S(1)}, u32[]{:S(2)}, u32[]{:S(2)}) collective-permute-start(f32[12,128]{1,0:T(8,128)S(1)} %shard_map.72), channel_id=1, source_target_pairs={{0,16},{8,24},{16,0},{24,8},{1,17},{9,25},{17,1},{25,9},{2,18},{10... | collective-permute-start | bytes 18440 | tf_op jit(solution)/shard_map/ppermute | solution.py:20
  76.5 3.7 %collective-permute-start.29 = (f32[12,128]{1,0:T(8,128)S(1)}, f32[12,128]{1,0:T(8,128)S(1)}, u32[]{:S(2)}, u32[]{:S(2)}) collective-permute-start(f32[12,128]{1,0:T(8,128)S(1)} %shard_map.72), channel_id=1, source_target_pairs={{0,8},{8,0},{16,24},{24,16},{1,9},{9,1},{17,25},{25,17},{2,10},{10... | collective-permute-start | bytes 18440 | tf_op jit(solution)/shard_map/ppermute | solution.py:20
  80.9 3.1 %collective-permute-start.30 = (f32[2,4,128]{2,1,0:T(4,128)S(1)}, f32[2,4,128]{2,1,0:T(4,128)S(1)}, u32[]{:S(2)}, u32[]{:S(2)}) collective-permute-start(f32[2,4,128]{2,1,0:T(4,128)S(1)} %pad_maximum_fusion.3), channel_id=1, source_target_pairs={{0,3},{1,2},{2,1},{3,0},{4,7},{5,6},{6,5},{7,4},{8,11},{9,10},{10,... | collective-permute-start | bytes 12296 | tf_op jit(solution)/shard_map/ppermute | solution.py:20
  81.0 3.7 %collective-permute-start.31 = (f32[2,4,128]{2,1,0:T(4,128)S(1)}, f32[2,4,128]{2,1,0:T(4,128)S(1)}, u32[]{:S(2)}, u32[]{:S(2)}) collective-permute-start(f32[2,4,128]{2,1,0:T(4,128)S(1)} %pad_maximum_fusion.3), channel_id=1, source_target_pairs={{0,2},{1,3},{2,0},{3,1},{4,6},{5,7},{6,4},{7,5},{8,10},{9,11},{10,... | collective-permute-start | bytes 12296 | tf_op jit(solution)/shard_map/ppermute | solution.py:20
  81.3 3.3 %collective-permute-start.32 = (f32[2,4,128]{2,1,0:T(4,128)S(1)}, f32[2,4,128]{2,1,0:T(4,128)S(1)}, u32[]{:S(2)}, u32[]{:S(2)}) collective-permute-start(f32[2,4,128]{2,1,0:T(4,128)S(1)} %pad_maximum_fusion.3), channel_id=1, source_target_pairs={{0,1},{1,0},{2,3},{3,2},{4,5},{5,4},{6,7},{7,6},{8,9},{9,8},{10,11... | collective-permute-start | bytes 12296 | tf_op jit(solution)/shard_map/ppermute | solution.py:20
  85.5 2.4 %collective-permute-start.33 = (f32[256,768]{1,0:T(8,128)S(1)}, f32[256,768]{1,0:T(8,128)S(1)}, u32[]{:S(2)}, u32[]{:S(2)}) collective-permute-start(f32[256,768]{1,0:T(8,128)S(1)} %shard_map.75), channel_id=1, source_target_pairs={{0,1},{1,0},{2,3},{3,2},{4,5},{5,4},{6,7},{7,6},{8,9},{9,8},{10,11... | collective-permute-start | bytes 2359304 | tf_op jit(solution)/shard_map/ppermute | solution.py:20
  87.9 7.0 %collective-permute-start.34 = (f16[128,768]{1,0:T(8,128)(2,1)S(1)}, f16[128,768]{1,0:T(8,128)(2,1)S(1)}, u32[]{:S(2)}, u32[]{:S(2)}) collective-permute-start(f16[128,768]{1,0:T(8,128)(2,1)S(1)} %fusion.1), channel_id=1, source_target_pairs={{0,2},{2,0},{1,3},{3,1},{4,6},{6,4},{5,7},{7,5},{8,10},{10,8},{9,1... | collective-permute-start | bytes 589832 | tf_op jit(solution)/shard_map/ppermute | solution.py:20
